TPU v7x, 512 devices: a whole 4x8x8 slice. The times are simulated.
512 devices in a mesh: tm: 8 (over z_hi, core), space: 64 (over z_lo, y, x).
Axes of the slice: x: 4, y: 8, z: 8 (z_hi: 4, z_lo: 2; z = z_hi * 2 + z_lo), core: 2. Of those that a mesh axis runs over, the one named last changes fastest.
Arguments:
- equilibrium: float32 [16, 512, 128], P('tm', 'space'), may hold values from -6 to 6
- measurement: float32 [512, 128], P('space'), may hold values from -12 to 12
- coding_masks: int32 [16, 512, 128], P('tm', 'space'), may hold values 0 or 1
- upstream: float32 [16, 512, 128], P('tm', 'space'), may hold values from -6 to 6
- saved_second: bfloat16 [16, 64, 512, 128], P('tm', None, 'space'), may hold values from -8 to 8
- conv_first: bfloat16 [9, 64], replicated, may hold values from -2 to 2
- conv_second: bfloat16 [9, 64, 64], replicated, may hold values from -0.25 to 0.25
- conv_third: bfloat16 [9, 64], replicated, may hold values from -0.75 to 0.75
Outputs:
- adjoint: float32 [16, 512, 128], P('tm', 'space')
- measurement_grad: float32 [512, 128], P('space')
- grad_first: float32 [9, 64], replicated
- grad_second: float32 [9, 64, 64], replicated
- grad_third: float32 [9, 64], replicated
All inputs are finite; a program needn't handle non-finite values. No bound on the sum of `coding_masks` on one device may be relied on, other than what follows from the above.
Results may differ from a plain program's by a relative error of at most 0.013.
Values may be sent and summed in bfloat16 or wider, within the bound.
No kernel may reach another device: no remote copies, remote signals or barrier semaphores. Data moves between devices by JAX's collectives and lax.ppermute only.
A program may use at most 64 MiB of HBM per device.

v0:
```python
import math

import jax
import jax.numpy as jnp
from jax import lax
from jax.sharding import PartitionSpec as P

ITERS = 3


KERNEL_TAPS = [(row_step, col_step) for row_step in (-1, 0, 1) for col_step in (-1, 0, 1)]


def with_halo(block, sides, width):
    for axis, dim in sides:
        count = lax.axis_size(axis)
        forward = [(i, i + 1) for i in range(count - 1)]
        backward = [(target, source) for source, target in forward]
        low = lax.ppermute(
            lax.slice_in_dim(block, block.shape[dim] - width, None, axis=dim), axis, forward
        )
        high = lax.ppermute(lax.slice_in_dim(block, 0, width, axis=dim), axis, backward)
        block = jnp.concatenate([low, block, high], axis=dim)
    return block


def silu_slope(value):
    logistic = jax.nn.sigmoid(value)
    return logistic * (1.0 + value * (1.0 - logistic))


def shift_cols(field, col_step):
    if col_step == 0:
        return field
    blank_col = jnp.zeros_like(field[..., :1])
    if col_step > 0:
        return jnp.concatenate([field[..., 1:], blank_col], axis=-1)
    return jnp.concatenate([blank_col, field[..., :-1]], axis=-1)


def tap_view(field, row_step, col_step, count):
    row_band = lax.slice_in_dim(field, 1 + row_step, 1 + row_step + count, axis=field.ndim - 2)
    return shift_cols(row_band, col_step)


def conv_forward(source_ext, weight_f):
    count = source_ext.shape[1] - 2
    result = jnp.zeros(
        (source_ext.shape[0], weight_f.shape[1], count, source_ext.shape[2]), jnp.float32
    )
    for tap_index, (row_step, col_step) in enumerate(KERNEL_TAPS):
        result = (
            result
            + weight_f[tap_index][None, :, None, None]
            * tap_view(source_ext, row_step, col_step, count)[:, None]
        )
    return result


def conv_third_back(adjoint_ext, weight_f):
    count = adjoint_ext.shape[1] - 2
    result = jnp.zeros(
        (adjoint_ext.shape[0], weight_f.shape[1], count, adjoint_ext.shape[2]), jnp.float32
    )
    for tap_index, (row_step, col_step) in enumerate(KERNEL_TAPS):
        result = (
            result
            + weight_f[tap_index][None, :, None, None]
            * tap_view(adjoint_ext, -row_step, -col_step, count)[:, None]
        )
    return result


def conv_second_back(grad_ext, weight):
    count = grad_ext.shape[2] - 2
    result = jnp.zeros((grad_ext.shape[0], weight.shape[2], count, grad_ext.shape[3]), jnp.float32)
    for tap_index, (row_step, col_step) in enumerate(KERNEL_TAPS):
        result = result + jnp.einsum(
            "oc,forw->fcrw",
            weight[tap_index],
            tap_view(grad_ext, -row_step, -col_step, count),
            preferred_element_type=jnp.float32,
        )
    return result


def conv_first_back(grad_ext, weight):
    count = grad_ext.shape[2] - 2
    result = jnp.zeros((grad_ext.shape[0], count, grad_ext.shape[3]), jnp.float32)
    for tap_index, (row_step, col_step) in enumerate(KERNEL_TAPS):
        result = result + jnp.einsum(
            "o,forw->frw",
            weight[tap_index],
            tap_view(grad_ext, -row_step, -col_step, count),
            preferred_element_type=jnp.float32,
        )
    return result


def frame_total(field, masks):
    return lax.psum(jnp.sum(masks * field, axis=0), "tm")


def per_device(
    equilibrium,
    measurement,
    coding_masks,
    upstream,
    saved_second,
    conv_first,
    conv_second,
    conv_third,
):
    frame_count, row_count, col_count = equilibrium.shape
    tile_count = lax.axis_size("space")
    total_frames = frame_count * lax.axis_size("tm")
    step_size = 1.0 / total_frames
    scale = 1.0 / math.sqrt(total_frames * row_count * tile_count * col_count)
    masks = coding_masks.astype(jnp.float32)
    frame_sum = lax.psum(jnp.sum(masks * equilibrium, axis=0), "tm")
    denoiser_input = equilibrium - step_size * masks * (frame_sum - measurement)[None]
    first_f = conv_first.astype(jnp.float32)
    third_f = conv_third.astype(jnp.float32)
    input_ext = with_halo(denoiser_input, (("space", 1),), 1)
    first_pre = conv_forward(input_ext, first_f)
    gate_second = silu_slope(saved_second.astype(jnp.float32))
    gate_first = silu_slope(first_pre)

    def adjoint_map(field):
        field_ext = with_halo(field, (("space", 1),), 1)
        d_second = (gate_second * conv_third_back(field_ext, third_f)).astype(jnp.bfloat16)
        second_ext = with_halo(d_second, (("space", 2),), 1)
        d_first = (gate_first * conv_second_back(second_ext, conv_second)).astype(jnp.bfloat16)
        first_ext = with_halo(d_first, (("space", 2),), 1)
        return (field + conv_first_back(first_ext, conv_first), field_ext, second_ext, first_ext)

    adjoint = upstream
    for sweep_index in range(ITERS):
        mapped = adjoint_map(adjoint)[0]
        totals = frame_total(mapped, masks)
        adjoint = upstream + mapped - step_size * masks * totals[None]
    mapped, adjoint_ext, second_ext, first_ext = adjoint_map(adjoint)
    measurement_grad = step_size * frame_total(mapped, masks)
    hidden_first = jax.nn.silu(first_pre).astype(jnp.bfloat16)
    hidden_second = jax.nn.silu(saved_second.astype(jnp.float32))
    first_terms = []
    second_terms = []
    third_terms = []
    for row_step, col_step in KERNEL_TAPS:
        second_terms.append(
            jnp.einsum(
                "forw,fcrw->oc",
                tap_view(second_ext, -row_step, -col_step, row_count),
                hidden_first,
                preferred_element_type=jnp.float32,
            )
        )
        first_terms.append(
            jnp.sum(
                tap_view(first_ext, -row_step, -col_step, row_count) * denoiser_input[:, None],
                axis=(0, 2, 3),
            )
        )
        third_terms.append(
            jnp.sum(
                hidden_second * tap_view(adjoint_ext, -row_step, -col_step, row_count)[:, None],
                axis=(0, 2, 3),
            )
        )
    grad_first, grad_second, grad_third = lax.psum(
        (jnp.stack(first_terms), jnp.stack(second_terms), jnp.stack(third_terms)), ("tm", "space")
    )
    return (adjoint, measurement_grad, grad_first * scale, grad_second * scale, grad_third * scale)


def solution(mesh):
    placed = (
        P("tm", "space", None),
        P("space", None),
        P("tm", "space", None),
        P("tm", "space", None),
        P("tm", None, "space", None),
        P(),
        P(),
        P(),
    )
    return jax.shard_map(
        per_device,
        mesh=mesh,
        in_specs=placed,
        out_specs=(P("tm", "space", None), P("space", None), P(), P(), P()),
        check_vma=False,
    )
```

profile of v0, /device:TPU:1, one launch (start us, length us, event | category | flops | bytes accessed | tf_op | source)
XLA Modules:
  0.0 519.8 jit_solution(15387892712597915754)
XLA Ops:
  7.2 0.8 fusion.499
  8.0 3.9 collective-permute-start.3
  11.9 1.3 collective-permute-start.2
  13.2 0.7 multiply_reduce_fusion.22
  14.0 19.8 %psum.56 = f32[8,128]{1,0:T(8,128)S(1)} all-reduce(f32[8,128]{1,0:T(8,128)S(1)} %multiply_reduce_fusion.22), channel_id=1, replica_groups=mesh['tm'=8,'space'=64] {'tm'}, use_global_device_ids=true, to_apply=%region_1.0 | all-reduce | flops 1024 | bytes 8192 | tf_op jit(solution)/shard_map/psum | solution.py:120
  33.8 0.7 subtract_multiply_fusion
  34.5 0.7 multiply_subtract_fusion.3
  35.2 4.3 collective-permute-start
  39.5 1.3 collective-permute-start.1
  40.8 0.7 convert_element_type.70
  41.5 0.7 convert_element_type.67
  42.2 0.9 fusion.320
  43.2 0.9 fusion.500
  44.2 0.7 copy-done.3
  44.9 0.6 multiply_convert_fusion.4
  45.5 1.3 collective-permute-start.4
  46.8 4.6 collective-permute-start.5
  51.9 0.6 collective-permute-done.5
  55.0 0.7 fusion.18
  55.7 1.3 collective-permute-start.6
  57.0 4.3 collective-permute-start.7
  61.4 0.8 collective-permute-done.7
  64.1 0.7 copy-done.4
  64.8 19.4 %psum.57 = f32[8,128]{1,0:T(8,128)S(1)} all-reduce(f32[8,128]{1,0:T(8,128)S(1)} %get-tuple-element.32), channel_id=1, replica_groups=mesh['tm'=8,'space'=64] {'tm'}, use_global_device_ids=true, to_apply=%region_3.0 | all-reduce | flops 1024 | bytes 8192 | tf_op jit(solution)/shard_map/psum | solution.py:101
  84.2 1.3 collective-permute-start.8
  85.5 4.6 collective-permute-start.9
  90.1 0.7 collective-permute-done.9
  91.0 0.7 convert_multiply_fusion
  91.7 1.3 collective-permute-start.10
  93.0 6.0 %collective-permute-start.11 = (bf16[2,64,1,128]{3,1,2,0:T(8,128)(2,1)S(1)}, bf16[2,64,1,128]{3,1,2,0:T(8,128)(2,1)S(1)}, u32[]{:S(2)}, u32[]{:S(2)}) collective-permute-start(bf16[2,64,1,128]{3,1,2,0:T(8,128)(2,1)S(1)} %get-tuple-element.91), channel_id=1, source_target_pairs={{0,1},{1,2},{2,3},{3,4},{4,5},{5,6},{6,7},{7,8},{8,9},{9,10},{10,1... | collective-permute-start | bytes 98312 | tf_op jit(solution)/shard_map/ppermute | solution.py:19
  99.1 1.0 collective-permute-done.11
  102.5 0.7 fusion.17
  103.2 1.3 collective-permute-start.12
  104.5 6.7 %collective-permute-start.13 = (bf16[2,64,1,128]{3,1,2,0:T(8,128)(2,1)S(1)}, bf16[2,64,1,128]{3,1,2,0:T(8,128)(2,1)S(1)}, u32[]{:S(2)}, u32[]{:S(2)}) collective-permute-start(bf16[2,64,1,128]{3,1,2,0:T(8,128)(2,1)S(1)} %get-tuple-element.85), channel_id=1, source_target_pairs={{0,1},{1,2},{2,3},{3,4},{4,5},{5,6},{6,7},{7,8},{8,9},{9,10},{10,1... | collective-permute-start | bytes 98312 | tf_op jit(solution)/shard_map/ppermute | solution.py:19
  111.4 0.9 collective-permute-done.13
  114.0 16.8 %psum.58 = f32[8,128]{1,0:T(8,128)S(1)} all-reduce(f32[8,128]{1,0:T(8,128)S(1)} %get-tuple-element.30), channel_id=1, replica_groups=mesh['tm'=8,'space'=64] {'tm'}, use_global_device_ids=true, to_apply=%region_5.0 | all-reduce | flops 1024 | bytes 8192 | tf_op jit(solution)/shard_map/psum | solution.py:101
  130.9 1.3 collective-permute-start.14
  132.2 6.7 %collective-permute-start.15 = (f32[2,1,128]{2,1,0:T(1,128)S(1)}, f32[2,1,128]{2,1,0:T(1,128)S(1)}, u32[]{:S(2)}, u32[]{:S(2)}) collective-permute-start(f32[2,1,128]{2,1,0:T(1,128)S(1)} %get-tuple-element.139), channel_id=1, source_target_pairs={{0,1},{1,2},{2,3},{3,4},{4,5},{5,6},{6,7},{7,8},{8,9},{9,10},{10,1... | collective-permute-start | bytes 3080 | tf_op jit(solution)/shard_map/ppermute | solution.py:19
  138.9 0.7 collective-permute-done.15
  139.8 0.6 multiply_convert_fusion.2
  140.4 1.3 collective-permute-start.16
  141.7 6.8 %collective-permute-start.17 = (bf16[2,64,1,128]{3,1,2,0:T(8,128)(2,1)S(1)}, bf16[2,64,1,128]{3,1,2,0:T(8,128)(2,1)S(1)}, u32[]{:S(2)}, u32[]{:S(2)}) collective-permute-start(bf16[2,64,1,128]{3,1,2,0:T(8,128)(2,1)S(1)} %get-tuple-element.79), channel_id=1, source_target_pairs={{0,1},{1,2},{2,3},{3,4},{4,5},{5,6},{6,7},{7,8},{8,9},{9,10},{10,1... | collective-permute-start | bytes 98312 | tf_op jit(solution)/shard_map/ppermute | solution.py:19
  148.6 0.8 collective-permute-done.17
  151.9 0.7 fusion.16
  152.6 1.3 collective-permute-start.18
  153.9 6.7 %collective-permute-start.19 = (bf16[2,64,1,128]{3,1,2,0:T(8,128)(2,1)S(1)}, bf16[2,64,1,128]{3,1,2,0:T(8,128)(2,1)S(1)}, u32[]{:S(2)}, u32[]{:S(2)}) collective-permute-start(bf16[2,64,1,128]{3,1,2,0:T(8,128)(2,1)S(1)} %get-tuple-element.73), channel_id=1, source_target_pairs={{0,1},{1,2},{2,3},{3,4},{4,5},{5,6},{6,7},{7,8},{8,9},{9,10},{10,1... | collective-permute-start | bytes 98312 | tf_op jit(solution)/shard_map/ppermute | solution.py:19
  160.7 0.9 collective-permute-done.19
  163.4 16.8 %psum.59 = f32[8,128]{1,0:T(8,128)S(1)} all-reduce(f32[8,128]{1,0:T(8,128)S(1)} %get-tuple-element.28), channel_id=1, replica_groups=mesh['tm'=8,'space'=64] {'tm'}, use_global_device_ids=true, to_apply=%region_7.0 | all-reduce | flops 1024 | bytes 8192 | tf_op jit(solution)/shard_map/psum | solution.py:101
  180.2 1.3 collective-permute-start.20
  181.5 6.7 %collective-permute-start.21 = (f32[2,1,128]{2,1,0:T(1,128)S(1)}, f32[2,1,128]{2,1,0:T(1,128)S(1)}, u32[]{:S(2)}, u32[]{:S(2)}) collective-permute-start(f32[2,1,128]{2,1,0:T(1,128)S(1)} %get-tuple-element.131), channel_id=1, source_target_pairs={{0,1},{1,2},{2,3},{3,4},{4,5},{5,6},{6,7},{7,8},{8,9},{9,10},{10,1... | collective-permute-start | bytes 3080 | tf_op jit(solution)/shard_map/ppermute | solution.py:19
  188.2 0.6 multiply_convert_fusion
  189.2 0.6 multiply_convert_fusion.1
  189.8 1.3 collective-permute-start.22
  191.1 6.6 %collective-permute-start.23 = (bf16[2,64,1,128]{3,1,2,0:T(8,128)(2,1)S(1)}, bf16[2,64,1,128]{3,1,2,0:T(8,128)(2,1)S(1)}, u32[]{:S(2)}, u32[]{:S(2)}) collective-permute-start(bf16[2,64,1,128]{3,1,2,0:T(8,128)(2,1)S(1)} %get-tuple-element.67), channel_id=1, source_target_pairs={{0,1},{1,2},{2,3},{3,4},{4,5},{5,6},{6,7},{7,8},{8,9},{9,10},{10,1... | collective-permute-start | bytes 98312 | tf_op jit(solution)/shard_map/ppermute | solution.py:19
  203.9 0.7 fusion.15
  204.6 1.3 collective-permute-start.24
  205.9 6.7 %collective-permute-start.25 = (bf16[2,64,1,128]{3,1,2,0:T(8,128)(2,1)S(1)}, bf16[2,64,1,128]{3,1,2,0:T(8,128)(2,1)S(1)}, u32[]{:S(2)}, u32[]{:S(2)}) collective-permute-start(bf16[2,64,1,128]{3,1,2,0:T(8,128)(2,1)S(1)} %get-tuple-element.61), channel_id=1, source_target_pairs={{0,1},{1,2},{2,3},{3,4},{4,5},{5,6},{6,7},{7,8},{8,9},{9,10},{10,1... | collective-permute-start | bytes 98312 | tf_op jit(solution)/shard_map/ppermute | solution.py:19
  212.7 0.8 collective-permute-done.25
  215.4 16.8 %psum.60 = f32[8,128]{1,0:T(8,128)S(1)} all-reduce(f32[8,128]{1,0:T(8,128)S(1)} %multiply_reduce_fusion.18), channel_id=1, replica_groups=mesh['tm'=8,'space'=64] {'tm'}, use_global_device_ids=true, to_apply=%region_9.0 | all-reduce | flops 1024 | bytes 8192 | tf_op jit(solution)/shard_map/psum | solution.py:101
  232.2 0.8 multiply_reduce_fusion.9
  233.0 133.3 %all-reduce.78 = (f32[9,64]{1,0:T(8,128)S(1)}, f32[9,64]{1,0:T(8,128)S(1)}) all-reduce(f32[9,64]{1,0:T(8,128)S(1)} %stack.99, f32[9,64]{1,0:T(8,128)S(1)} %stack.119), channel_id=1, replica_groups=mesh['tm'=8,'space'=64] {'tm','space'}, use_global_device_ids=true, to_apply=%region_19.20 | all-reduce | flops 1152 | bytes 9216 | tf_op jit(solution)/shard_map/psum | solution.py:170
  366.3 0.6 broadcast_multiply_fusion.1
  367.5 143.8 %all-reduce.81.cloned.1.call-done = f32[9,64,64]{2,1,0:T(8,128)} async-done(((f32[9,64,64]{2,1,0:T(8,128)}), f32[9,64,64]{2,1,0:T(8,128)}) %all-reduce.81.cloned.1.call-update) | async-done | bytes 147472 | tf_op jit(solution)/shard_map/psum | solution.py:170
  511.3 1.7 broadcast_multiply_fusion
  (176 shorter events, 23.6 us)
Async XLA Ops:
  7.2 37.0 %copy-start = (bf16[2,64,8,128]{3,2,1,0:T(8,128)(2,1)S(1)}, bf16[2,64,8,128]{3,2,1,0:T(8,128)(2,1)}, u32[]{:S(2)}) copy-start(bf16[2,64,8,128]{3,2,1,0:T(8,128)(2,1)} %param.12) | copy-start | bytes 786436
  7.2 504.1 %all-reduce.81.cloned.1.call-start = ((), (), s32[]{:S(2)}) async-start(), calls=%async_computation | async-start | bytes 589824 | tf_op jit(solution)/shard_map/psum | solution.py:170
  8.0 34.2 %collective-permute-start.3 = (f32[2,1,128]{2,1,0:T(1,128)S(1)}, f32[2,1,128]{2,1,0:T(1,128)S(1)}, u32[]{:S(2)}, u32[]{:S(2)}) collective-permute-start(f32[2,1,128]{2,1,0:T(1,128)S(1)} %get-tuple-element.175), channel_id=1, source_target_pairs={{0,1},{1,2},{2,3},{3,4},{4,5},{5,6},{6,7},{7,8},{8,9},{9,10},{10,1... | collective-permute-start | bytes 3080 | tf_op jit(solution)/shard_map/ppermute | solution.py:19
  11.9 31.1 %collective-permute-start.2 = (f32[2,1,128]{2,1,0:T(1,128)S(1)}, f32[2,1,128]{2,1,0:T(1,128)S(1)}, u32[]{:S(2)}, u32[]{:S(2)}) collective-permute-start(f32[2,1,128]{2,1,0:T(1,128)S(1)} %get-tuple-element.174), channel_id=1, source_target_pairs={{1,0},{2,1},{3,2},{4,3},{5,4},{6,5},{7,6},{8,7},{9,8},{10,9},{11,1... | collective-permute-start | bytes 3080 | tf_op jit(solution)/shard_map/ppermute | solution.py:22
  35.2 16.3 %collective-permute-start = (f32[2,1,128]{2,1,0:T(1,128)S(1)}, f32[2,1,128]{2,1,0:T(1,128)S(1)}, u32[]{:S(2)}, u32[]{:S(2)}) collective-permute-start(f32[2,1,128]{2,1,0:T(1,128)S(1)} %get-tuple-element.163), channel_id=1, source_target_pairs={{0,1},{1,2},{2,3},{3,4},{4,5},{5,6},{6,7},{7,8},{8,9},{9,10},{10,1... | collective-permute-start | bytes 3080 | tf_op jit(solution)/shard_map/ppermute | solution.py:19
  39.5 12.0 %collective-permute-start.1 = (f32[2,1,128]{2,1,0:T(1,128)S(1)}, f32[2,1,128]{2,1,0:T(1,128)S(1)}, u32[]{:S(2)}, u32[]{:S(2)}) collective-permute-start(f32[2,1,128]{2,1,0:T(1,128)S(1)} %get-tuple-element.164), channel_id=1, source_target_pairs={{1,0},{2,1},{3,2},{4,3},{5,4},{6,5},{7,6},{8,7},{9,8},{10,9},{11,1... | collective-permute-start | bytes 3080 | tf_op jit(solution)/shard_map/ppermute | solution.py:22
  44.2 0.7 copy-start.3
  45.5 6.3 %collective-permute-start.4 = (bf16[2,64,1,128]{3,1,2,0:T(8,128)(2,1)S(1)}, bf16[2,64,1,128]{3,1,2,0:T(8,128)(2,1)S(1)}, u32[]{:S(2)}, u32[]{:S(2)}) collective-permute-start(bf16[2,64,1,128]{3,1,2,0:T(8,128)(2,1)S(1)} %get-tuple-element.102), channel_id=1, source_target_pairs={{1,0},{2,1},{3,2},{4,3},{5,4},{6,5},{7,6},{8,7},{9,8},{10,9},{11,1... | collective-permute-start | bytes 98312 | tf_op jit(solution)/shard_map/ppermute | solution.py:22
  46.8 5.6 %collective-permute-start.5 = (bf16[2,64,1,128]{3,1,2,0:T(8,128)(2,1)S(1)}, bf16[2,64,1,128]{3,1,2,0:T(8,128)(2,1)S(1)}, u32[]{:S(2)}, u32[]{:S(2)}) collective-permute-start(bf16[2,64,1,128]{3,1,2,0:T(8,128)(2,1)S(1)} %get-tuple-element.103), channel_id=1, source_target_pairs={{0,1},{1,2},{2,3},{3,4},{4,5},{5,6},{6,7},{7,8},{8,9},{9,10},{10,1... | collective-permute-start | bytes 98312 | tf_op jit(solution)/shard_map/ppermute | solution.py:19
  51.9 0.9 copy-start.1
  55.0 6.3 %copy-start.2 = (bf16[9,64]{1,0:T(8,128)(2,1)S(1)}, bf16[9,64]{1,0:T(8,128)(2,1)}, u32[]{:S(2)}) copy-start(bf16[9,64]{1,0:T(8,128)(2,1)} %param.13) | copy-start | bytes 3460
  55.7 5.7 %collective-permute-start.6 = (bf16[2,64,1,128]{3,1,2,0:T(8,128)(2,1)S(1)}, bf16[2,64,1,128]{3,1,2,0:T(8,128)(2,1)S(1)}, u32[]{:S(2)}, u32[]{:S(2)}) collective-permute-start(bf16[2,64,1,128]{3,1,2,0:T(8,128)(2,1)S(1)} %get-tuple-element.96), channel_id=1, source_target_pairs={{1,0},{2,1},{3,2},{4,3},{5,4},{6,5},{7,6},{8,7},{9,8},{10,9},{11,1... | collective-permute-start | bytes 98312 | tf_op jit(solution)/shard_map/ppermute | solution.py:22
  57.0 5.3 %collective-permute-start.7 = (bf16[2,64,1,128]{3,1,2,0:T(8,128)(2,1)S(1)}, bf16[2,64,1,128]{3,1,2,0:T(8,128)(2,1)S(1)}, u32[]{:S(2)}, u32[]{:S(2)}) collective-permute-start(bf16[2,64,1,128]{3,1,2,0:T(8,128)(2,1)S(1)} %get-tuple-element.97), channel_id=1, source_target_pairs={{0,1},{1,2},{2,3},{3,4},{4,5},{5,6},{6,7},{7,8},{8,9},{9,10},{10,1... | collective-permute-start | bytes 98312 | tf_op jit(solution)/shard_map/ppermute | solution.py:19
  64.1 0.7 copy-start.4
  84.2 5.9 %collective-permute-start.8 = (f32[2,1,128]{2,1,0:T(1,128)S(1)}, f32[2,1,128]{2,1,0:T(1,128)S(1)}, u32[]{:S(2)}, u32[]{:S(2)}) collective-permute-start(f32[2,1,128]{2,1,0:T(1,128)S(1)} %get-tuple-element.146), channel_id=1, source_target_pairs={{1,0},{2,1},{3,2},{4,3},{5,4},{6,5},{7,6},{8,7},{9,8},{10,9},{11,1... | collective-permute-start | bytes 3080 | tf_op jit(solution)/shard_map/ppermute | solution.py:22
  85.5 5.3 %collective-permute-start.9 = (f32[2,1,128]{2,1,0:T(1,128)S(1)}, f32[2,1,128]{2,1,0:T(1,128)S(1)}, u32[]{:S(2)}, u32[]{:S(2)}) collective-permute-start(f32[2,1,128]{2,1,0:T(1,128)S(1)} %get-tuple-element.147), channel_id=1, source_target_pairs={{0,1},{1,2},{2,3},{3,4},{4,5},{5,6},{6,7},{7,8},{8,9},{9,10},{10,1... | collective-permute-start | bytes 3080 | tf_op jit(solution)/shard_map/ppermute | solution.py:19
  91.7 7.3 %collective-permute-start.10 = (bf16[2,64,1,128]{3,1,2,0:T(8,128)(2,1)S(1)}, bf16[2,64,1,128]{3,1,2,0:T(8,128)(2,1)S(1)}, u32[]{:S(2)}, u32[]{:S(2)}) collective-permute-start(bf16[2,64,1,128]{3,1,2,0:T(8,128)(2,1)S(1)} %get-tuple-element.90), channel_id=1, source_target_pairs={{1,0},{2,1},{3,2},{4,3},{5,4},{6,5},{7,6},{8,7},{9,8},{10,9},{11,1... | collective-permute-start | bytes 98312 | tf_op jit(solution)/shard_map/ppermute | solution.py:22
  93.0 7.0 %collective-permute-start.11 = (bf16[2,64,1,128]{3,1,2,0:T(8,128)(2,1)S(1)}, bf16[2,64,1,128]{3,1,2,0:T(8,128)(2,1)S(1)}, u32[]{:S(2)}, u32[]{:S(2)}) collective-permute-start(bf16[2,64,1,128]{3,1,2,0:T(8,128)(2,1)S(1)} %get-tuple-element.91), channel_id=1, source_target_pairs={{0,1},{1,2},{2,3},{3,4},{4,5},{5,6},{6,7},{7,8},{8,9},{9,10},{10,1... | collective-permute-start | bytes 98312 | tf_op jit(solution)/shard_map/ppermute | solution.py:19
  103.2 8.1 %collective-permute-start.12 = (bf16[2,64,1,128]{3,1,2,0:T(8,128)(2,1)S(1)}, bf16[2,64,1,128]{3,1,2,0:T(8,128)(2,1)S(1)}, u32[]{:S(2)}, u32[]{:S(2)}) collective-permute-start(bf16[2,64,1,128]{3,1,2,0:T(8,128)(2,1)S(1)} %get-tuple-element.84), channel_id=1, source_target_pairs={{1,0},{2,1},{3,2},{4,3},{5,4},{6,5},{7,6},{8,7},{9,8},{10,9},{11,1... | collective-permute-start | bytes 98312 | tf_op jit(solution)/shard_map/ppermute | solution.py:22
  104.5 7.7 %collective-permute-start.13 = (bf16[2,64,1,128]{3,1,2,0:T(8,128)(2,1)S(1)}, bf16[2,64,1,128]{3,1,2,0:T(8,128)(2,1)S(1)}, u32[]{:S(2)}, u32[]{:S(2)}) collective-permute-start(bf16[2,64,1,128]{3,1,2,0:T(8,128)(2,1)S(1)} %get-tuple-element.85), channel_id=1, source_target_pairs={{0,1},{1,2},{2,3},{3,4},{4,5},{5,6},{6,7},{7,8},{8,9},{9,10},{10,1... | collective-permute-start | bytes 98312 | tf_op jit(solution)/shard_map/ppermute | solution.py:19
  130.9 8.0 %collective-permute-start.14 = (f32[2,1,128]{2,1,0:T(1,128)S(1)}, f32[2,1,128]{2,1,0:T(1,128)S(1)}, u32[]{:S(2)}, u32[]{:S(2)}) collective-permute-start(f32[2,1,128]{2,1,0:T(1,128)S(1)} %get-tuple-element.138), channel_id=1, source_target_pairs={{1,0},{2,1},{3,2},{4,3},{5,4},{6,5},{7,6},{8,7},{9,8},{10,9},{11,1... | collective-permute-start | bytes 3080 | tf_op jit(solution)/shard_map/ppermute | solution.py:22
  132.2 7.4 %collective-permute-start.15 = (f32[2,1,128]{2,1,0:T(1,128)S(1)}, f32[2,1,128]{2,1,0:T(1,128)S(1)}, u32[]{:S(2)}, u32[]{:S(2)}) collective-permute-start(f32[2,1,128]{2,1,0:T(1,128)S(1)} %get-tuple-element.139), channel_id=1, source_target_pairs={{0,1},{1,2},{2,3},{3,4},{4,5},{5,6},{6,7},{7,8},{8,9},{9,10},{10,1... | collective-permute-start | bytes 3080 | tf_op jit(solution)/shard_map/ppermute | solution.py:19
  140.4 8.1 %collective-permute-start.16 = (bf16[2,64,1,128]{3,1,2,0:T(8,128)(2,1)S(1)}, bf16[2,64,1,128]{3,1,2,0:T(8,128)(2,1)S(1)}, u32[]{:S(2)}, u32[]{:S(2)}) collective-permute-start(bf16[2,64,1,128]{3,1,2,0:T(8,128)(2,1)S(1)} %get-tuple-element.78), channel_id=1, source_target_pairs={{1,0},{2,1},{3,2},{4,3},{5,4},{6,5},{7,6},{8,7},{9,8},{10,9},{11,1... | collective-permute-start | bytes 98312 | tf_op jit(solution)/shard_map/ppermute | solution.py:22
  141.7 7.6 %collective-permute-start.17 = (bf16[2,64,1,128]{3,1,2,0:T(8,128)(2,1)S(1)}, bf16[2,64,1,128]{3,1,2,0:T(8,128)(2,1)S(1)}, u32[]{:S(2)}, u32[]{:S(2)}) collective-permute-start(bf16[2,64,1,128]{3,1,2,0:T(8,128)(2,1)S(1)} %get-tuple-element.79), channel_id=1, source_target_pairs={{0,1},{1,2},{2,3},{3,4},{4,5},{5,6},{6,7},{7,8},{8,9},{9,10},{10,1... | collective-permute-start | bytes 98312 | tf_op jit(solution)/shard_map/ppermute | solution.py:19
  152.6 8.1 %collective-permute-start.18 = (bf16[2,64,1,128]{3,1,2,0:T(8,128)(2,1)S(1)}, bf16[2,64,1,128]{3,1,2,0:T(8,128)(2,1)S(1)}, u32[]{:S(2)}, u32[]{:S(2)}) collective-permute-start(bf16[2,64,1,128]{3,1,2,0:T(8,128)(2,1)S(1)} %get-tuple-element.72), channel_id=1, source_target_pairs={{1,0},{2,1},{3,2},{4,3},{5,4},{6,5},{7,6},{8,7},{9,8},{10,9},{11,1... | collective-permute-start | bytes 98312 | tf_op jit(solution)/shard_map/ppermute | solution.py:22
  153.9 7.7 %collective-permute-start.19 = (bf16[2,64,1,128]{3,1,2,0:T(8,128)(2,1)S(1)}, bf16[2,64,1,128]{3,1,2,0:T(8,128)(2,1)S(1)}, u32[]{:S(2)}, u32[]{:S(2)}) collective-permute-start(bf16[2,64,1,128]{3,1,2,0:T(8,128)(2,1)S(1)} %get-tuple-element.73), channel_id=1, source_target_pairs={{0,1},{1,2},{2,3},{3,4},{4,5},{5,6},{6,7},{7,8},{8,9},{9,10},{10,1... | collective-permute-start | bytes 98312 | tf_op jit(solution)/shard_map/ppermute | solution.py:19
  180.2 35.2 %copy-start.5 = (f32[2,8,128]{2,1,0:T(8,128)}, f32[2,8,128]{2,1,0:T(8,128)S(1)}, u32[]{:S(2)}) copy-start(f32[2,8,128]{2,1,0:T(8,128)S(1)} %multiply_subtract_fusion) | copy-start | bytes 24580
  180.2 8.6 %collective-permute-start.20 = (f32[2,1,128]{2,1,0:T(1,128)S(1)}, f32[2,1,128]{2,1,0:T(1,128)S(1)}, u32[]{:S(2)}, u32[]{:S(2)}) collective-permute-start(f32[2,1,128]{2,1,0:T(1,128)S(1)} %get-tuple-element.130), channel_id=1, source_target_pairs={{1,0},{2,1},{3,2},{4,3},{5,4},{6,5},{7,6},{8,7},{9,8},{10,9},{11,1... | collective-permute-start | bytes 3080 | tf_op jit(solution)/shard_map/ppermute | solution.py:22
  181.5 7.4 %collective-permute-start.21 = (f32[2,1,128]{2,1,0:T(1,128)S(1)}, f32[2,1,128]{2,1,0:T(1,128)S(1)}, u32[]{:S(2)}, u32[]{:S(2)}) collective-permute-start(f32[2,1,128]{2,1,0:T(1,128)S(1)} %get-tuple-element.131), channel_id=1, source_target_pairs={{0,1},{1,2},{2,3},{3,4},{4,5},{5,6},{6,7},{7,8},{8,9},{9,10},{10,1... | collective-permute-start | bytes 3080 | tf_op jit(solution)/shard_map/ppermute | solution.py:19
  189.8 8.5 %collective-permute-start.22 = (bf16[2,64,1,128]{3,1,2,0:T(8,128)(2,1)S(1)}, bf16[2,64,1,128]{3,1,2,0:T(8,128)(2,1)S(1)}, u32[]{:S(2)}, u32[]{:S(2)}) collective-permute-start(bf16[2,64,1,128]{3,1,2,0:T(8,128)(2,1)S(1)} %get-tuple-element.66), channel_id=1, source_target_pairs={{1,0},{2,1},{3,2},{4,3},{5,4},{6,5},{7,6},{8,7},{9,8},{10,9},{11,1... | collective-permute-start | bytes 98312 | tf_op jit(solution)/shard_map/ppermute | solution.py:22
  191.1 7.6 %collective-permute-start.23 = (bf16[2,64,1,128]{3,1,2,0:T(8,128)(2,1)S(1)}, bf16[2,64,1,128]{3,1,2,0:T(8,128)(2,1)S(1)}, u32[]{:S(2)}, u32[]{:S(2)}) collective-permute-start(bf16[2,64,1,128]{3,1,2,0:T(8,128)(2,1)S(1)} %get-tuple-element.67), channel_id=1, source_target_pairs={{0,1},{1,2},{2,3},{3,4},{4,5},{5,6},{6,7},{7,8},{8,9},{9,10},{10,1... | collective-permute-start | bytes 98312 | tf_op jit(solution)/shard_map/ppermute | solution.py:19
  201.5 0.7 copy-start.6
  204.6 8.2 %collective-permute-start.24 = (bf16[2,64,1,128]{3,1,2,0:T(8,128)(2,1)S(1)}, bf16[2,64,1,128]{3,1,2,0:T(8,128)(2,1)S(1)}, u32[]{:S(2)}, u32[]{:S(2)}) collective-permute-start(bf16[2,64,1,128]{3,1,2,0:T(8,128)(2,1)S(1)} %get-tuple-element.60), channel_id=1, source_target_pairs={{1,0},{2,1},{3,2},{4,3},{5,4},{6,5},{7,6},{8,7},{9,8},{10,9},{11,1... | collective-permute-start | bytes 98312 | tf_op jit(solution)/shard_map/ppermute | solution.py:22
  205.9 7.7 %collective-permute-start.25 = (bf16[2,64,1,128]{3,1,2,0:T(8,128)(2,1)S(1)}, bf16[2,64,1,128]{3,1,2,0:T(8,128)(2,1)S(1)}, u32[]{:S(2)}, u32[]{:S(2)}) collective-permute-start(bf16[2,64,1,128]{3,1,2,0:T(8,128)(2,1)S(1)} %get-tuple-element.61), channel_id=1, source_target_pairs={{0,1},{1,2},{2,3},{3,4},{4,5},{5,6},{6,7},{7,8},{8,9},{9,10},{10,1... | collective-permute-start | bytes 98312 | tf_op jit(solution)/shard_map/ppermute | solution.py:19
Sparse Core Ops, SparseCore 0:
  212.8 298.3 all-reduce.80
where the time goes:
time: 522 us; the launch traced here: 520 us
  blocking collectives  223 us (43%)
  waiting for transfers between devices  152 us (29%)
  starting transfers between devices  91.3 us (17%)
  matrix products  20 us (4%)
  other arithmetic  15.5 us (3%)
  between operations  14.9 us (3%)
    psum x1, waiting for transfers between devices, per_device(): lax.psum((jnp.stack(first_terms), jnp.stack(second_terms), jnp.stack(thir...  144 us
    psum x1, blocking collectives, per_device(): lax.psum((jnp.stack(first_terms), jnp.stack(second_terms), jnp.stack(thir...  133 us
    ppermute x13, starting transfers between devices, with_halo(): lax.ppermute(lax.slice_in_dim(block, block.shape[dim] - width, None, axis...  74.5 us
    psum x4, blocking collectives, frame_total(): return lax.psum(jnp.sum(masks * field, axis=0), 'tm')  69.7 us
    psum x1, blocking collectives, per_device(): frame_sum = lax.psum(jnp.sum(masks * equilibrium, axis=0), 'tm')  19.8 us
    ppermute x13, starting transfers between devices, with_halo(): lax.ppermute(lax.slice_in_dim(block, 0, width, axis=dim), axis, backward)  16.8 us
    dot_general x36, matrix products, conv_second_back(): jnp.einsum('oc,forw->fcrw', weight[tap_index], tap_view(grad_ext, -row_st...  11.3 us
  transfers between devices with their start and end apart: 27, of which 12 were waited for; matrix products, arithmetic and copies ran while one was open for 2% of the time, Pallas kernels for 0%

commit v1 on v0

v1 whole, which is shorter than its diff:
```python
import functools
import math

import jax
import jax.numpy as jnp
from jax import lax
from jax.experimental import pallas as pl
from jax.experimental.pallas import tpu as pltpu
from jax.sharding import Mesh, PartitionSpec as P

ITERS = 3
C = 64
W = 128
LANES = 2 * W
R = 8
HALO = 6
EXT = R + 2 * HALO
SMALL = 16
Q = 16
PIECE = 32
BF = jnp.bfloat16
F32 = jnp.float32

TM = ("zh", "core")
SPACE = ("zl", "y", "x")


def roll_cols(value, step):
    if step == 0:
        return value
    lane = lax.broadcasted_iota(jnp.int32, (value.shape[0], W), 1)
    edge = 0 if step > 0 else W - 1
    halves = []
    for frame in range(2):
        half = value[:, frame * W:(frame + 1) * W]
        half = pltpu.roll(half, step % W, 1)
        halves.append(jnp.where(lane == edge, 0.0, half))
    return jnp.concatenate(halves, axis=1)


def slope_parts(value):
    logistic = 0.5 * jnp.tanh(0.5 * value) + 0.5
    return logistic, logistic * (1.0 + value * (1.0 - logistic))


def put_slot(ref, at, count, value):
    for frame in range(2):
        ref[frame, pl.ds(at, count, stride=Q), :] = value[:, frame * W:(frame + 1) * W]


def take_slot(ref, at, count):
    return jnp.concatenate(
        [ref[frame, pl.ds(at, count, stride=Q), :] for frame in range(2)], axis=1)


def put_rows(ref, at, value):
    for frame in range(2):
        ref[frame, at:at + value.shape[0], :] = value[:, frame * W:(frame + 1) * W]


def take_rows(ref, first, last):
    return jnp.concatenate([ref[frame, first:last, :] for frame in range(2)], axis=1)


def fill_shifted(field, copies, sign):
    count = field.shape[0]
    for slot, step in enumerate((-1, 0, 1)):
        shifted = roll_cols(field, sign * step)
        high = shifted.astype(BF).astype(F32)
        put_slot(copies, slot, count, high)
        put_slot(copies, 3 + slot, count, shifted - high)


def dot(left, right):
    return jnp.dot(left, right, preferred_element_type=F32)


def dot_nt(left, right):
    return lax.dot_general(left, right, (((1,), (1,)), ((), ())), preferred_element_type=F32)


def adjoint_map(first, field, gate2, gate1, third_w, second_w, first_w, copies, d2, d1, taps):
    rows = EXT - 2 * first
    fill_shifted(field, copies, 1)
    for k in range(rows - 2):
        third = dot(third_w, take_rows(copies, k * Q, (k + 3) * Q).astype(BF))
        at = first + k
        d2[k * C:(k + 1) * C, :] = (gate2[at * C:(at + 1) * C, :] * third).astype(BF)
    for k in range(rows - 4):
        parts = dot(second_w, d2[k * C:(k + 3) * C, :])
        total = (
            roll_cols(parts[:C], -1) + parts[C:2 * C] + roll_cols(parts[2 * C:], 1)
        )
        at = first + k
        row = (gate1[at * C:(at + 1) * C, :] * total).astype(BF)
        d1[k * C:(k + 1) * C, :] = row
        put_rows(taps, k * Q, dot(first_w, row))
    count = rows - 6
    result = field[3:3 + count]
    for j in (-1, 0, 1):
        column = None
        for i in (-1, 0, 1):
            tap = 3 * (i + 1) + (j + 1)
            part = take_slot(taps, (1 - i) * Q + tap, count)
            column = part if column is None else column + part
        result = result + roll_cols(column, j)
    return result


def masked_sum(masks, field):
    product = masks * field
    return product[:, :W] + product[:, W:]


def twice(field):
    return jnp.concatenate([field, field], axis=1)


def gathered_sum(ref):
    total = ref[0]
    for k in range(1, ref.shape[0]):
        total = total + ref[k]
    return total


def unpack_kernel(step, low, own, high, part, up, masks, base, small):
    pieces = ((low, 0, HALO), (own, HALO, R), (high, HALO + R, HALO))
    for ref, at, count in pieces:
        put_rows(small, at * SMALL, ref[...].astype(F32).reshape(count * SMALL, LANES))
    def channel(slot):
        return take_slot(small, slot, EXT)
    up[...] = channel(0) + channel(1)
    mask = channel(4)
    masks[...] = mask
    fixed = channel(2) + channel(3)
    pair = channel(5)
    snapshot = pair[:, :W] + pair[:, W:]
    base[...] = fixed + step * mask * twice(snapshot)
    total = masked_sum(mask, fixed)
    for k in range(part.shape[0]):
        part[k, 0:EXT, :] = total
        part[k, EXT:, :] = jnp.zeros((part.shape[1] - EXT, W), F32)


def first_kernel(step, inside, low, own, high, sums, up, masks, base, third_w, second_w, first_w,
                 forward_w, part, moved, gate2, gate1, hidden, inputs, copies, d2, d1, taps):
    before = inside[0]
    after = inside[1]
    frame_sum = gathered_sum(sums)[:EXT]
    denoiser_input = base[...] - step * masks[...] * twice(frame_sum)
    copies[...] = jnp.zeros_like(copies)
    fill_shifted(denoiser_input, copies, -1)
    inputs[...] = take_rows(copies, (HALO - 1) * Q, (HALO + R + 1) * Q).astype(BF)

    def inside_of(at):
        if at < HALO:
            return before
        if at >= HALO + R:
            return after
        return None

    for k in range(EXT - 4):
        at = k + 2
        value = dot(forward_w[...], take_rows(copies, (at - 1) * Q, (at + 2) * Q).astype(BF))
        logistic, slope = slope_parts(value)
        keep = inside_of(at)
        gate1[k * C:(k + 1) * C, :] = slope if keep is None else slope * keep
        if keep is None:
            own_at = at - HALO
            hidden[own_at * C:(own_at + 1) * C, :] = (value * logistic).astype(BF)
    for k in range(EXT - 2):
        at = k + 1
        if at < HALO:
            value = low[at]
        elif at < HALO + R:
            value = own[at - HALO]
        else:
            value = high[at - HALO - R]
        slope = slope_parts(value.astype(F32))[1]
        keep = inside_of(at)
        gate2[k * C:(k + 1) * C, :] = slope if keep is None else slope * keep
    field = adjoint_map(0, up[...], gate2, gate1, third_w[...], second_w[...], first_w[...],
                        copies, d2, d1, taps)
    finish_wide(field, before, after, masks, part, moved)


def finish_wide(field, before, after, masks, part, moved):
    count = EXT - 6
    row = lax.broadcasted_iota(jnp.int32, field.shape, 0)
    keep = jnp.where(row < HALO - 3, before, jnp.where(row >= HALO - 3 + R, after, 1.0))
    field = field * keep
    moved[...] = field
    total = masked_sum(masks[3:3 + count, :], field)
    for k in range(part.shape[0]):
        part[k, 0:count, :] = total
        part[k, count:, :] = jnp.zeros((part.shape[1] - count, W), F32)


def narrow_field(step, sums, moved, up, masks):
    count = EXT - 6
    totals = gathered_sum(sums)[:count]
    return up[3:3 + count, :] + moved[...] - step * masks[3:3 + count, :] * twice(totals)


def second_kernel(step, sums, moved, up, masks, gate2, gate1, third_w, second_w, first_w,
                  part, out, copies, d2, d1, taps):
    copies[...] = jnp.zeros_like(copies)
    field = narrow_field(step, sums, moved, up, masks)
    result = adjoint_map(3, field, gate2, gate1, third_w[...], second_w[...], first_w[...],
                         copies, d2, d1, taps)
    out[...] = result
    total = masked_sum(masks[HALO:HALO + R, :], result)
    for k in range(part.shape[0]):
        part[k] = total


def update_kernel(step, sums, moved, up, masks, out):
    totals = gathered_sum(sums)
    out[...] = (up[HALO:HALO + R, :] + moved[...]
                - step * masks[HALO:HALO + R, :] * twice(totals))


def third_kernel(inside, low, own, high, masks, gate2, gate1, third_w, second_w, first_w,
                 part, moved, copies, d2, d1, taps, whole):
    copies[...] = jnp.zeros_like(copies)
    whole[0:HALO, :] = low[R - HALO:, :]
    whole[HALO:HALO + R, :] = own[...]
    whole[HALO + R:, :] = high[:HALO, :]
    field = adjoint_map(0, whole[...], gate2, gate1, third_w[...], second_w[...], first_w[...],
                        copies, d2, d1, taps)
    finish_wide(field, inside[0], inside[1], masks, part, moved)


def last_kernel(step, sums, moved, up, masks, gate2, gate1, saved, hidden, inputs, third_w,
                second_w, first_w, adjoint, grads, copies, d2, d1, taps, total):
    copies[...] = jnp.zeros_like(copies)
    field = narrow_field(step, sums, moved, up, masks)
    adjoint[0] = field[3:3 + R, :W]
    adjoint[1] = field[3:3 + R, W:]
    result = adjoint_map(3, field, gate2, gate1, third_w[...], second_w[...], first_w[...],
                         copies, d2, d1, taps)
    snapshot = masked_sum(masks[HALO:HALO + R, :], result)
    left = []
    right = []
    left_first = []
    right_first = []
    left_third = []
    right_third = []
    for r in range(R):
        left.append(d2[(r + 1) * C:(r + 4) * C, :])
        value = hidden[r * C:(r + 1) * C, :].astype(F32)
        right.append(jnp.concatenate(
            [roll_cols(value, 1), value, roll_cols(value, -1)], axis=0).astype(BF))
        left_first.append(inputs[r * Q:(r + 3) * Q, :])
        right_first.append(d1[(r + 1) * C:(r + 2) * C, :])
        left_third.append(take_rows(copies, (r + 2) * Q, (r + 5) * Q).astype(BF))
        wide = saved[r].astype(F32)
        right_third.append((wide * slope_parts(wide)[0]).astype(BF))
    def join(parts):
        return jnp.concatenate(parts, axis=1)
    second = dot_nt(join(left), join(right))
    first = dot_nt(join(left_first), join(right_first))
    third = dot_nt(join(left_third), join(right_third))
    total[:, 0:3 * C] = second
    total[0:3 * Q, 3 * C:] = first
    total[3 * Q:6 * Q, 3 * C:] = third
    total[6 * Q:, 3 * C:] = jnp.zeros((3 * C - 6 * Q, C), F32)
    count = grads.shape[0]
    rows = 3 * C // count
    lines = R // count
    for k in range(count):
        tail = jnp.zeros((grads.shape[1] - rows, LANES), F32)
        row = lax.broadcasted_iota(jnp.int32, tail.shape, 0)
        for line in range(lines):
            one = snapshot[k * lines + line:k * lines + line + 1, :]
            tail = jnp.where(row == line, twice(one), tail)
        grads[k] = jnp.concatenate([total[k * rows:(k + 1) * rows, :], tail], axis=0).astype(BF)


def reduce_kernel(received, out):
    total = received[0].astype(F32)
    for k in range(1, received.shape[0]):
        total = total + received[k].astype(F32)
    total = total.astype(BF)
    for k in range(out.shape[0]):
        out[k] = total


def join_kernel(rows, received, mine, out):
    total = received[0].astype(F32)
    for k in range(1, received.shape[0]):
        total = total + received[k].astype(F32)
    row = lax.broadcasted_iota(jnp.int32, total.shape, 0)
    total = jnp.where(row < rows, total, mine[0].astype(F32)).astype(BF)
    for k in range(out.shape[0]):
        out[k] = total


def output_kernel(step, scale, received, snapshot, first, second, third, total):
    count = received.shape[0]
    rows = 3 * C // count
    lines = R // count
    for k in range(count):
        piece = received[k].astype(F32)
        total[k * rows:(k + 1) * rows, :] = piece[:rows] * scale
        snapshot[k * lines:(k + 1) * lines, :] = step * piece[rows:rows + lines, :W]
    for i in (-1, 0, 1):
        for j in (-1, 0, 1):
            tap = 3 * (i + 1) + (j + 1)
            back = 1 - i
            ahead = 1 + i
            second[tap] = total[back * C:(back + 1) * C, (j + 1) * C:(j + 2) * C]
            at = ahead * Q + j + 1
            first[tap:tap + 1, :] = total[at:at + 1, 3 * C:] + total[at + 3:at + 4, 3 * C:]
            at = 3 * Q + back * Q + j + 1
            third[tap:tap + 1, :] = total[at:at + 1, 3 * C:] + total[at + 3:at + 4, 3 * C:]


def call(kernel, outs, scratch, *operands, specs=None):
    grid = () if specs is None else (1,)
    if specs is None:
        specs = [pl.BlockSpec(memory_space=pltpu.VMEM)] * len(operands)
    return pl.pallas_call(
        kernel,
        grid=grid,
        out_shape=[jax.ShapeDtypeStruct(shape, dtype) for shape, dtype in outs],
        in_specs=specs,
        out_specs=[pl.BlockSpec(memory_space=pltpu.VMEM)] * len(outs),
        scratch_shapes=[pltpu.VMEM(shape, dtype) for shape, dtype in scratch],
        compiler_params=pltpu.CompilerParams(vmem_limit_bytes=40 * 2**20),
    )(*operands)


def split_parts(field):
    high = field.astype(BF)
    return high, (field - high.astype(F32)).astype(BF)


def by_row(field):
    return jnp.transpose(field, (1, 0, 2)).reshape(R, LANES)


def pad_slots(weight):
    both = jnp.concatenate([weight, weight, jnp.zeros((3, Q - 6, C), BF)], axis=1)
    return jnp.transpose(both.reshape(3 * Q, C))


def exchange(value, axis):
    return lax.all_to_all(value, axis, 0, 0, tiled=True)


def from_neighbours(value):
    count = lax.axis_size(SPACE)
    forward = [(i, i + 1) for i in range(count - 1)]
    backward = [(i + 1, i) for i in range(count - 1)]
    return forward, backward


def per_device(equilibrium, measurement, coding_masks, upstream, saved_second, conv_first,
               conv_second, conv_third):
    frames = lax.axis_size(TM)
    tiles = lax.axis_size(SPACE)
    total_frames = 2 * frames
    step = 1.0 / total_frames
    scale = 1.0 / math.sqrt(total_frames * R * tiles * W)
    forward = [(i, i + 1) for i in range(tiles - 1)]
    backward = [(i + 1, i) for i in range(tiles - 1)]
    place = lax.axis_index(SPACE)
    inside = jnp.stack([place > 0, place < tiles - 1]).astype(F32)

    saved = jnp.transpose(saved_second, (2, 1, 0, 3)).reshape(R, C, LANES)
    channels = [*split_parts(by_row(upstream)), *split_parts(by_row(equilibrium)),
                by_row(coding_masks).astype(BF),
                jnp.concatenate(split_parts(measurement), axis=1)]
    channels += [jnp.zeros((R, LANES), BF)] * (SMALL - len(channels))
    pack = jnp.concatenate([saved, jnp.stack(channels, axis=1)], axis=1)
    low = lax.ppermute(pack[R - HALO:], SPACE, forward)
    high = lax.ppermute(pack[:HALO], SPACE, backward)

    first_taps = conv_first.reshape(3, 3, C)
    forward_w = pad_slots(first_taps)
    third_w = pad_slots(conv_third.reshape(3, 3, C)[::-1])
    second_w = jnp.transpose(
        conv_second.reshape(3, 3, C, C)[::-1], (1, 3, 0, 2)).reshape(3 * C, 3 * C)
    first_w = jnp.concatenate([conv_first, jnp.zeros((Q - 9, C), BF)], axis=0)

    def rows_of(count, channels_at, width):
        return pl.BlockSpec((count, width, LANES), lambda _: (0, channels_at, 0))

    whole = pl.BlockSpec(memory_space=pltpu.VMEM)
    scalars = pl.BlockSpec(memory_space=pltpu.SMEM)
    ext = ((EXT, LANES), F32)
    part, up, masks, base = call(
        functools.partial(unpack_kernel, step),
        [((frames, 24, W), F32), ext, ext, ext],
        [((2, EXT * SMALL, W), F32)],
        low, pack, high,
        specs=[rows_of(HALO, C // SMALL, SMALL), rows_of(R, C // SMALL, SMALL),
               rows_of(HALO, C // SMALL, SMALL)])
    sums = exchange(part, TM)

    narrow = EXT - 6
    weights = (third_w, second_w, first_w)
    wide_scratch = [((2, EXT * Q, W), F32), (((EXT - 2) * C, LANES), BF),
                    (((EXT - 4) * C, LANES), BF), ((2, (EXT - 4) * Q, W), F32)]
    slim_scratch = [((2, narrow * Q, W), F32), (((narrow - 2) * C, LANES), BF),
                    (((narrow - 4) * C, LANES), BF), ((2, (narrow - 4) * Q, W), F32)]
    wide_outs = [((frames, 16, W), F32), ((narrow, LANES), F32)]
    part, moved, gate2, gate1, hidden, inputs = call(
        functools.partial(first_kernel, step),
        wide_outs + [(((EXT - 2) * C, LANES), F32), (((EXT - 4) * C, LANES), F32),
                     ((R * C, LANES), BF), (((R + 2) * Q, LANES), BF)],
        wide_scratch,
        inside, low, pack, high, sums, up, masks, base, *weights, forward_w,
        specs=[scalars, rows_of(HALO, 0, C), rows_of(R, 0, C), rows_of(HALO, 0, C)] + [whole] * 8)
    sums = exchange(part, TM)

    part, moved = call(
        functools.partial(second_kernel, step),
        [((frames, R, W), F32), ((R, LANES), F32)], slim_scratch,
        sums, moved, up, masks, gate2, gate1, *weights)
    sums = exchange(part, TM)

    field, = call(functools.partial(update_kernel, step), [((R, LANES), F32)], [],
                  sums, moved, up, masks)
    field_low = lax.ppermute(field, SPACE, forward)
    field_high = lax.ppermute(field, SPACE, backward)
    part, moved = call(
        third_kernel, wide_outs, wide_scratch + [ext],
        inside, field_low, field, field_high, masks, gate2, gate1, *weights,
        specs=[scalars] + [whole] * 9)
    sums = exchange(part, TM)

    piece = 3 * C // frames + max(8, R // frames)
    adjoint, grads = call(
        functools.partial(last_kernel, step),
        [((2, R, W), F32), ((frames, piece, LANES), BF)],
        slim_scratch + [((3 * C, LANES), F32)],
        sums, moved, up, masks, gate2, gate1, pack, hidden, inputs, *weights,
        specs=[whole] * 6 + [rows_of(R, 0, C)] + [whole] * 5)

    mine = exchange(grads, TM)
    count_y = lax.axis_size("y")
    count_near = lax.axis_size(("zl", "x"))
    mine, = call(reduce_kernel, [((count_y, piece, LANES), BF)], [], mine)
    received = exchange(mine, "y")
    received, = call(reduce_kernel, [((count_near, piece, LANES), BF)], [], received)
    received = exchange(received, ("zl", "x"))
    received, = call(functools.partial(join_kernel, 3 * C // frames),
                     [((frames, piece, LANES), BF)], [], received, mine)
    received = exchange(received, TM)
    snapshot, grad_first, grad_second, grad_third = call(
        functools.partial(output_kernel, step, scale),
        [((R, W), F32), ((9, C), F32), ((9, C, C), F32), ((9, C), F32)],
        [((3 * C, LANES), F32)], received)
    return adjoint, snapshot, grad_first, grad_second, grad_third


AXES = (("zh", 4), ("core", 2), ("zl", 2), ("y", 8), ("x", 4))


def solution(mesh, axes=AXES):
    names = tuple(name for name, _ in axes)
    sizes = tuple(size for _, size in axes)
    fine = Mesh(mesh.devices.reshape(sizes), names)
    placed = (
        P(TM, SPACE, None),
        P(SPACE, None),
        P(TM, SPACE, None),
        P(TM, SPACE, None),
        P(TM, None, SPACE, None),
        P(),
        P(),
        P(),
    )
    return jax.shard_map(
        per_device,
        mesh=fine,
        in_specs=placed,
        out_specs=(P(TM, SPACE, None), P(SPACE, None), P(), P(), P()),
        check_vma=False,
    )
```

time: 522 us -> 149 us (0.29)
  waiting for transfers between devices: 152 us -> 9.82 us
  blocking collectives: 223 us -> 91.2 us
  starting transfers between devices: 91.3 us -> 25.6 us
  matrix products: 20 us -> 0 us
  Pallas kernels: 0 us -> 14.4 us
  between operations: 14.9 us -> 0.86 us
  other arithmetic: 15.5 us -> 1.66 us
    psum x6 -> x0, blocking collectives: 223 us -> none  [the longest x1 133 us: per_device(): lax.psum((jnp.stack(first_terms), jnp.stack(second_terms), jnp.stack(thir...]
    psum x1 -> x0, waiting for transfers between devices: 144 us -> none  [per_device(): lax.psum((jnp.stack(first_terms), jnp.stack(second_terms), jnp.stack(thir...]
    all_to_all x0 -> x7, blocking collectives: none -> 91.2 us  [exchange(): return lax.all_to_all(value, axis, 0, 0, tiled=True)]
    ppermute x26 -> x4, starting transfers between devices: 91.3 us -> 12 us  [the longest x1 4.74 us: per_device(): field_low = lax.ppermute(field, SPACE, forward)]
    dot_general x81 -> x0, matrix products: 20 us -> none  [the longest x36 11.3 us: conv_second_back(): jnp.einsum('oc,forw->fcrw', weight[tap_index], tap_view(grad_ext, -row_st...]
    pallas_call x0 -> x10, Pallas kernels: none -> 14.4 us  [call(): pl.pallas_call(kernel, grid=grid, out_shape=[jax.ShapeDtypeStruct(shape,...]
    all_to_all x0 -> x1, starting transfers between devices: none -> 13.6 us  [exchange(): return lax.all_to_all(value, axis, 0, 0, tiled=True)]
    all_to_all x0 -> x1, waiting for transfers between devices: none -> 6.09 us  [exchange(): return lax.all_to_all(value, axis, 0, 0, tiled=True)]
  transfers between devices with their start and end apart: 27 -> 5, of which waited for: 12 -> 4; matrix products, arithmetic and copies ran while one was open for 2% -> 1% of each run, Pallas kernels for 0% -> 0%
where the time goes in v1:
time: 149 us; the launch traced here: 148 us
  blocking collectives  91.2 us (61%)
  starting transfers between devices  25.6 us (17%)
  Pallas kernels  14.4 us (10%)
  waiting for transfers between devices  9.82 us (7%)
  local copies, waits for them, and re-layouts  4.53 us (3%)
  other arithmetic  1.66 us (1%)
    all_to_all x7, blocking collectives, exchange(): return lax.all_to_all(value, axis, 0, 0, tiled=True)  91.2 us
    pallas_call x10, Pallas kernels, call(): pl.pallas_call(kernel, grid=grid, out_shape=[jax.ShapeDtypeStruct(shape,...  14.4 us
    all_to_all x1, starting transfers between devices, exchange(): return lax.all_to_all(value, axis, 0, 0, tiled=True)  13.6 us
    all_to_all x1, waiting for transfers between devices, exchange(): return lax.all_to_all(value, axis, 0, 0, tiled=True)  6.09 us
    ppermute x1, starting transfers between devices, per_device(): field_low = lax.ppermute(field, SPACE, forward)  4.74 us
    ppermute x1, starting transfers between devices, per_device(): low = lax.ppermute(pack[R - HALO:], SPACE, forward)  4.59 us
  transfers between devices with their start and end apart: 5, of which 4 were waited for; matrix products, arithmetic and copies ran while one was open for 1% of the time, Pallas kernels for 0%

profile of v1, /device:TPU:1, one launch (start us, length us, event | category | flops | bytes accessed | tf_op | source)
XLA Modules:
  0.0 148.1 jit_solution(10688845611055871820)
XLA Ops:
  0.6 0.7 copy.23
  1.3 0.7 copy.22
  2.1 0.7 convert_bitcast_fusion
  2.8 0.8 subtract_convert_fusion.2
  3.6 1.2 copy.21
  4.8 0.0 copy-start.2
  4.8 0.0 copy-start.1
  4.8 0.2 reshape.107
  5.0 0.2 concatenate.24.own.saved
  5.2 0.0 copy-start
  5.3 1.4 collective-permute-start.1
  6.7 4.6 %collective-permute-start = (bf16[6,80,256]{2,1,0:T(8,128)(2,1)S(1)}, bf16[6,80,256]{2,1,0:T(8,128)(2,1)S(1)}, u32[]{:S(2)}, u32[]{:S(2)}) collective-permute-start(bf16[6,80,256]{2,1,0:T(8,128)(2,1)S(1)} %get-tuple-element.48), channel_id=1, source_target_pairs={{0,1},{1,2},{2,3},{3,4},{4,5},{5,6},{6,7},{7,8},{8,9},{9,10},{10,1... | collective-permute-start | bytes 737288 | tf_op jit(solution)/shard_map/ppermute | solution.py:377
  11.3 0.0 copy-done.2
  11.3 0.0 copy-done.1
  11.4 0.1 pad.6.clone
  11.5 1.5 %collective-permute-done.1.high = bf16[6,80,256]{2,1,0:T(8,128)(2,1)S(1)} collective-permute-done((bf16[6,80,256]{2,1,0:T(8,128)(2,1)S(1)}, bf16[6,80,256]{2,1,0:T(8,128)(2,1)S(1)}, u32[]{:S(2)}, u32[]{:S(2)}) %collective-permute-start.1) | collective-permute-done | bytes 245792 | tf_op jit(solution)/shard_map/ppermute | solution.py:378
  12.9 1.5 collective-permute-done.low
  14.4 0.7 shard_map.119
  15.1 13.6 %all-to-all-start = ((f32[8,24,128]{2,1,0:T(8,128)}), f32[8,24,128]{2,1,0:T(8,128)S(1)}, u32[]{:S(2)}, u32[]{:S(2)}) async-start(f32[8,24,128]{2,1,0:T(8,128)} %get-tuple-element.25), calls=%async_computation | async-start | bytes 196608 | tf_op jit(solution)/shard_map/all_to_all | solution.py:349
  28.7 0.1 maximum_maximum_fusion.1
  28.8 0.1 copy.26
  28.9 0.1 copy.28
  29.0 0.0 copy-done
  29.0 0.2 copy.27
  29.2 0.8 rev.7
  30.0 0.2 reshape.113.second_w
  30.1 0.1 add_convert_fusion.inside
  30.2 6.1 %all-to-all-done.sums = f32[8,24,128]{2,1,0:T(8,128)S(1)} async-done(((f32[8,24,128]{2,1,0:T(8,128)}), f32[8,24,128]{2,1,0:T(8,128)S(1)}, u32[]{:S(2)}, u32[]{:S(2)}) %all-to-all-start) | async-done | bytes 98336 | tf_op jit(solution)/shard_map/all_to_all | solution.py:349
  36.3 4.2 %shard_map.120 = (f32[8,16,128]{2,1,0:T(8,128)S(1)}, f32[14,256]{1,0:T(8,128)S(1)}, f32[1152,256]{1,0:T(8,128)S(1)}, f32[1024,256]{1,0:T(8,128)S(1)}, bf16[512,2...) custom-call(f32[2]{0:T(128)S(1)} %add_convert_fusion.inside, bf16[6,80,256]{2,1,0:T(8,128)(2,1)S(1)} %collective-permute-done.low, ...), custom_call_target="tpu_custom_call" | custom-call | tf_op jit(solution)/shard_map/pallas_call | solution.py:323
  40.5 10.9 %all_to_all.40.sums = f32[8,16,128]{2,1,0:T(8,128)S(1)} all-to-all(f32[8,16,128]{2,1,0:T(8,128)S(1)} %get-tuple-element.29), channel_id=1, replica_groups=mesh['zh'=4,'core'=2,'zl'=2,'y'=8,'x'=4] {'zh','core'}, dimensions={0} | all-to-all | bytes 131072 | tf_op jit(solution)/shard_map/all_to_all | solution.py:349
  51.4 2.2 %shard_map.121 = (f32[8,8,128]{2,1,0:T(8,128)S(1)}, f32[8,256]{1,0:T(8,128)S(1)}) custom-call(f32[8,16,128]{2,1,0:T(8,128)S(1)} %all_to_all.40.sums, f32[14,256]{1,0:T(8,128)S(1)} %get-tuple-element.30.moved, f32[20,256]{1,0:T(8,128)S(1)} %get-tuple-element.26.up, f32[20,256]{1,0:T(8,128)S(1)} %get-tuple-element.27.masks, ...), custom_call_target="tpu_custom_call" | custom-call | tf_op jit(solution)/shard_map/pallas_call | solution.py:323
  53.7 10.3 %all_to_all.41.sums = f32[8,8,128]{2,1,0:T(8,128)S(1)} all-to-all(f32[8,8,128]{2,1,0:T(8,128)S(1)} %get-tuple-element.33), channel_id=1, replica_groups=mesh['zh'=4,'core'=2,'zl'=2,'y'=8,'x'=4] {'zh','core'}, dimensions={0} | all-to-all | bytes 65536 | tf_op jit(solution)/shard_map/all_to_all | solution.py:349
  64.1 1.3 collective-permute-start.3
  65.4 4.7 %collective-permute-start.2 = (f32[8,256]{1,0:T(8,128)S(1)}, f32[8,256]{1,0:T(8,128)S(1)}, u32[]{:S(2)}, u32[]{:S(2)}) collective-permute-start(f32[8,256]{1,0:T(8,128)S(1)} %shard_map.122.own), channel_id=1, source_target_pairs={{0,1},{1,2},{2,3},{3,4},{4,5},{5,6},{6,7},{7,8},{8,9},{9,10},{10,1... | collective-permute-start | bytes 24584 | tf_op jit(solution)/shard_map/ppermute | solution.py:426
  70.1 0.0 collective-permute-done.3.high
  70.1 0.8 collective-permute-done.2.low
  70.9 3.7 %shard_map.123 = (f32[8,16,128]{2,1,0:T(8,128)S(1)}, f32[14,256]{1,0:T(8,128)S(1)}) custom-call(f32[2]{0:T(128)S(1)} %add_convert_fusion.inside, f32[8,256]{1,0:T(8,128)S(1)} %collective-permute-done.2.low, f32[8,256]{1,0:T(8,128)S(1)} %shard_map.122.own, f32[8,256]{1,0:T(8,128)S(1)} %collective-permute-done.3.high, f32[20,256]{1,0:T(8,128)S(1)} %get-tuple-element.27.masks, ...), custom_call_target="tpu_custom_call" | custom-call | tf_op jit(solution)/shard_map/pallas_call | solution.py:323
  74.6 11.4 %all_to_all.42.sums = f32[8,16,128]{2,1,0:T(8,128)S(1)} all-to-all(f32[8,16,128]{2,1,0:T(8,128)S(1)} %get-tuple-element.35), channel_id=1, replica_groups=mesh['zh'=4,'core'=2,'zl'=2,'y'=8,'x'=4] {'zh','core'}, dimensions={0} | all-to-all | bytes 131072 | tf_op jit(solution)/shard_map/all_to_all | solution.py:349
  86.0 2.6 %shard_map.124 = (f32[2,8,128]{2,1,0:T(8,128)}, bf16[8,32,256]{2,1,0:T(8,128)(2,1)S(1)}) custom-call(f32[8,16,128]{2,1,0:T(8,128)S(1)} %all_to_all.42.sums, f32[14,256]{1,0:T(8,128)S(1)} %get-tuple-element.36.moved, f32[20,256]{1,0:T(8,128)S(1)} %get-tuple-element.26.up, f32[20,256]{1,0:T(8,128)S(1)} %get-tuple-element.27.masks, ...), custom_call_target="tpu_custom_call" | custom-call | tf_op jit(solution)/shard_map/pallas_call | solution.py:323
  88.6 11.3 %all_to_all.43.received = bf16[8,32,256]{2,1,0:T(8,128)(2,1)S(1)} all-to-all(bf16[8,32,256]{2,1,0:T(8,128)(2,1)S(1)} %get-tuple-element.40), channel_id=1, replica_groups=mesh['zh'=4,'core'=2,'zl'=2,'y'=8,'x'=4] {'zh','core'}, dimensions={0} | all-to-all | bytes 262144 | tf_op jit(solution)/shard_map/all_to_all | solution.py:349
  100.0 24.8 %all_to_all.44.received = bf16[8,32,256]{2,1,0:T(8,128)(2,1)S(1)} all-to-all(bf16[8,32,256]{2,1,0:T(8,128)(2,1)S(1)} %shard_map.125.mine), channel_id=1, replica_groups=mesh['zh'=4,'core'=2,'zl'=2,'y'=8,'x'=4] {'y'}, dimensions={0} | all-to-all | bytes 262144 | tf_op jit(solution)/shard_map/all_to_all | solution.py:349
  124.8 7.8 %all_to_all.45.received = bf16[8,32,256]{2,1,0:T(8,128)(2,1)S(1)} all-to-all(bf16[8,32,256]{2,1,0:T(8,128)(2,1)S(1)} %shard_map.126), channel_id=1, replica_groups=mesh['zh'=4,'core'=2,'zl'=2,'y'=8,'x'=4] {'zl','x'}, dimensions={0} | all-to-all | bytes 262144 | tf_op jit(solution)/shard_map/all_to_all | solution.py:349
  132.6 14.7 %all_to_all.46.received = bf16[8,32,256]{2,1,0:T(8,128)(2,1)S(1)} all-to-all(bf16[8,32,256]{2,1,0:T(8,128)(2,1)S(1)} %shard_map.127), channel_id=1, replica_groups=mesh['zh'=4,'core'=2,'zl'=2,'y'=8,'x'=4] {'zh','core'}, dimensions={0} | all-to-all | bytes 262144 | tf_op jit(solution)/shard_map/all_to_all | solution.py:349
  147.3 0.8 shard_map.128
  (18 shorter events, 0.2 us)
Async XLA Ops:
  4.8 6.5 %copy-start.2 = (bf16[9,64]{1,0:T(8,128)(2,1)S(1)}, bf16[9,64]{1,0:T(8,128)(2,1)}, u32[]{:S(2)}) copy-start(bf16[9,64]{1,0:T(8,128)(2,1)} %param.15) | copy-start | bytes 3460
  4.8 6.5 %copy-start.1 = (bf16[9,64]{1,0:T(8,128)(2,1)S(1)}, bf16[9,64]{1,0:T(8,128)(2,1)}, u32[]{:S(2)}) copy-start(bf16[9,64]{1,0:T(8,128)(2,1)} %param.13) | copy-start | bytes 3460
  5.2 23.8 %copy-start = (bf16[9,64,64]{2,1,0:T(8,128)(2,1)S(1)}, bf16[9,64,64]{2,1,0:T(8,128)(2,1)}, u32[]{:S(2)}) copy-start(bf16[9,64,64]{2,1,0:T(8,128)(2,1)} %param.14) | copy-start | bytes 221188
  5.3 7.7 %collective-permute-start.1 = (bf16[6,80,256]{2,1,0:T(8,128)(2,1)S(1)}, bf16[6,80,256]{2,1,0:T(8,128)(2,1)S(1)}, u32[]{:S(2)}, u32[]{:S(2)}) collective-permute-start(bf16[6,80,256]{2,1,0:T(8,128)(2,1)S(1)} %get-tuple-element.47), channel_id=1, source_target_pairs={{1,0},{2,1},{3,2},{4,3},{5,4},{6,5},{7,6},{8,7},{9,8},{10,9},{11,1... | collective-permute-start | bytes 737288 | tf_op jit(solution)/shard_map/ppermute | solution.py:378
  6.7 7.7 %collective-permute-start = (bf16[6,80,256]{2,1,0:T(8,128)(2,1)S(1)}, bf16[6,80,256]{2,1,0:T(8,128)(2,1)S(1)}, u32[]{:S(2)}, u32[]{:S(2)}) collective-permute-start(bf16[6,80,256]{2,1,0:T(8,128)(2,1)S(1)} %get-tuple-element.48), channel_id=1, source_target_pairs={{0,1},{1,2},{2,3},{3,4},{4,5},{5,6},{6,7},{7,8},{8,9},{9,10},{10,1... | collective-permute-start | bytes 737288 | tf_op jit(solution)/shard_map/ppermute | solution.py:377
  15.1 21.2 %all-to-all-start = ((f32[8,24,128]{2,1,0:T(8,128)}), f32[8,24,128]{2,1,0:T(8,128)S(1)}, u32[]{:S(2)}, u32[]{:S(2)}) async-start(f32[8,24,128]{2,1,0:T(8,128)} %get-tuple-element.25), calls=%async_computation | async-start | bytes 196608 | tf_op jit(solution)/shard_map/all_to_all | solution.py:349
  64.1 6.0 %collective-permute-start.3 = (f32[8,256]{1,0:T(8,128)S(1)}, f32[8,256]{1,0:T(8,128)S(1)}, u32[]{:S(2)}, u32[]{:S(2)}) collective-permute-start(f32[8,256]{1,0:T(8,128)S(1)} %shard_map.122.own), channel_id=1, source_target_pairs={{1,0},{2,1},{3,2},{4,3},{5,4},{6,5},{7,6},{8,7},{9,8},{10,9},{11,1... | collective-permute-start | bytes 24584 | tf_op jit(solution)/shard_map/ppermute | solution.py:427
  65.4 5.5 %collective-permute-start.2 = (f32[8,256]{1,0:T(8,128)S(1)}, f32[8,256]{1,0:T(8,128)S(1)}, u32[]{:S(2)}, u32[]{:S(2)}) collective-permute-start(f32[8,256]{1,0:T(8,128)S(1)} %shard_map.122.own), channel_id=1, source_target_pairs={{0,1},{1,2},{2,3},{3,4},{4,5},{5,6},{6,7},{7,8},{8,9},{9,10},{10,1... | collective-permute-start | bytes 24584 | tf_op jit(solution)/shard_map/ppermute | solution.py:426

commit v2 on v1

--- a/solution.py
+++ b/solution.py
@@ -23,6 +23,8 @@
 
 TM = ("zh", "core")
 SPACE = ("zl", "y", "x")
+NEAR = ("core", "zl", "x")
+FAR = ("zh", "y")
 
 
 def roll_cols(value, step):
@@ -79,7 +81,7 @@
     return lax.dot_general(left, right, (((1,), (1,)), ((), ())), preferred_element_type=F32)
 
 
-def adjoint_map(first, field, gate2, gate1, third_w, second_w, first_w, copies, d2, d1, taps):
+def back_rows(first, field, gate2, third_w, second_w, copies, d2):
     rows = EXT - 2 * first
     fill_shifted(field, copies, 1)
     for k in range(rows - 2):
@@ -91,11 +93,20 @@
         total = (
             roll_cols(parts[:C], -1) + parts[C:2 * C] + roll_cols(parts[2 * C:], 1)
         )
+        yield k, total
+
+
+def adjoint_map(first, field, gate2, gate1, third_w, second_w, first_w, copies, d2, d1, taps):
+    for k, total in back_rows(first, field, gate2, third_w, second_w, copies, d2):
         at = first + k
         row = (gate1[at * C:(at + 1) * C, :] * total).astype(BF)
         d1[k * C:(k + 1) * C, :] = row
         put_rows(taps, k * Q, dot(first_w, row))
-    count = rows - 6
+    return map_end(first, field, taps)
+
+
+def map_end(first, field, taps):
+    count = EXT - 2 * first - 6
     result = field[3:3 + count]
     for j in (-1, 0, 1):
         column = None
@@ -121,6 +132,37 @@
     for k in range(1, ref.shape[0]):
         total = total + ref[k]
     return total
+
+
+def pack_kernel(upstream, equilibrium, masks, measurement, saved, out, small):
+    small[...] = jnp.zeros_like(small)
+    for frame in range(2):
+        fields = (*split_parts(upstream[frame]), *split_parts(equilibrium[frame]),
+                  masks[frame].astype(F32), split_parts(measurement[...])[frame])
+        for slot, field in enumerate(fields):
+            small[frame, pl.ds(slot, R, stride=SMALL), :] = field.astype(F32)
+        lanes = slice(frame * W, (frame + 1) * W)
+        out[:, C:, lanes] = small[frame].astype(BF).reshape(R, SMALL, W)
+        out[:, :C, lanes] = jnp.swapaxes(saved[frame].astype(F32), 0, 1).astype(BF)
+
+
+def weights_kernel(first, second, third, forward_w, third_w, second_w, first_w):
+    forward = first[...].astype(F32)
+    backward = third[...].astype(F32)
+    pad = jnp.zeros((Q - 6, C), F32)
+    ahead = []
+    back = []
+    for i in range(3):
+        row = forward[3 * i:3 * i + 3]
+        ahead += [row, row, pad]
+        row = backward[6 - 3 * i:9 - 3 * i]
+        back += [row, row, pad]
+        for j in range(3):
+            tile = second[3 * (2 - i) + j].astype(F32)
+            second_w[j * C:(j + 1) * C, i * C:(i + 1) * C] = jnp.transpose(tile).astype(BF)
+    forward_w[...] = jnp.transpose(jnp.concatenate(ahead, axis=0)).astype(BF)
+    third_w[...] = jnp.transpose(jnp.concatenate(back, axis=0)).astype(BF)
+    first_w[...] = jnp.concatenate([forward, jnp.zeros((Q - 9, C), F32)], axis=0).astype(BF)
 
 
 def unpack_kernel(step, low, own, high, part, up, masks, base, small):
@@ -142,32 +184,16 @@
         part[k, EXT:, :] = jnp.zeros((part.shape[1] - EXT, W), F32)
 
 
-def first_kernel(step, inside, low, own, high, sums, up, masks, base, third_w, second_w, first_w,
-                 forward_w, part, moved, gate2, gate1, hidden, inputs, copies, d2, d1, taps):
-    before = inside[0]
-    after = inside[1]
-    frame_sum = gathered_sum(sums)[:EXT]
-    denoiser_input = base[...] - step * masks[...] * twice(frame_sum)
+def keep_row(value, at, before, after):
+    if at < HALO:
+        return value * before
+    if at >= HALO + R:
+        return value * after
+    return value
+
+
+def early_kernel(inside, low, own, high, up, third_w, second_w, gate2, back, copies, d2):
     copies[...] = jnp.zeros_like(copies)
-    fill_shifted(denoiser_input, copies, -1)
-    inputs[...] = take_rows(copies, (HALO - 1) * Q, (HALO + R + 1) * Q).astype(BF)
-
-    def inside_of(at):
-        if at < HALO:
-            return before
-        if at >= HALO + R:
-            return after
-        return None
-
-    for k in range(EXT - 4):
-        at = k + 2
-        value = dot(forward_w[...], take_rows(copies, (at - 1) * Q, (at + 2) * Q).astype(BF))
-        logistic, slope = slope_parts(value)
-        keep = inside_of(at)
-        gate1[k * C:(k + 1) * C, :] = slope if keep is None else slope * keep
-        if keep is None:
-            own_at = at - HALO
-            hidden[own_at * C:(own_at + 1) * C, :] = (value * logistic).astype(BF)
     for k in range(EXT - 2):
         at = k + 1
         if at < HALO:
@@ -177,11 +203,31 @@
         else:
             value = high[at - HALO - R]
         slope = slope_parts(value.astype(F32))[1]
-        keep = inside_of(at)
-        gate2[k * C:(k + 1) * C, :] = slope if keep is None else slope * keep
-    field = adjoint_map(0, up[...], gate2, gate1, third_w[...], second_w[...], first_w[...],
-                        copies, d2, d1, taps)
-    finish_wide(field, before, after, masks, part, moved)
+        gate2[k * C:(k + 1) * C, :] = keep_row(slope, at, inside[0], inside[1])
+    for k, total in back_rows(0, up[...], gate2, third_w[...], second_w[...], copies, d2):
+        back[k * C:(k + 1) * C, :] = total
+
+
+def first_kernel(step, inside, sums, up, masks, base, back, first_w, forward_w,
+                 part, moved, gate1, hidden, inputs, copies, taps):
+    frame_sum = gathered_sum(sums)[:EXT]
+    denoiser_input = base[...] - step * masks[...] * twice(frame_sum)
+    copies[...] = jnp.zeros_like(copies)
+    fill_shifted(denoiser_input, copies, -1)
+    inputs[...] = take_rows(copies, (HALO - 1) * Q, (HALO + R + 1) * Q).astype(BF)
+    for k in range(EXT - 4):
+        at = k + 2
+        value = dot(forward_w[...], take_rows(copies, (at - 1) * Q, (at + 2) * Q).astype(BF))
+        logistic, slope = slope_parts(value)
+        slope = keep_row(slope, at, inside[0], inside[1])
+        gate1[k * C:(k + 1) * C, :] = slope
+        if HALO <= at < HALO + R:
+            own_at = at - HALO
+            hidden[own_at * C:(own_at + 1) * C, :] = (value * logistic).astype(BF)
+        row = (slope * back[k * C:(k + 1) * C, :]).astype(BF)
+        put_rows(taps, k * Q, dot(first_w[...], row))
+    field = map_end(0, up[...], taps)
+    finish_wide(field, inside[0], inside[1], masks, part, moved)
 
 
 def finish_wide(field, before, after, masks, part, moved):
@@ -261,49 +307,56 @@
     second = dot_nt(join(left), join(right))
     first = dot_nt(join(left_first), join(right_first))
     third = dot_nt(join(left_third), join(right_third))
-    total[:, 0:3 * C] = second
+    total[0:3 * C, 0:3 * C] = second
     total[0:3 * Q, 3 * C:] = first
     total[3 * Q:6 * Q, 3 * C:] = third
-    total[6 * Q:, 3 * C:] = jnp.zeros((3 * C - 6 * Q, C), F32)
+    total[6 * Q:, 3 * C:] = jnp.zeros((total.shape[0] - 6 * Q, C), F32)
+    total[3 * C:, 0:3 * C] = jnp.zeros((total.shape[0] - 3 * C, 3 * C), F32)
     count = grads.shape[0]
     rows = 3 * C // count
-    lines = R // count
+    line = lax.broadcasted_iota(jnp.int32, grads.shape[1:], 0)
+    extra = jnp.zeros(grads.shape[1:], F32)
+    for k in range(R // 2):
+        pair = jnp.concatenate([snapshot[2 * k:2 * k + 1], snapshot[2 * k + 1:2 * k + 2]], axis=1)
+        extra = jnp.where(line == rows + k, pair, extra)
     for k in range(count):
-        tail = jnp.zeros((grads.shape[1] - rows, LANES), F32)
-        row = lax.broadcasted_iota(jnp.int32, tail.shape, 0)
-        for line in range(lines):
-            one = snapshot[k * lines + line:k * lines + line + 1, :]
-            tail = jnp.where(row == line, twice(one), tail)
-        grads[k] = jnp.concatenate([total[k * rows:(k + 1) * rows, :], tail], axis=0).astype(BF)
-
-
-def reduce_kernel(received, out):
+        grads[k] = jnp.where(line < rows, total[k * rows:k * rows + grads.shape[1], :],
+                             extra).astype(BF)
+
+
+def reduce_pieces(rows, place, stride, received):
+    count = received.shape[0]
     total = received[0].astype(F32)
-    for k in range(1, received.shape[0]):
+    for k in range(1, count):
         total = total + received[k].astype(F32)
+    extra = received[place].astype(F32)
+    for k in range(1, count // stride):
+        extra = extra + received[place + k * stride].astype(F32)
+    line = lax.broadcasted_iota(jnp.int32, total.shape, 0)
+    return jnp.where(line < rows, total, extra)
+
+
+def near_kernel(rows, stride, place, received, out):
+    total = reduce_pieces(rows, place[0], stride, received).astype(BF)
+    for k in range(out.shape[0]):
+        out[k] = total
+
+
+def far_kernel(rows, stride, step, place, received, out, snapshot):
+    total = reduce_pieces(rows, place[0], stride, received)
+    for k in range(R // 2):
+        snapshot[2 * k:2 * k + 1, :] = step * total[rows + k:rows + k + 1, :W]
+        snapshot[2 * k + 1:2 * k + 2, :] = step * total[rows + k:rows + k + 1, W:]
     total = total.astype(BF)
     for k in range(out.shape[0]):
         out[k] = total
 
 
-def join_kernel(rows, received, mine, out):
-    total = received[0].astype(F32)
-    for k in range(1, received.shape[0]):
-        total = total + received[k].astype(F32)
-    row = lax.broadcasted_iota(jnp.int32, total.shape, 0)
-    total = jnp.where(row < rows, total, mine[0].astype(F32)).astype(BF)
-    for k in range(out.shape[0]):
-        out[k] = total
-
-
-def output_kernel(step, scale, received, snapshot, first, second, third, total):
+def output_kernel(scale, received, first, second, third, total):
     count = received.shape[0]
     rows = 3 * C // count
-    lines = R // count
     for k in range(count):
-        piece = received[k].astype(F32)
-        total[k * rows:(k + 1) * rows, :] = piece[:rows] * scale
-        snapshot[k * lines:(k + 1) * lines, :] = step * piece[rows:rows + lines, :W]
+        total[k * rows:(k + 1) * rows, :] = received[k].astype(F32)[:rows] * scale
     for i in (-1, 0, 1):
         for j in (-1, 0, 1):
             tap = 3 * (i + 1) + (j + 1)
@@ -316,7 +369,7 @@
             third[tap:tap + 1, :] = total[at:at + 1, 3 * C:] + total[at + 3:at + 4, 3 * C:]
 
 
-def call(kernel, outs, scratch, *operands, specs=None):
+def call(kernel, outs, scratch, *operands, specs=None, cost=None):
     grid = () if specs is None else (1,)
     if specs is None:
         specs = [pl.BlockSpec(memory_space=pltpu.VMEM)] * len(operands)
@@ -328,6 +381,7 @@
         out_specs=[pl.BlockSpec(memory_space=pltpu.VMEM)] * len(outs),
         scratch_shapes=[pltpu.VMEM(shape, dtype) for shape, dtype in scratch],
         compiler_params=pltpu.CompilerParams(vmem_limit_bytes=40 * 2**20),
+        cost_estimate=cost,
     )(*operands)
 
 
@@ -336,24 +390,8 @@
     return high, (field - high.astype(F32)).astype(BF)
 
 
-def by_row(field):
-    return jnp.transpose(field, (1, 0, 2)).reshape(R, LANES)
-
-
-def pad_slots(weight):
-    both = jnp.concatenate([weight, weight, jnp.zeros((3, Q - 6, C), BF)], axis=1)
-    return jnp.transpose(both.reshape(3 * Q, C))
-
-
 def exchange(value, axis):
     return lax.all_to_all(value, axis, 0, 0, tiled=True)
-
-
-def from_neighbours(value):
-    count = lax.axis_size(SPACE)
-    forward = [(i, i + 1) for i in range(count - 1)]
-    backward = [(i + 1, i) for i in range(count - 1)]
-    return forward, backward
 
 
 def per_device(equilibrium, measurement, coding_masks, upstream, saved_second, conv_first,
@@ -368,21 +406,17 @@
     place = lax.axis_index(SPACE)
     inside = jnp.stack([place > 0, place < tiles - 1]).astype(F32)
 
-    saved = jnp.transpose(saved_second, (2, 1, 0, 3)).reshape(R, C, LANES)
-    channels = [*split_parts(by_row(upstream)), *split_parts(by_row(equilibrium)),
-                by_row(coding_masks).astype(BF),
-                jnp.concatenate(split_parts(measurement), axis=1)]
-    channels += [jnp.zeros((R, LANES), BF)] * (SMALL - len(channels))
-    pack = jnp.concatenate([saved, jnp.stack(channels, axis=1)], axis=1)
+    pack, = call(
+        pack_kernel, [((R, C + SMALL, LANES), BF)], [((2, R * SMALL, W), F32)],
+        upstream, equilibrium, coding_masks, measurement, saved_second)
     low = lax.ppermute(pack[R - HALO:], SPACE, forward)
     high = lax.ppermute(pack[:HALO], SPACE, backward)
 
-    first_taps = conv_first.reshape(3, 3, C)
-    forward_w = pad_slots(first_taps)
-    third_w = pad_slots(conv_third.reshape(3, 3, C)[::-1])
-    second_w = jnp.transpose(
-        conv_second.reshape(3, 3, C, C)[::-1], (1, 3, 0, 2)).reshape(3 * C, 3 * C)
-    first_w = jnp.concatenate([conv_first, jnp.zeros((Q - 9, C), BF)], axis=0)
+    forward_w, third_w, second_w, first_w = call(
+        weights_kernel,
+        [((C, 3 * Q), BF), ((C, 3 * Q), BF), ((3 * C, 3 * C), BF), ((Q, C), BF)], [],
+        conv_first, conv_second, conv_third,
+        cost=pl.CostEstimate(flops=2 * 10**6, bytes_accessed=10**6, transcendentals=0))
 
     def rows_of(count, channels_at, width):
         return pl.BlockSpec((count, width, LANES), lambda _: (0, channels_at, 0))
@@ -401,18 +435,26 @@
 
     narrow = EXT - 6
     weights = (third_w, second_w, first_w)
-    wide_scratch = [((2, EXT * Q, W), F32), (((EXT - 2) * C, LANES), BF),
-                    (((EXT - 4) * C, LANES), BF), ((2, (EXT - 4) * Q, W), F32)]
+    copies = ((2, EXT * Q, W), F32)
+    d2 = (((EXT - 2) * C, LANES), BF)
+    d1 = (((EXT - 4) * C, LANES), BF)
+    taps = ((2, (EXT - 4) * Q, W), F32)
     slim_scratch = [((2, narrow * Q, W), F32), (((narrow - 2) * C, LANES), BF),
                     (((narrow - 4) * C, LANES), BF), ((2, (narrow - 4) * Q, W), F32)]
     wide_outs = [((frames, 16, W), F32), ((narrow, LANES), F32)]
-    part, moved, gate2, gate1, hidden, inputs = call(
+    gate2, back = call(
+        early_kernel,
+        [(((EXT - 2) * C, LANES), F32), (((EXT - 4) * C, LANES), F32)], [copies, d2],
+        inside, low, pack, high, up, third_w, second_w,
+        specs=[scalars, rows_of(HALO, 0, C), rows_of(R, 0, C), rows_of(HALO, 0, C)] + [whole] * 3,
+        cost=pl.CostEstimate(flops=10**9, bytes_accessed=8 * 10**6, transcendentals=3 * 10**5))
+    part, moved, gate1, hidden, inputs = call(
         functools.partial(first_kernel, step),
-        wide_outs + [(((EXT - 2) * C, LANES), F32), (((EXT - 4) * C, LANES), F32),
-                     ((R * C, LANES), BF), (((R + 2) * Q, LANES), BF)],
-        wide_scratch,
-        inside, low, pack, high, sums, up, masks, base, *weights, forward_w,
-        specs=[scalars, rows_of(HALO, 0, C), rows_of(R, 0, C), rows_of(HALO, 0, C)] + [whole] * 8)
+        wide_outs + [(((EXT - 4) * C, LANES), F32), ((R * C, LANES), BF),
+                     (((R + 2) * Q, LANES), BF)],
+        [copies, taps],
+        inside, sums, up, masks, base, back, first_w, forward_w,
+        specs=[scalars] + [whole] * 7)
     sums = exchange(part, TM)
 
     part, moved = call(
@@ -426,32 +468,41 @@
     field_low = lax.ppermute(field, SPACE, forward)
     field_high = lax.ppermute(field, SPACE, backward)
     part, moved = call(
-        third_kernel, wide_outs, wide_scratch + [ext],
+        third_kernel, wide_outs, [copies, d2, d1, taps, ext],
         inside, field_low, field, field_high, masks, gate2, gate1, *weights,
         specs=[scalars] + [whole] * 9)
     sums = exchange(part, TM)
 
-    piece = 3 * C // frames + max(8, R // frames)
+    near_sizes = [lax.axis_size(name) for name in NEAR]
+    far_sizes = [lax.axis_size(name) for name in FAR]
+    near_count = math.prod(near_sizes)
+    far_count = math.prod(far_sizes)
+    rows = 3 * C // near_count
+    piece = -(-(rows + R // 2) // 16) * 16
     adjoint, grads = call(
         functools.partial(last_kernel, step),
-        [((2, R, W), F32), ((frames, piece, LANES), BF)],
-        slim_scratch + [((3 * C, LANES), F32)],
+        [((2, R, W), F32), ((near_count, piece, LANES), BF)],
+        slim_scratch + [((3 * C + piece, LANES), F32)],
         sums, moved, up, masks, gate2, gate1, pack, hidden, inputs, *weights,
         specs=[whole] * 6 + [rows_of(R, 0, C)] + [whole] * 5)
 
-    mine = exchange(grads, TM)
-    count_y = lax.axis_size("y")
-    count_near = lax.axis_size(("zl", "x"))
-    mine, = call(reduce_kernel, [((count_y, piece, LANES), BF)], [], mine)
-    received = exchange(mine, "y")
-    received, = call(reduce_kernel, [((count_near, piece, LANES), BF)], [], received)
-    received = exchange(received, ("zl", "x"))
-    received, = call(functools.partial(join_kernel, 3 * C // frames),
-                     [((frames, piece, LANES), BF)], [], received, mine)
-    received = exchange(received, TM)
-    snapshot, grad_first, grad_second, grad_third = call(
-        functools.partial(output_kernel, step, scale),
-        [((R, W), F32), ((9, C), F32), ((9, C, C), F32), ((9, C), F32)],
+    received = exchange(grads, NEAR)
+    near_stride = near_count // near_sizes[0]
+    near_place = lax.axis_index(NEAR[1:])[None]
+    far_stride = far_count // far_sizes[0]
+    far_place = lax.axis_index(FAR[1:])[None]
+    received, = call(
+        functools.partial(near_kernel, rows, near_stride),
+        [((far_count, piece, LANES), BF)], [], near_place, received, specs=[scalars, whole])
+    received = exchange(received, FAR)
+    received, snapshot = call(
+        functools.partial(far_kernel, rows, far_stride, step),
+        [((near_count, piece, LANES), BF), ((R, W), F32)], [], far_place, received,
+        specs=[scalars, whole])
+    received = exchange(received, NEAR)
+    grad_first, grad_second, grad_third = call(
+        functools.partial(output_kernel, scale),
+        [((9, C), F32), ((9, C, C), F32), ((9, C), F32)],
         [((3 * C, LANES), F32)], received)
     return adjoint, snapshot, grad_first, grad_second, grad_third
 

time: 149 us -> 143 us (0.960)
  blocking collectives: 91.2 us -> 61.1 us
  starting transfers between devices: 25.6 us -> 43.4 us
  waiting for transfers between devices: 9.82 us -> 15.6 us
  Pallas kernels: 14.4 us -> 17.1 us
  other arithmetic: 1.66 us -> 0.08 us
    all_to_all x7 -> x5, blocking collectives: 91.2 us -> 61.1 us  [exchange(): return lax.all_to_all(value, axis, 0, 0, tiled=True)]
    all_to_all x1 -> x2, starting transfers between devices: 13.6 us -> 31.5 us  [exchange(): return lax.all_to_all(value, axis, 0, 0, tiled=True)]
    all_to_all x1 -> x2, waiting for transfers between devices: 6.09 us -> 12.1 us  [exchange(): return lax.all_to_all(value, axis, 0, 0, tiled=True)]
    unnamed x6 -> x16, local copies, waits for them, and re-layouts: 0.02 us -> 3.73 us
    pallas_call x10 -> x12, Pallas kernels: 14.4 us -> 17.1 us  [call(): pl.pallas_call(kernel, grid=grid, out_shape=[jax.ShapeDtypeStruct(shape,...]
    transpose x3 -> x0, local copies, waits for them, and re-layouts: 2.63 us -> none  [the longest x2 1.41 us: by_row(): return jnp.transpose(field, (1, 0, 2)).reshape(R, LANES)]
    convert_element_type x5 -> x0, other arithmetic: 1.5 us -> none  [the longest x2 0.78 us: split_parts(): return (high, (field - high.astype(F32)).astype(BF))]
  transfers between devices with their start and end apart: 5 -> 6, of which waited for: 4 -> 5; matrix products, arithmetic and copies ran while one was open for 1% -> 0% of each run, Pallas kernels for 0% -> 1%
where the time goes in v2:
time: 143 us; the launch traced here: 142 us
  blocking collectives  61.1 us (43%)
  starting transfers between devices  43.4 us (30%)
  Pallas kernels  17.1 us (12%)
  waiting for transfers between devices  15.6 us (11%)
  local copies, waits for them, and re-layouts  3.76 us (3%)
    all_to_all x5, blocking collectives, exchange(): return lax.all_to_all(value, axis, 0, 0, tiled=True)  61.1 us
    all_to_all x2, starting transfers between devices, exchange(): return lax.all_to_all(value, axis, 0, 0, tiled=True)  31.5 us
    pallas_call x12, Pallas kernels, call(): pl.pallas_call(kernel, grid=grid, out_shape=[jax.ShapeDtypeStruct(shape,...  17.1 us
    all_to_all x2, waiting for transfers between devices, exchange(): return lax.all_to_all(value, axis, 0, 0, tiled=True)  12.1 us
    ppermute x1, starting transfers between devices, per_device(): field_low = lax.ppermute(field, SPACE, forward)  4.73 us
    ppermute x1, starting transfers between devices, per_device(): low = lax.ppermute(pack[R - HALO:], SPACE, forward)  4.59 us
    unnamed x16, local copies, waits for them, and re-layouts  3.73 us
  transfers between devices with their start and end apart: 6, of which 5 were waited for; matrix products, arithmetic and copies ran while one was open for 0% of the time, Pallas kernels for 1%

profile of v2, /device:TPU:1, one launch (start us, length us, event | category | flops | bytes accessed | tf_op | source)
XLA Modules:
  0.0 141.7 jit_solution(14798472250785712977)
XLA Ops:
  0.6 0.0 copy-start
  0.6 0.9 copy-done
  1.6 0.0 copy-start.2
  1.6 0.7 copy-done.2
  2.3 0.0 copy-start.3
  2.3 0.7 copy-done.3
  3.0 0.0 copy-start.4
  3.0 0.7 copy-done.4
  3.7 0.0 copy-start.5
  3.7 0.7 copy-done.5
  4.4 0.0 copy-start.1
  4.4 0.0 copy-start.6
  4.4 0.0 copy-start.7
  4.4 0.2 shard_map.119.own.saved
  4.6 1.3 collective-permute-start.1
  5.9 4.6 %collective-permute-start = (bf16[6,80,256]{2,1,0:T(8,128)(2,1)S(1)}, bf16[6,80,256]{2,1,0:T(8,128)(2,1)S(1)}, u32[]{:S(2)}, u32[]{:S(2)}) collective-permute-start(bf16[6,80,256]{2,1,0:T(8,128)(2,1)S(1)} %get-tuple-element.58), channel_id=1, source_target_pairs={{0,1},{1,2},{2,3},{3,4},{4,5},{5,6},{6,7},{7,8},{8,9},{9,10},{10,1... | collective-permute-start | bytes 737288 | tf_op jit(solution)/shard_map/ppermute | solution.py:412
  10.5 0.0 copy-done.1
  10.5 0.0 copy-done.6
  10.5 0.0 copy-done.7
  10.5 0.3 shard_map.121
  10.9 1.3 collective-permute-done.1.high
  12.1 1.5 %collective-permute-done.low = bf16[6,80,256]{2,1,0:T(8,128)(2,1)S(1)} collective-permute-done((bf16[6,80,256]{2,1,0:T(8,128)(2,1)S(1)}, bf16[6,80,256]{2,1,0:T(8,128)(2,1)S(1)}, u32[]{:S(2)}, u32[]{:S(2)}) %collective-permute-start) | collective-permute-done | bytes 245792 | tf_op jit(solution)/shard_map/ppermute | solution.py:412
  13.6 0.7 shard_map.120
  14.3 13.6 %all-to-all-start = ((f32[8,24,128]{2,1,0:T(8,128)}), f32[8,24,128]{2,1,0:T(8,128)S(1)}, u32[]{:S(2)}, u32[]{:S(2)}) async-start(f32[8,24,128]{2,1,0:T(8,128)} %get-tuple-element.31), calls=%async_computation | async-start | bytes 196608 | tf_op jit(solution)/shard_map/all_to_all | solution.py:394
  27.9 0.1 add_convert_fusion.inside
  27.9 1.8 %shard_map.122 = (f32[1152,256]{1,0:T(8,128)S(1)}, f32[1024,256]{1,0:T(8,128)S(1)}) custom-call(f32[2]{0:T(128)S(1)} %add_convert_fusion.inside, bf16[6,80,256]{2,1,0:T(8,128)(2,1)S(1)} %collective-permute-done.low, bf16[8,80,256]{2,1,0:T(8,128)(2,1)S(1)} %shard_map.119.own.saved, bf16[6,80,256]{2,1,0:T(8,128)(2,1)S(1)} %collective-permute-done.1.high, ...), custom_call_target="tpu_custom_call" | custom-call | flops 1000000000 | bytes 8000000 | tf_op jit(solution)/shard_map/pallas_call | solution.py:376
  29.8 5.8 %all-to-all-done.sums = f32[8,24,128]{2,1,0:T(8,128)S(1)} async-done(((f32[8,24,128]{2,1,0:T(8,128)}), f32[8,24,128]{2,1,0:T(8,128)S(1)}, u32[]{:S(2)}, u32[]{:S(2)}) %all-to-all-start) | async-done | bytes 98336 | tf_op jit(solution)/shard_map/all_to_all | solution.py:394
  35.5 3.4 %shard_map.123 = (f32[8,16,128]{2,1,0:T(8,128)S(1)}, f32[14,256]{1,0:T(8,128)S(1)}, f32[1024,256]{1,0:T(8,128)S(1)}, bf16[512,256]{1,0:T(8,128)(2,1)S(1)}, bf16[160,256]{1,0:T(8,128)(2,1)S(1)}) custom-call(f32[2]{0:T(128)S(1)} %add_convert_fusion.inside, f32[8,24,128]{2,1,0:T(8,128)S(1)} %all-to-all-done.sums, f32[20,256]{1,0:T(8,128)S(1)} %get-tuple-element.32.up, ...), custom_call_target="tpu_custom_call" | custom-call | tf_op jit(solution)/shard_map/pallas_call | solution.py:376
  38.9 10.9 %all_to_all.35.sums = f32[8,16,128]{2,1,0:T(8,128)S(1)} all-to-all(f32[8,16,128]{2,1,0:T(8,128)S(1)} %get-tuple-element.40), channel_id=1, replica_groups=mesh['zh'=4,'core'=2,'zl'=2,'y'=8,'x'=4] {'zh','core'}, dimensions={0} | all-to-all | bytes 131072 | tf_op jit(solution)/shard_map/all_to_all | solution.py:394
  49.8 2.3 %shard_map.124 = (f32[8,8,128]{2,1,0:T(8,128)S(1)}, f32[8,256]{1,0:T(8,128)S(1)}) custom-call(f32[8,16,128]{2,1,0:T(8,128)S(1)} %all_to_all.35.sums, f32[14,256]{1,0:T(8,128)S(1)} %get-tuple-element.41.moved, f32[20,256]{1,0:T(8,128)S(1)} %get-tuple-element.32.up, f32[20,256]{1,0:T(8,128)S(1)} %get-tuple-element.33.masks, ...), custom_call_target="tpu_custom_call" | custom-call | tf_op jit(solution)/shard_map/pallas_call | solution.py:376
  52.0 10.3 %all_to_all.36.sums = f32[8,8,128]{2,1,0:T(8,128)S(1)} all-to-all(f32[8,8,128]{2,1,0:T(8,128)S(1)} %get-tuple-element.44), channel_id=1, replica_groups=mesh['zh'=4,'core'=2,'zl'=2,'y'=8,'x'=4] {'zh','core'}, dimensions={0} | all-to-all | bytes 65536 | tf_op jit(solution)/shard_map/all_to_all | solution.py:394
  62.4 1.3 collective-permute-start.3
  63.7 4.7 %collective-permute-start.2 = (f32[8,256]{1,0:T(8,128)S(1)}, f32[8,256]{1,0:T(8,128)S(1)}, u32[]{:S(2)}, u32[]{:S(2)}) collective-permute-start(f32[8,256]{1,0:T(8,128)S(1)} %shard_map.125.own), channel_id=1, source_target_pairs={{0,1},{1,2},{2,3},{3,4},{4,5},{5,6},{6,7},{7,8},{8,9},{9,10},{10,1... | collective-permute-start | bytes 24584 | tf_op jit(solution)/shard_map/ppermute | solution.py:468
  68.4 0.0 collective-permute-done.3.high
  68.5 0.8 collective-permute-done.2.low
  69.2 3.7 %shard_map.126 = (f32[8,16,128]{2,1,0:T(8,128)S(1)}, f32[14,256]{1,0:T(8,128)S(1)}) custom-call(f32[2]{0:T(128)S(1)} %add_convert_fusion.inside, f32[8,256]{1,0:T(8,128)S(1)} %collective-permute-done.2.low, f32[8,256]{1,0:T(8,128)S(1)} %shard_map.125.own, f32[8,256]{1,0:T(8,128)S(1)} %collective-permute-done.3.high, f32[20,256]{1,0:T(8,128)S(1)} %get-tuple-element.33.masks, ...), custom_call_target="tpu_custom_call" | custom-call | tf_op jit(solution)/shard_map/pallas_call | solution.py:376
  73.0 11.4 %all_to_all.37.sums = f32[8,16,128]{2,1,0:T(8,128)S(1)} all-to-all(f32[8,16,128]{2,1,0:T(8,128)S(1)} %get-tuple-element.46), channel_id=1, replica_groups=mesh['zh'=4,'core'=2,'zl'=2,'y'=8,'x'=4] {'zh','core'}, dimensions={0} | all-to-all | bytes 131072 | tf_op jit(solution)/shard_map/all_to_all | solution.py:394
  84.4 3.2 %shard_map.127 = (f32[2,8,128]{2,1,0:T(8,128)}, bf16[16,16,256]{2,1,0:T(8,128)(2,1)}) custom-call(f32[8,16,128]{2,1,0:T(8,128)S(1)} %all_to_all.37.sums, f32[14,256]{1,0:T(8,128)S(1)} %get-tuple-element.47.moved, f32[20,256]{1,0:T(8,128)S(1)} %get-tuple-element.32.up, f32[20,256]{1,0:T(8,128)S(1)} %get-tuple-element.33.masks, ...), custom_call_target="tpu_custom_call" | custom-call | tf_op jit(solution)/shard_map/pallas_call | solution.py:376
  87.6 17.9 %all-to-all-start.4 = ((bf16[16,16,256]{2,1,0:T(8,128)(2,1)}), bf16[16,16,256]{2,1,0:T(8,128)(2,1)S(1)}, u32[]{:S(2)}, u32[]{:S(2)}) async-start(bf16[16,16,256]{2,1,0:T(8,128)(2,1)} %get-tuple-element.51), calls=%async_computation.4 | async-start | bytes 262144 | tf_op jit(solution)/shard_map/all_to_all | solution.py:394
  105.5 6.3 %all-to-all-done.4.received = bf16[16,16,256]{2,1,0:T(8,128)(2,1)S(1)} async-done(((bf16[16,16,256]{2,1,0:T(8,128)(2,1)}), bf16[16,16,256]{2,1,0:T(8,128)(2,1)S(1)}, u32[]{:S(2)}, u32[]{:S(2)}) %all-to-all-start.4) | async-done | bytes 131104 | tf_op jit(solution)/shard_map/all_to_all | solution.py:394
  111.9 16.5 %all_to_all.38.received = bf16[32,16,256]{2,1,0:T(8,128)(2,1)S(1)} all-to-all(bf16[32,16,256]{2,1,0:T(8,128)(2,1)S(1)} %shard_map.128), channel_id=1, replica_groups=mesh['zh'=4,'core'=2,'zl'=2,'y'=8,'x'=4] {'zh','y'}, dimensions={0} | all-to-all | bytes 524288 | tf_op jit(solution)/shard_map/all_to_all | solution.py:394
  128.3 0.6 shard_map.129
  129.0 11.9 %all_to_all.39.received = bf16[16,16,256]{2,1,0:T(8,128)(2,1)S(1)} all-to-all(bf16[16,16,256]{2,1,0:T(8,128)(2,1)S(1)} %get-tuple-element.53), channel_id=1, replica_groups=mesh['zh'=4,'core'=2,'zl'=2,'y'=8,'x'=4] {'core','zl','x'}, dimensions={0} | all-to-all | bytes 262144 | tf_op jit(solution)/shard_map/all_to_all | solution.py:394
  140.9 0.8 shard_map.130
  (3 shorter events, 0.1 us)
Async XLA Ops:
  0.6 1.0 copy-start
  1.6 0.7 copy-start.2
  2.3 0.7 copy-start.3
  3.0 0.7 copy-start.4
  3.7 0.7 copy-start.5
  4.4 6.1 %copy-start.1 = (bf16[9,64,64]{2,1,0:T(8,128)(2,1)S(1)}, bf16[9,64,64]{2,1,0:T(8,128)(2,1)}, u32[]{:S(2)}) copy-start(bf16[9,64,64]{2,1,0:T(8,128)(2,1)} %second.1) | copy-start | bytes 221188
  4.4 6.2 %copy-start.6 = (bf16[9,64]{1,0:T(8,128)(2,1)S(1)}, bf16[9,64]{1,0:T(8,128)(2,1)}, u32[]{:S(2)}) copy-start(bf16[9,64]{1,0:T(8,128)(2,1)} %first.1) | copy-start | bytes 3460
  4.4 6.2 %copy-start.7 = (bf16[9,64]{1,0:T(8,128)(2,1)S(1)}, bf16[9,64]{1,0:T(8,128)(2,1)}, u32[]{:S(2)}) copy-start(bf16[9,64]{1,0:T(8,128)(2,1)} %third.1) | copy-start | bytes 3460
  4.6 7.5 %collective-permute-start.1 = (bf16[6,80,256]{2,1,0:T(8,128)(2,1)S(1)}, bf16[6,80,256]{2,1,0:T(8,128)(2,1)S(1)}, u32[]{:S(2)}, u32[]{:S(2)}) collective-permute-start(bf16[6,80,256]{2,1,0:T(8,128)(2,1)S(1)} %get-tuple-element.57), channel_id=1, source_target_pairs={{1,0},{2,1},{3,2},{4,3},{5,4},{6,5},{7,6},{8,7},{9,8},{10,9},{11,1... | collective-permute-start | bytes 737288 | tf_op jit(solution)/shard_map/ppermute | solution.py:413
  5.9 7.7 %collective-permute-start = (bf16[6,80,256]{2,1,0:T(8,128)(2,1)S(1)}, bf16[6,80,256]{2,1,0:T(8,128)(2,1)S(1)}, u32[]{:S(2)}, u32[]{:S(2)}) collective-permute-start(bf16[6,80,256]{2,1,0:T(8,128)(2,1)S(1)} %get-tuple-element.58), channel_id=1, source_target_pairs={{0,1},{1,2},{2,3},{3,4},{4,5},{5,6},{6,7},{7,8},{8,9},{9,10},{10,1... | collective-permute-start | bytes 737288 | tf_op jit(solution)/shard_map/ppermute | solution.py:412
  14.3 21.2 %all-to-all-start = ((f32[8,24,128]{2,1,0:T(8,128)}), f32[8,24,128]{2,1,0:T(8,128)S(1)}, u32[]{:S(2)}, u32[]{:S(2)}) async-start(f32[8,24,128]{2,1,0:T(8,128)} %get-tuple-element.31), calls=%async_computation | async-start | bytes 196608 | tf_op jit(solution)/shard_map/all_to_all | solution.py:394
  62.4 6.0 %collective-permute-start.3 = (f32[8,256]{1,0:T(8,128)S(1)}, f32[8,256]{1,0:T(8,128)S(1)}, u32[]{:S(2)}, u32[]{:S(2)}) collective-permute-start(f32[8,256]{1,0:T(8,128)S(1)} %shard_map.125.own), channel_id=1, source_target_pairs={{1,0},{2,1},{3,2},{4,3},{5,4},{6,5},{7,6},{8,7},{9,8},{10,9},{11,1... | collective-permute-start | bytes 24584 | tf_op jit(solution)/shard_map/ppermute | solution.py:469
  63.7 5.5 %collective-permute-start.2 = (f32[8,256]{1,0:T(8,128)S(1)}, f32[8,256]{1,0:T(8,128)S(1)}, u32[]{:S(2)}, u32[]{:S(2)}) collective-permute-start(f32[8,256]{1,0:T(8,128)S(1)} %shard_map.125.own), channel_id=1, source_target_pairs={{0,1},{1,2},{2,3},{3,4},{4,5},{5,6},{6,7},{7,8},{8,9},{9,10},{10,1... | collective-permute-start | bytes 24584 | tf_op jit(solution)/shard_map/ppermute | solution.py:468
  87.6 24.3 %all-to-all-start.4 = ((bf16[16,16,256]{2,1,0:T(8,128)(2,1)}), bf16[16,16,256]{2,1,0:T(8,128)(2,1)S(1)}, u32[]{:S(2)}, u32[]{:S(2)}) async-start(bf16[16,16,256]{2,1,0:T(8,128)(2,1)} %get-tuple-element.51), calls=%async_computation.4 | async-start | bytes 262144 | tf_op jit(solution)/shard_map/all_to_all | solution.py:394

commit v3 on v2

--- a/solution.py
+++ b/solution.py
@@ -101,12 +101,13 @@
         at = first + k
         row = (gate1[at * C:(at + 1) * C, :] * total).astype(BF)
         d1[k * C:(k + 1) * C, :] = row
-        put_rows(taps, k * Q, dot(first_w, row))
-    return map_end(first, field, taps)
-
-
-def map_end(first, field, taps):
+    return map_end(first, field, first_w, d1, taps)
+
+
+def map_end(first, field, first_w, d1, taps):
     count = EXT - 2 * first - 6
+    for k in range(count + 2):
+        put_rows(taps, k * Q, dot(first_w, d1[k * C:(k + 1) * C, :]))
     result = field[3:3 + count]
     for j in (-1, 0, 1):
         column = None
@@ -134,7 +135,7 @@
     return total
 
 
-def pack_kernel(upstream, equilibrium, masks, measurement, saved, out, small):
+def pack_kernel(upstream, equilibrium, masks, measurement, saved, out, top, bottom, small):
     small[...] = jnp.zeros_like(small)
     for frame in range(2):
         fields = (*split_parts(upstream[frame]), *split_parts(equilibrium[frame]),
@@ -144,6 +145,8 @@
         lanes = slice(frame * W, (frame + 1) * W)
         out[:, C:, lanes] = small[frame].astype(BF).reshape(R, SMALL, W)
         out[:, :C, lanes] = jnp.swapaxes(saved[frame].astype(F32), 0, 1).astype(BF)
+    top[...] = out[:HALO]
+    bottom[...] = out[R - HALO:]
 
 
 def weights_kernel(first, second, third, forward_w, third_w, second_w, first_w):
@@ -209,7 +212,7 @@
 
 
 def first_kernel(step, inside, sums, up, masks, base, back, first_w, forward_w,
-                 part, moved, gate1, hidden, inputs, copies, taps):
+                 part, moved, gate1, hidden, inputs, copies, d1, taps):
     frame_sum = gathered_sum(sums)[:EXT]
     denoiser_input = base[...] - step * masks[...] * twice(frame_sum)
     copies[...] = jnp.zeros_like(copies)
@@ -224,9 +227,8 @@
         if HALO <= at < HALO + R:
             own_at = at - HALO
             hidden[own_at * C:(own_at + 1) * C, :] = (value * logistic).astype(BF)
-        row = (slope * back[k * C:(k + 1) * C, :]).astype(BF)
-        put_rows(taps, k * Q, dot(first_w[...], row))
-    field = map_end(0, up[...], taps)
+        d1[k * C:(k + 1) * C, :] = (slope * back[k * C:(k + 1) * C, :]).astype(BF)
+    field = map_end(0, up[...], first_w[...], d1, taps)
     finish_wide(field, inside[0], inside[1], masks, part, moved)
 
 
@@ -369,7 +371,7 @@
             third[tap:tap + 1, :] = total[at:at + 1, 3 * C:] + total[at + 3:at + 4, 3 * C:]
 
 
-def call(kernel, outs, scratch, *operands, specs=None, cost=None):
+def call(kernel, outs, scratch, *operands, specs=None, cost=None, limit=40):
     grid = () if specs is None else (1,)
     if specs is None:
         specs = [pl.BlockSpec(memory_space=pltpu.VMEM)] * len(operands)
@@ -380,9 +382,13 @@
         in_specs=specs,
         out_specs=[pl.BlockSpec(memory_space=pltpu.VMEM)] * len(outs),
         scratch_shapes=[pltpu.VMEM(shape, dtype) for shape, dtype in scratch],
-        compiler_params=pltpu.CompilerParams(vmem_limit_bytes=40 * 2**20),
+        compiler_params=pltpu.CompilerParams(vmem_limit_bytes=limit * 2**20),
         cost_estimate=cost,
     )(*operands)
+
+
+def full_block(*shape):
+    return pl.BlockSpec(shape, lambda _: (0,) * len(shape))
 
 
 def split_parts(field):
@@ -406,16 +412,19 @@
     place = lax.axis_index(SPACE)
     inside = jnp.stack([place > 0, place < tiles - 1]).astype(F32)
 
-    pack, = call(
-        pack_kernel, [((R, C + SMALL, LANES), BF)], [((2, R * SMALL, W), F32)],
-        upstream, equilibrium, coding_masks, measurement, saved_second)
-    low = lax.ppermute(pack[R - HALO:], SPACE, forward)
-    high = lax.ppermute(pack[:HALO], SPACE, backward)
+    edge = ((HALO, C + SMALL, LANES), BF)
+    pack, top, bottom = call(
+        pack_kernel, [((R, C + SMALL, LANES), BF), edge, edge], [((2, R * SMALL, W), F32)],
+        upstream, equilibrium, coding_masks, measurement, saved_second,
+        specs=[full_block(2, R, W)] * 3 + [full_block(R, W), full_block(2, C, R, W)], limit=60)
+    low = lax.ppermute(bottom, SPACE, forward)
+    high = lax.ppermute(top, SPACE, backward)
 
     forward_w, third_w, second_w, first_w = call(
         weights_kernel,
         [((C, 3 * Q), BF), ((C, 3 * Q), BF), ((3 * C, 3 * C), BF), ((Q, C), BF)], [],
         conv_first, conv_second, conv_third,
+        specs=[full_block(9, C), full_block(9, C, C), full_block(9, C)],
         cost=pl.CostEstimate(flops=2 * 10**6, bytes_accessed=10**6, transcendentals=0))
 
     def rows_of(count, channels_at, width):
@@ -452,7 +461,7 @@
         functools.partial(first_kernel, step),
         wide_outs + [(((EXT - 4) * C, LANES), F32), ((R * C, LANES), BF),
                      (((R + 2) * Q, LANES), BF)],
-        [copies, taps],
+        [copies, d1, taps],
         inside, sums, up, masks, base, back, first_w, forward_w,
         specs=[scalars] + [whole] * 7)
     sums = exchange(part, TM)

time: 143 us -> 138 us (0.965)
  Pallas kernels: 17.1 us -> 12.7 us
  blocking collectives: 61.1 us -> 63.2 us
  starting transfers between devices: 43.4 us -> 41.5 us
    pallas_call x12, Pallas kernels: 17.1 us -> 12.7 us  [call(): pl.pallas_call(kernel, grid=grid, out_shape=[jax.ShapeDtypeStruct(shape,...]
    all_to_all x5, blocking collectives: 61.1 us -> 63.2 us  [exchange(): return lax.all_to_all(value, axis, 0, 0, tiled=True)]
    unnamed x16 -> x12, local copies, waits for them, and re-layouts: 3.73 us -> 4.23 us
  transfers between devices with their start and end apart: 6 -> 6, of which waited for: 5 -> 4; matrix products, arithmetic and copies ran while one was open for 0% -> 0% of each run, Pallas kernels for 1% -> 2%
where the time goes in v3:
time: 138 us
  blocking collectives  63.2 us (46%)
  starting transfers between devices  41.5 us (30%)
  waiting for transfers between devices  15.1 us (11%)
  Pallas kernels  12.7 us (9%)
  local copies, waits for them, and re-layouts  4.23 us (3%)
    all_to_all x5, blocking collectives, exchange(): return lax.all_to_all(value, axis, 0, 0, tiled=True)  63.2 us
    all_to_all x2, starting transfers between devices, exchange(): return lax.all_to_all(value, axis, 0, 0, tiled=True)  30.5 us
    pallas_call x12, Pallas kernels, call(): pl.pallas_call(kernel, grid=grid, out_shape=[jax.ShapeDtypeStruct(shape,...  12.7 us
    all_to_all x2, waiting for transfers between devices, exchange(): return lax.all_to_all(value, axis, 0, 0, tiled=True)  11.1 us
    ppermute x1, starting transfers between devices, per_device(): field_low = lax.ppermute(field, SPACE, forward)  4.4 us
    unnamed x12, local copies, waits for them, and re-layouts  4.23 us
    ppermute x1, starting transfers between devices, per_device(): low = lax.ppermute(bottom, SPACE, forward)  3.95 us
    ppermute x1, waiting for transfers between devices, per_device(): high = lax.ppermute(top, SPACE, backward)  3.21 us
  transfers between devices with their start and end apart: 6, of which 4 were waited for; matrix products, arithmetic and copies ran while one was open for 0% of the time, Pallas kernels for 2%

profile of v3, /device:TPU:1, one launch (start us, length us, event | category | flops | bytes accessed | tf_op | source)
XLA Modules:
  0.0 137.6 jit_solution(12668562333931821309)
XLA Ops:
  0.6 2.1 %shard_map.119 = (bf16[8,80,256]{2,1,0:T(8,128)(2,1)}, bf16[6,80,256]{2,1,0:T(8,128)(2,1)}, bf16[6,80,256]{2,1,0:T(8,128)(2,1)}) custom-call(f32[2,8,128]{2,1,0:T(8,128)} %upstream.1, f32[2,8,128]{2,1,0:T(8,128)} %equilibrium.1, s32[2,8,128]{2,1,0:T(8,128)} %masks.1, f32[8,128]{1,0:T(8,128)} %measurement.1, bf16[2,64,8,128]{3,2,1,0:T(8,128)(2,1)} %saved.1), custom_call_target="tpu_custom_call" | custom-call | tf_op jit(solution)/shard_map/pallas_call | solution.py:378
  2.7 3.9 %collective-permute-start = (bf16[6,80,256]{2,1,0:T(8,128)(2,1)}, bf16[6,80,256]{2,1,0:T(8,128)(2,1)S(1)}, u32[]{:S(2)}, u32[]{:S(2)}) collective-permute-start(bf16[6,80,256]{2,1,0:T(8,128)(2,1)} %get-tuple-element.34), channel_id=1, source_target_pairs={{0,1},{1,2},{2,3},{3,4},{4,5},{5,6},{6,7},{7,8},{8,9},{9,10},{10,1... | collective-permute-start | bytes 737288 | tf_op jit(solution)/shard_map/ppermute | solution.py:420
  6.7 1.3 collective-permute-start.1
  8.0 0.0 copy-start.3
  8.0 0.9 copy-done.3
  8.9 0.0 copy-start.4
  8.9 0.7 copy-done.4
  9.6 0.0 copy-start.5
  9.6 0.7 copy-done.5
  10.3 0.3 shard_map.121
  10.6 0.0 collective-permute-done.low
  10.6 3.2 %collective-permute-done.1.high = bf16[6,80,256]{2,1,0:T(8,128)(2,1)S(1)} collective-permute-done((bf16[6,80,256]{2,1,0:T(8,128)(2,1)}, bf16[6,80,256]{2,1,0:T(8,128)(2,1)S(1)}, u32[]{:S(2)}, u32[]{:S(2)}) %collective-permute-start.1) | collective-permute-done | bytes 245792 | tf_op jit(solution)/shard_map/ppermute | solution.py:421
  13.8 0.0 copy-start
  13.8 1.0 copy-done
  14.8 0.7 shard_map.120
  15.5 13.6 %all-to-all-start = ((f32[8,24,128]{2,1,0:T(8,128)}), f32[8,24,128]{2,1,0:T(8,128)S(1)}, u32[]{:S(2)}, u32[]{:S(2)}) async-start(f32[8,24,128]{2,1,0:T(8,128)} %get-tuple-element.37), calls=%async_computation | async-start | bytes 196608 | tf_op jit(solution)/shard_map/all_to_all | solution.py:400
  29.1 0.1 add_convert_fusion.inside
  29.2 0.0 copy-start.1
  29.2 1.0 copy-done.1
  30.2 1.8 %shard_map.122 = (f32[1152,256]{1,0:T(8,128)S(1)}, f32[1024,256]{1,0:T(8,128)S(1)}) custom-call(f32[2]{0:T(128)S(1)} %add_convert_fusion.inside, bf16[6,80,256]{2,1,0:T(8,128)(2,1)S(1)} %collective-permute-done.low, bf16[8,80,256]{2,1,0:T(8,128)(2,1)S(1)} %copy-done.1, bf16[6,80,256]{2,1,0:T(8,128)(2,1)S(1)} %collective-permute-done.1.high, ...), custom_call_target="tpu_custom_call" | custom-call | flops 1000000000 | bytes 8000000 | tf_op jit(solution)/shard_map/pallas_call | solution.py:378
  32.0 4.8 %all-to-all-done.sums = f32[8,24,128]{2,1,0:T(8,128)S(1)} async-done(((f32[8,24,128]{2,1,0:T(8,128)}), f32[8,24,128]{2,1,0:T(8,128)S(1)}, u32[]{:S(2)}, u32[]{:S(2)}) %all-to-all-start) | async-done | bytes 98336 | tf_op jit(solution)/shard_map/all_to_all | solution.py:400
  36.8 1.4 shard_map.123
  38.1 10.9 %all_to_all.35.sums = f32[8,16,128]{2,1,0:T(8,128)S(1)} all-to-all(f32[8,16,128]{2,1,0:T(8,128)S(1)} %get-tuple-element.46), channel_id=1, replica_groups=mesh['zh'=4,'core'=2,'zl'=2,'y'=8,'x'=4] {'zh','core'}, dimensions={0} | all-to-all | bytes 131072 | tf_op jit(solution)/shard_map/all_to_all | solution.py:400
  49.0 1.0 shard_map.124
  50.1 10.4 %all_to_all.36.sums = f32[8,8,128]{2,1,0:T(8,128)S(1)} all-to-all(f32[8,8,128]{2,1,0:T(8,128)S(1)} %get-tuple-element.50), channel_id=1, replica_groups=mesh['zh'=4,'core'=2,'zl'=2,'y'=8,'x'=4] {'zh','core'}, dimensions={0} | all-to-all | bytes 65536 | tf_op jit(solution)/shard_map/all_to_all | solution.py:400
  60.4 0.0 copy-start.2
  60.4 1.4 %collective-permute-start.3 = (f32[8,256]{1,0:T(8,128)S(1)}, f32[8,256]{1,0:T(8,128)S(1)}, u32[]{:S(2)}, u32[]{:S(2)}) collective-permute-start(f32[8,256]{1,0:T(8,128)S(1)} %shard_map.125.own), channel_id=1, source_target_pairs={{1,0},{2,1},{3,2},{4,3},{5,4},{6,5},{7,6},{8,7},{9,8},{10,9},{11,1... | collective-permute-start | bytes 24584 | tf_op jit(solution)/shard_map/ppermute | solution.py:478
  61.9 4.4 %collective-permute-start.2 = (f32[8,256]{1,0:T(8,128)S(1)}, f32[8,256]{1,0:T(8,128)S(1)}, u32[]{:S(2)}, u32[]{:S(2)}) collective-permute-start(f32[8,256]{1,0:T(8,128)S(1)} %shard_map.125.own), channel_id=1, source_target_pairs={{0,1},{1,2},{2,3},{3,4},{4,5},{5,6},{6,7},{7,8},{8,9},{9,10},{10,1... | collective-permute-start | bytes 24584 | tf_op jit(solution)/shard_map/ppermute | solution.py:477
  66.3 0.0 collective-permute-done.3.high
  66.3 0.8 collective-permute-done.2.low
  67.1 1.8 %shard_map.126 = (f32[8,16,128]{2,1,0:T(8,128)S(1)}, f32[14,256]{1,0:T(8,128)S(1)}) custom-call(f32[2]{0:T(128)S(1)} %add_convert_fusion.inside, f32[8,256]{1,0:T(8,128)S(1)} %collective-permute-done.2.low, f32[8,256]{1,0:T(8,128)S(1)} %shard_map.125.own, f32[8,256]{1,0:T(8,128)S(1)} %collective-permute-done.3.high, f32[20,256]{1,0:T(8,128)S(1)} %get-tuple-element.39.masks, ...), custom_call_target="tpu_custom_call" | custom-call | tf_op jit(solution)/shard_map/pallas_call | solution.py:378
  68.9 11.4 %all_to_all.37.sums = f32[8,16,128]{2,1,0:T(8,128)S(1)} all-to-all(f32[8,16,128]{2,1,0:T(8,128)S(1)} %get-tuple-element.52), channel_id=1, replica_groups=mesh['zh'=4,'core'=2,'zl'=2,'y'=8,'x'=4] {'zh','core'}, dimensions={0} | all-to-all | bytes 131072 | tf_op jit(solution)/shard_map/all_to_all | solution.py:400
  80.3 0.0 copy-done.2
  80.3 2.1 %shard_map.127 = (f32[2,8,128]{2,1,0:T(8,128)}, bf16[16,16,256]{2,1,0:T(8,128)(2,1)}) custom-call(f32[8,16,128]{2,1,0:T(8,128)S(1)} %all_to_all.37.sums, f32[14,256]{1,0:T(8,128)S(1)} %get-tuple-element.53.moved, f32[20,256]{1,0:T(8,128)S(1)} %get-tuple-element.38.up, f32[20,256]{1,0:T(8,128)S(1)} %get-tuple-element.39.masks, ...), custom_call_target="tpu_custom_call" | custom-call | tf_op jit(solution)/shard_map/pallas_call | solution.py:378
  82.4 16.9 %all-to-all-start.4 = ((bf16[16,16,256]{2,1,0:T(8,128)(2,1)}), bf16[16,16,256]{2,1,0:T(8,128)(2,1)S(1)}, u32[]{:S(2)}, u32[]{:S(2)}) async-start(bf16[16,16,256]{2,1,0:T(8,128)(2,1)} %get-tuple-element.57), calls=%async_computation.4 | async-start | bytes 262144 | tf_op jit(solution)/shard_map/all_to_all | solution.py:400
  99.3 6.3 %all-to-all-done.4.received = bf16[16,16,256]{2,1,0:T(8,128)(2,1)S(1)} async-done(((bf16[16,16,256]{2,1,0:T(8,128)(2,1)}), bf16[16,16,256]{2,1,0:T(8,128)(2,1)S(1)}, u32[]{:S(2)}, u32[]{:S(2)}) %all-to-all-start.4) | async-done | bytes 131104 | tf_op jit(solution)/shard_map/all_to_all | solution.py:400
  105.6 18.6 %all_to_all.38.received = bf16[32,16,256]{2,1,0:T(8,128)(2,1)S(1)} all-to-all(bf16[32,16,256]{2,1,0:T(8,128)(2,1)S(1)} %shard_map.128), channel_id=1, replica_groups=mesh['zh'=4,'core'=2,'zl'=2,'y'=8,'x'=4] {'zh','y'}, dimensions={0} | all-to-all | bytes 524288 | tf_op jit(solution)/shard_map/all_to_all | solution.py:400
  124.2 0.6 shard_map.129
  124.9 11.9 %all_to_all.39.received = bf16[16,16,256]{2,1,0:T(8,128)(2,1)S(1)} all-to-all(bf16[16,16,256]{2,1,0:T(8,128)(2,1)S(1)} %get-tuple-element.59), channel_id=1, replica_groups=mesh['zh'=4,'core'=2,'zl'=2,'y'=8,'x'=4] {'core','zl','x'}, dimensions={0} | all-to-all | bytes 262144 | tf_op jit(solution)/shard_map/all_to_all | solution.py:400
  136.8 0.8 shard_map.130
  (2 shorter events, 0.1 us)
Async XLA Ops:
  2.7 7.9 %collective-permute-start = (bf16[6,80,256]{2,1,0:T(8,128)(2,1)}, bf16[6,80,256]{2,1,0:T(8,128)(2,1)S(1)}, u32[]{:S(2)}, u32[]{:S(2)}) collective-permute-start(bf16[6,80,256]{2,1,0:T(8,128)(2,1)} %get-tuple-element.34), channel_id=1, source_target_pairs={{0,1},{1,2},{2,3},{3,4},{4,5},{5,6},{6,7},{7,8},{8,9},{9,10},{10,1... | collective-permute-start | bytes 737288 | tf_op jit(solution)/shard_map/ppermute | solution.py:420
  6.7 7.2 %collective-permute-start.1 = (bf16[6,80,256]{2,1,0:T(8,128)(2,1)}, bf16[6,80,256]{2,1,0:T(8,128)(2,1)S(1)}, u32[]{:S(2)}, u32[]{:S(2)}) collective-permute-start(bf16[6,80,256]{2,1,0:T(8,128)(2,1)} %get-tuple-element.36), channel_id=1, source_target_pairs={{1,0},{2,1},{3,2},{4,3},{5,4},{6,5},{7,6},{8,7},{9,8},{10,9},{11,1... | collective-permute-start | bytes 737288 | tf_op jit(solution)/shard_map/ppermute | solution.py:421
  8.0 0.9 copy-start.3
  8.9 0.7 copy-start.4
  9.6 0.7 copy-start.5
  13.8 1.0 copy-start
  15.5 21.3 %all-to-all-start = ((f32[8,24,128]{2,1,0:T(8,128)}), f32[8,24,128]{2,1,0:T(8,128)S(1)}, u32[]{:S(2)}, u32[]{:S(2)}) async-start(f32[8,24,128]{2,1,0:T(8,128)} %get-tuple-element.37), calls=%async_computation | async-start | bytes 196608 | tf_op jit(solution)/shard_map/all_to_all | solution.py:400
  29.2 1.0 copy-start.1
  60.4 19.9 %copy-start.2 = (bf16[8,80,256]{2,1,0:T(8,128)(2,1)S(1)}, bf16[8,80,256]{2,1,0:T(8,128)(2,1)}, u32[]{:S(2)}) copy-start(bf16[8,80,256]{2,1,0:T(8,128)(2,1)} %get-tuple-element.35.own.saved) | copy-start | bytes 983044
  60.4 5.8 %collective-permute-start.3 = (f32[8,256]{1,0:T(8,128)S(1)}, f32[8,256]{1,0:T(8,128)S(1)}, u32[]{:S(2)}, u32[]{:S(2)}) collective-permute-start(f32[8,256]{1,0:T(8,128)S(1)} %shard_map.125.own), channel_id=1, source_target_pairs={{1,0},{2,1},{3,2},{4,3},{5,4},{6,5},{7,6},{8,7},{9,8},{10,9},{11,1... | collective-permute-start | bytes 24584 | tf_op jit(solution)/shard_map/ppermute | solution.py:478
  61.9 5.2 %collective-permute-start.2 = (f32[8,256]{1,0:T(8,128)S(1)}, f32[8,256]{1,0:T(8,128)S(1)}, u32[]{:S(2)}, u32[]{:S(2)}) collective-permute-start(f32[8,256]{1,0:T(8,128)S(1)} %shard_map.125.own), channel_id=1, source_target_pairs={{0,1},{1,2},{2,3},{3,4},{4,5},{5,6},{6,7},{7,8},{8,9},{9,10},{10,1... | collective-permute-start | bytes 24584 | tf_op jit(solution)/shard_map/ppermute | solution.py:477
  82.4 23.2 %all-to-all-start.4 = ((bf16[16,16,256]{2,1,0:T(8,128)(2,1)}), bf16[16,16,256]{2,1,0:T(8,128)(2,1)S(1)}, u32[]{:S(2)}, u32[]{:S(2)}) async-start(bf16[16,16,256]{2,1,0:T(8,128)(2,1)} %get-tuple-element.57), calls=%async_computation.4 | async-start | bytes 262144 | tf_op jit(solution)/shard_map/all_to_all | solution.py:400

commit v4 on v3

--- a/solution.py
+++ b/solution.py
@@ -15,7 +15,8 @@
 R = 8
 HALO = 6
 EXT = R + 2 * HALO
-SMALL = 16
+EDGE = HALO - 1
+FIELDS = 6
 Q = 16
 PIECE = 32
 BF = jnp.bfloat16
@@ -135,21 +136,52 @@
     return total
 
 
-def pack_kernel(upstream, equilibrium, masks, measurement, saved, out, top, bottom, small):
-    small[...] = jnp.zeros_like(small)
+def pack_kernel(upstream, equilibrium, masks, measurement, saved, out, top, bottom, own_fields,
+                up_in, fixed_in, masks_in, snapshot_in, saved_in, sems):
+    copies = [
+        pltpu.make_async_copy(source, target, sems.at[k])
+        for k, (source, target) in enumerate((
+            (saved, saved_in), (upstream, up_in), (equilibrium, fixed_in), (masks, masks_in),
+            (measurement, snapshot_in)))
+    ]
+    for copy in copies:
+        copy.start()
+    for copy in copies[1:]:
+        copy.wait()
+
+    def by_frame(ref):
+        return jnp.concatenate([ref[0], ref[1]], axis=1)
+
+    up = by_frame(up_in)
+    fixed = by_frame(fixed_in)
+    mask = by_frame(masks_in).astype(F32)
+    snapshot = snapshot_in[...]
+    for k, field in enumerate((up, mask, fixed, twice(snapshot))):
+        own_fields[k * R:(k + 1) * R, :] = field
+    fields = (*split_parts(up), *split_parts(fixed), mask.astype(BF),
+              jnp.concatenate(split_parts(snapshot), axis=1))
+    for k in range(0, len(fields), 2):
+        pair = jnp.concatenate([field.astype(F32) for field in fields[k:k + 2]], axis=0).astype(BF)
+        at = EDGE * C + k * R
+        top[at:at + 2 * R, :] = pair
+        bottom[at:at + 2 * R, :] = pair
+    copies[0].wait()
     for frame in range(2):
-        fields = (*split_parts(upstream[frame]), *split_parts(equilibrium[frame]),
-                  masks[frame].astype(F32), split_parts(measurement[...])[frame])
-        for slot, field in enumerate(fields):
-            small[frame, pl.ds(slot, R, stride=SMALL), :] = field.astype(F32)
         lanes = slice(frame * W, (frame + 1) * W)
-        out[:, C:, lanes] = small[frame].astype(BF).reshape(R, SMALL, W)
-        out[:, :C, lanes] = jnp.swapaxes(saved[frame].astype(F32), 0, 1).astype(BF)
-    top[...] = out[:HALO]
-    bottom[...] = out[R - HALO:]
-
-
-def weights_kernel(first, second, third, forward_w, third_w, second_w, first_w):
+        rows = jnp.swapaxes(saved_in[frame].astype(F32), 0, 1).astype(BF).reshape(R * C, W)
+        out[:, lanes] = rows
+        top[:EDGE * C, lanes] = rows[:EDGE * C]
+        bottom[:EDGE * C, lanes] = rows[(R - EDGE) * C:]
+
+
+def stage_kernel(first, second, third, saved, own_fields, forward_w, third_w, second_w, first_w,
+                 gate2, hidden2, fields):
+    fields[...] = own_fields[...]
+    for r in range(R):
+        value = saved_row(saved, r).astype(F32)
+        logistic, slope = slope_parts(value)
+        gate2[r * C:(r + 1) * C, :] = slope
+        hidden2[r * C:(r + 1) * C, :] = (value * logistic).astype(BF)
     forward = first[...].astype(F32)
     backward = third[...].astype(F32)
     pad = jnp.zeros((Q - 6, C), F32)
@@ -168,23 +200,28 @@
     first_w[...] = jnp.concatenate([forward, jnp.zeros((Q - 9, C), F32)], axis=0).astype(BF)
 
 
-def unpack_kernel(step, low, own, high, part, up, masks, base, small):
-    pieces = ((low, 0, HALO), (own, HALO, R), (high, HALO + R, HALO))
-    for ref, at, count in pieces:
-        put_rows(small, at * SMALL, ref[...].astype(F32).reshape(count * SMALL, LANES))
-    def channel(slot):
-        return take_slot(small, slot, EXT)
-    up[...] = channel(0) + channel(1)
-    mask = channel(4)
-    masks[...] = mask
-    fixed = channel(2) + channel(3)
-    pair = channel(5)
-    snapshot = pair[:, :W] + pair[:, W:]
-    base[...] = fixed + step * mask * twice(snapshot)
-    total = masked_sum(mask, fixed)
+def unpack_kernel(step, low, own_fields, high, part, up, masks, base, fixed, snapshot):
+    for k, target in enumerate((up, masks, fixed, snapshot)):
+        target[HALO:HALO + R, :] = own_fields[k * R:(k + 1) * R, :]
+    for ref, at, first in ((low, 0, R - HALO), (high, HALO + R, 0)):
+        fields = ref[EDGE * C:EDGE * C + FIELDS * R, :].astype(F32)
+
+        def field(k):
+            return fields[k * R:(k + 1) * R]
+
+        for target, value in ((up, field(0) + field(1)), (fixed, field(2) + field(3)),
+                              (masks, field(4)),
+                              (snapshot, twice(field(5)[:, :W] + field(5)[:, W:]))):
+            target[at:at + HALO, :] = value[first:first + HALO]
+    total = masked_sum(masks[...], fixed[...])
     for k in range(part.shape[0]):
         part[k, 0:EXT, :] = total
         part[k, EXT:, :] = jnp.zeros((part.shape[1] - EXT, W), F32)
+    base[...] = fixed[...] + step * masks[...] * snapshot[...]
+
+
+def saved_row(ref, at):
+    return ref[at * C:(at + 1) * C, :]
 
 
 def keep_row(value, at, before, after):
@@ -199,14 +236,12 @@
     copies[...] = jnp.zeros_like(copies)
     for k in range(EXT - 2):
         at = k + 1
-        if at < HALO:
-            value = low[at]
-        elif at < HALO + R:
-            value = own[at - HALO]
+        if HALO <= at < HALO + R:
+            gate2[k * C:(k + 1) * C, :] = saved_row(own, at - HALO)
         else:
-            value = high[at - HALO - R]
-        slope = slope_parts(value.astype(F32))[1]
-        gate2[k * C:(k + 1) * C, :] = keep_row(slope, at, inside[0], inside[1])
+            value = saved_row(low, k) if at < HALO else saved_row(high, at - HALO - R)
+            slope = slope_parts(value.astype(F32))[1]
+            gate2[k * C:(k + 1) * C, :] = keep_row(slope, at, inside[0], inside[1])
     for k, total in back_rows(0, up[...], gate2, third_w[...], second_w[...], copies, d2):
         back[k * C:(k + 1) * C, :] = total
 
@@ -279,7 +314,7 @@
     finish_wide(field, inside[0], inside[1], masks, part, moved)
 
 
-def last_kernel(step, sums, moved, up, masks, gate2, gate1, saved, hidden, inputs, third_w,
+def last_kernel(step, sums, moved, up, masks, gate2, gate1, hidden2, hidden, inputs, third_w,
                 second_w, first_w, adjoint, grads, copies, d2, d1, taps, total):
     copies[...] = jnp.zeros_like(copies)
     field = narrow_field(step, sums, moved, up, masks)
@@ -302,8 +337,7 @@
         left_first.append(inputs[r * Q:(r + 3) * Q, :])
         right_first.append(d1[(r + 1) * C:(r + 2) * C, :])
         left_third.append(take_rows(copies, (r + 2) * Q, (r + 5) * Q).astype(BF))
-        wide = saved[r].astype(F32)
-        right_third.append((wide * slope_parts(wide)[0]).astype(BF))
+        right_third.append(saved_row(hidden2, r))
     def join(parts):
         return jnp.concatenate(parts, axis=1)
     second = dot_nt(join(left), join(right))
@@ -371,24 +405,19 @@
             third[tap:tap + 1, :] = total[at:at + 1, 3 * C:] + total[at + 3:at + 4, 3 * C:]
 
 
-def call(kernel, outs, scratch, *operands, specs=None, cost=None, limit=40):
-    grid = () if specs is None else (1,)
+def call(kernel, outs, scratch, *operands, specs=None, cost=None, sems=0, limit=40):
     if specs is None:
         specs = [pl.BlockSpec(memory_space=pltpu.VMEM)] * len(operands)
     return pl.pallas_call(
         kernel,
-        grid=grid,
         out_shape=[jax.ShapeDtypeStruct(shape, dtype) for shape, dtype in outs],
         in_specs=specs,
         out_specs=[pl.BlockSpec(memory_space=pltpu.VMEM)] * len(outs),
-        scratch_shapes=[pltpu.VMEM(shape, dtype) for shape, dtype in scratch],
+        scratch_shapes=[pltpu.VMEM(shape, dtype) for shape, dtype in scratch]
+        + [pltpu.SemaphoreType.DMA((sems,))] * (sems > 0),
         compiler_params=pltpu.CompilerParams(vmem_limit_bytes=limit * 2**20),
         cost_estimate=cost,
     )(*operands)
-
-
-def full_block(*shape):
-    return pl.BlockSpec(shape, lambda _: (0,) * len(shape))
 
 
 def split_parts(field):
@@ -412,34 +441,32 @@
     place = lax.axis_index(SPACE)
     inside = jnp.stack([place > 0, place < tiles - 1]).astype(F32)
 
-    edge = ((HALO, C + SMALL, LANES), BF)
-    pack, top, bottom = call(
-        pack_kernel, [((R, C + SMALL, LANES), BF), edge, edge], [((2, R * SMALL, W), F32)],
+    hbm = pl.BlockSpec(memory_space=pltpu.HBM)
+    edge = ((EDGE * C + FIELDS * R, LANES), BF)
+    fields = ((4 * R, LANES), F32)
+    frame = ((2, R, W), F32)
+    own, top, bottom, own_fields = call(
+        pack_kernel, [((R * C, LANES), BF), edge, edge, fields],
+        [frame, frame, ((2, R, W), jnp.int32), ((R, W), F32), ((2, C, R, W), BF)],
         upstream, equilibrium, coding_masks, measurement, saved_second,
-        specs=[full_block(2, R, W)] * 3 + [full_block(R, W), full_block(2, C, R, W)], limit=60)
+        specs=[hbm] * 5, sems=5, limit=60)
     low = lax.ppermute(bottom, SPACE, forward)
     high = lax.ppermute(top, SPACE, backward)
 
-    forward_w, third_w, second_w, first_w = call(
-        weights_kernel,
-        [((C, 3 * Q), BF), ((C, 3 * Q), BF), ((3 * C, 3 * C), BF), ((Q, C), BF)], [],
-        conv_first, conv_second, conv_third,
-        specs=[full_block(9, C), full_block(9, C, C), full_block(9, C)],
+    forward_w, third_w, second_w, first_w, gate2_own, hidden2, own_fields = call(
+        stage_kernel,
+        [((C, 3 * Q), BF), ((C, 3 * Q), BF), ((3 * C, 3 * C), BF), ((Q, C), BF),
+         ((R * C, LANES), F32), ((R * C, LANES), BF), fields], [],
+        conv_first, conv_second, conv_third, own, own_fields,
         cost=pl.CostEstimate(flops=2 * 10**6, bytes_accessed=10**6, transcendentals=0))
-
-    def rows_of(count, channels_at, width):
-        return pl.BlockSpec((count, width, LANES), lambda _: (0, channels_at, 0))
 
     whole = pl.BlockSpec(memory_space=pltpu.VMEM)
     scalars = pl.BlockSpec(memory_space=pltpu.SMEM)
     ext = ((EXT, LANES), F32)
     part, up, masks, base = call(
         functools.partial(unpack_kernel, step),
-        [((frames, 24, W), F32), ext, ext, ext],
-        [((2, EXT * SMALL, W), F32)],
-        low, pack, high,
-        specs=[rows_of(HALO, C // SMALL, SMALL), rows_of(R, C // SMALL, SMALL),
-               rows_of(HALO, C // SMALL, SMALL)])
+        [((frames, 24, W), F32), ext, ext, ext], [ext, ext],
+        low, own_fields, high)
     sums = exchange(part, TM)
 
     narrow = EXT - 6
@@ -454,8 +481,8 @@
     gate2, back = call(
         early_kernel,
         [(((EXT - 2) * C, LANES), F32), (((EXT - 4) * C, LANES), F32)], [copies, d2],
-        inside, low, pack, high, up, third_w, second_w,
-        specs=[scalars, rows_of(HALO, 0, C), rows_of(R, 0, C), rows_of(HALO, 0, C)] + [whole] * 3,
+        inside, low, gate2_own, high, up, third_w, second_w,
+        specs=[scalars] + [whole] * 6,
         cost=pl.CostEstimate(flops=10**9, bytes_accessed=8 * 10**6, transcendentals=3 * 10**5))
     part, moved, gate1, hidden, inputs = call(
         functools.partial(first_kernel, step),
@@ -492,8 +519,7 @@
         functools.partial(last_kernel, step),
         [((2, R, W), F32), ((near_count, piece, LANES), BF)],
         slim_scratch + [((3 * C + piece, LANES), F32)],
-        sums, moved, up, masks, gate2, gate1, pack, hidden, inputs, *weights,
-        specs=[whole] * 6 + [rows_of(R, 0, C)] + [whole] * 5)
+        sums, moved, up, masks, gate2, gate1, hidden2, hidden, inputs, *weights)
 
     received = exchange(grads, NEAR)
     near_stride = near_count // near_sizes[0]

time: 138 us -> 136 us (0.986)
  waiting for transfers between devices: 15.1 us -> 12 us
  local copies, waits for them, and re-layouts: 4.23 us -> 5.83 us
    ppermute x1, waiting for transfers between devices: 3.21 us -> 0.01 us  [per_device(): high = lax.ppermute(top, SPACE, backward)]
    unnamed x12 -> x14, local copies, waits for them, and re-layouts: 4.23 us -> 5.83 us
  transfers between devices with their start and end apart: 6 -> 6, of which waited for: 4 -> 3; matrix products, arithmetic and copies ran while one was open for 0% -> 0% of each run, Pallas kernels for 2% -> 2%
where the time goes in v4:
time: 136 us; the launch traced here: 135 us
  blocking collectives  63.2 us (46%)
  starting transfers between devices  40.7 us (30%)
  Pallas kernels  12.5 us (9%)
  waiting for transfers between devices  12 us (9%)
  local copies, waits for them, and re-layouts  5.83 us (4%)
    all_to_all x5, blocking collectives, exchange(): return lax.all_to_all(value, axis, 0, 0, tiled=True)  63.2 us
    all_to_all x2, starting transfers between devices, exchange(): return lax.all_to_all(value, axis, 0, 0, tiled=True)  29.8 us
    pallas_call x12, Pallas kernels, call(): pl.pallas_call(kernel, out_shape=[jax.ShapeDtypeStruct(shape, dtype) for...  12.5 us
    all_to_all x2, waiting for transfers between devices, exchange(): return lax.all_to_all(value, axis, 0, 0, tiled=True)  11.3 us
    unnamed x14, local copies, waits for them, and re-layouts  5.83 us
    ppermute x1, starting transfers between devices, per_device(): field_low = lax.ppermute(field, SPACE, forward)  4.41 us
    ppermute x1, starting transfers between devices, per_device(): low = lax.ppermute(bottom, SPACE, forward)  3.96 us
  transfers between devices with their start and end apart: 6, of which 3 were waited for; matrix products, arithmetic and copies ran while one was open for 0% of the time, Pallas kernels for 2%

profile of v4, /device:TPU:1, one launch (start us, length us, event | category | flops | bytes accessed | tf_op | source)
XLA Modules:
  0.0 135.2 jit_solution(3348582699913598083)
XLA Ops:
  0.6 1.9 %shard_map.119 = (bf16[512,256]{1,0:T(8,128)(2,1)}, bf16[368,256]{1,0:T(8,128)(2,1)}, bf16[368,256]{1,0:T(8,128)(2,1)}, f32[32,256]{1,0:T(8,128)}) custom-call(f32[2,8,128]{2,1,0:T(8,128)} %upstream.1, f32[2,8,128]{2,1,0:T(8,128)} %equilibrium.1, s32[2,8,128]{2,1,0:T(8,128)} %masks.1, f32[8,128]{1,0:T(8,128)} %measurement.1, bf16[2,64,8,128]{3,2,1,0:T(8,128)(2,1)} %saved.1), custom_call_target="tpu_custom_call" | custom-call | tf_op jit(solution)/shard_map/pallas_call | solution.py:411
  2.6 4.0 %collective-permute-start = (bf16[368,256]{1,0:T(8,128)(2,1)}, bf16[368,256]{1,0:T(8,128)(2,1)S(1)}, u32[]{:S(2)}, u32[]{:S(2)}) collective-permute-start(bf16[368,256]{1,0:T(8,128)(2,1)} %get-tuple-element.38), channel_id=1, source_target_pairs={{0,1},{1,2},{2,3},{3,4},{4,5},{5,6},{6,7},{7,8},{8,9},{9,10},{10,1... | collective-permute-start | bytes 565256 | tf_op jit(solution)/shard_map/ppermute | solution.py:453
  6.5 1.3 collective-permute-start.1
  7.9 0.0 copy-start
  7.9 0.9 copy-done
  8.8 0.0 copy-start.1
  8.8 0.9 copy-done.1
  9.7 0.0 copy-start.2
  9.7 0.8 copy-done.2
  10.5 0.0 copy-start.3
  10.5 0.7 copy-done.3
  11.2 0.0 copy-start.4
  11.2 0.7 copy-done.4
  11.9 0.5 shard_map.120
  12.3 0.0 copy-start.5
  12.3 0.8 copy-done.5
  13.1 0.0 collective-permute-done.low
  13.1 0.0 collective-permute-done.1.high
  13.1 0.7 shard_map.121
  13.8 13.0 %all-to-all-start = ((f32[8,24,128]{2,1,0:T(8,128)}), f32[8,24,128]{2,1,0:T(8,128)S(1)}, u32[]{:S(2)}, u32[]{:S(2)}) async-start(f32[8,24,128]{2,1,0:T(8,128)} %get-tuple-element.43), calls=%async_computation | async-start | bytes 196608 | tf_op jit(solution)/shard_map/all_to_all | solution.py:429
  26.8 0.1 add_convert_fusion.inside
  26.8 0.0 copy-start.6
  26.8 1.0 copy-done.6
  27.9 1.6 %shard_map.122 = (f32[1152,256]{1,0:T(8,128)S(1)}, f32[1024,256]{1,0:T(8,128)S(1)}) custom-call(f32[2]{0:T(128)S(1)} %add_convert_fusion.inside, bf16[368,256]{1,0:T(8,128)(2,1)S(1)} %collective-permute-done.low, f32[512,256]{1,0:T(8,128)S(1)} %copy-done.6, bf16[368,256]{1,0:T(8,128)(2,1)S(1)} %collective-permute-done.1.high, ...), custom_call_target="tpu_custom_call" | custom-call | flops 1000000000 | bytes 8000000 | tf_op jit(solution)/shard_map/pallas_call | solution.py:411
  29.5 4.9 %all-to-all-done.sums = f32[8,24,128]{2,1,0:T(8,128)S(1)} async-done(((f32[8,24,128]{2,1,0:T(8,128)}), f32[8,24,128]{2,1,0:T(8,128)S(1)}, u32[]{:S(2)}, u32[]{:S(2)}) %all-to-all-start) | async-done | bytes 98336 | tf_op jit(solution)/shard_map/all_to_all | solution.py:429
  34.4 1.4 %shard_map.123 = (f32[8,16,128]{2,1,0:T(8,128)S(1)}, f32[14,256]{1,0:T(8,128)S(1)}, f32[1024,256]{1,0:T(8,128)S(1)}, bf16[512,256]{1,0:T(8,128)(2,1)S(1)}, bf16[160,256]{1,0:T(8,128)(2,1)S(1)}) custom-call(f32[2]{0:T(128)S(1)} %add_convert_fusion.inside, f32[8,24,128]{2,1,0:T(8,128)S(1)} %all-to-all-done.sums, f32[20,256]{1,0:T(8,128)S(1)} %get-tuple-element.44.up, ...), custom_call_target="tpu_custom_call" | custom-call | tf_op jit(solution)/shard_map/pallas_call | solution.py:411
  35.8 10.9 %all_to_all.35.sums = f32[8,16,128]{2,1,0:T(8,128)S(1)} all-to-all(f32[8,16,128]{2,1,0:T(8,128)S(1)} %get-tuple-element.53), channel_id=1, replica_groups=mesh['zh'=4,'core'=2,'zl'=2,'y'=8,'x'=4] {'zh','core'}, dimensions={0} | all-to-all | bytes 131072 | tf_op jit(solution)/shard_map/all_to_all | solution.py:429
  46.7 1.0 shard_map.124
  47.7 10.3 %all_to_all.36.sums = f32[8,8,128]{2,1,0:T(8,128)S(1)} all-to-all(f32[8,8,128]{2,1,0:T(8,128)S(1)} %get-tuple-element.57), channel_id=1, replica_groups=mesh['zh'=4,'core'=2,'zl'=2,'y'=8,'x'=4] {'zh','core'}, dimensions={0} | all-to-all | bytes 65536 | tf_op jit(solution)/shard_map/all_to_all | solution.py:429
  58.1 1.3 collective-permute-start.3
  59.4 4.4 %collective-permute-start.2 = (f32[8,256]{1,0:T(8,128)S(1)}, f32[8,256]{1,0:T(8,128)S(1)}, u32[]{:S(2)}, u32[]{:S(2)}) collective-permute-start(f32[8,256]{1,0:T(8,128)S(1)} %shard_map.125.own), channel_id=1, source_target_pairs={{0,1},{1,2},{2,3},{3,4},{4,5},{5,6},{6,7},{7,8},{8,9},{9,10},{10,1... | collective-permute-start | bytes 24584 | tf_op jit(solution)/shard_map/ppermute | solution.py:504
  63.8 0.0 collective-permute-done.3.high
  63.8 0.8 collective-permute-done.2.low
  64.6 1.8 %shard_map.126 = (f32[8,16,128]{2,1,0:T(8,128)S(1)}, f32[14,256]{1,0:T(8,128)S(1)}) custom-call(f32[2]{0:T(128)S(1)} %add_convert_fusion.inside, f32[8,256]{1,0:T(8,128)S(1)} %collective-permute-done.2.low, f32[8,256]{1,0:T(8,128)S(1)} %shard_map.125.own, f32[8,256]{1,0:T(8,128)S(1)} %collective-permute-done.3.high, f32[20,256]{1,0:T(8,128)S(1)} %get-tuple-element.45.masks, ...), custom_call_target="tpu_custom_call" | custom-call | tf_op jit(solution)/shard_map/pallas_call | solution.py:411
  66.4 11.4 %all_to_all.37.sums = f32[8,16,128]{2,1,0:T(8,128)S(1)} all-to-all(f32[8,16,128]{2,1,0:T(8,128)S(1)} %get-tuple-element.59), channel_id=1, replica_groups=mesh['zh'=4,'core'=2,'zl'=2,'y'=8,'x'=4] {'zh','core'}, dimensions={0} | all-to-all | bytes 131072 | tf_op jit(solution)/shard_map/all_to_all | solution.py:429
  77.8 2.1 %shard_map.127 = (f32[2,8,128]{2,1,0:T(8,128)}, bf16[16,16,256]{2,1,0:T(8,128)(2,1)}) custom-call(f32[8,16,128]{2,1,0:T(8,128)S(1)} %all_to_all.37.sums, f32[14,256]{1,0:T(8,128)S(1)} %get-tuple-element.60.moved, f32[20,256]{1,0:T(8,128)S(1)} %get-tuple-element.44.up, f32[20,256]{1,0:T(8,128)S(1)} %get-tuple-element.45.masks, ...), custom_call_target="tpu_custom_call" | custom-call | tf_op jit(solution)/shard_map/pallas_call | solution.py:411
  79.9 16.8 %all-to-all-start.4 = ((bf16[16,16,256]{2,1,0:T(8,128)(2,1)}), bf16[16,16,256]{2,1,0:T(8,128)(2,1)S(1)}, u32[]{:S(2)}, u32[]{:S(2)}) async-start(bf16[16,16,256]{2,1,0:T(8,128)(2,1)} %get-tuple-element.65), calls=%async_computation.4 | async-start | bytes 262144 | tf_op jit(solution)/shard_map/all_to_all | solution.py:429
  96.7 6.3 %all-to-all-done.4.received = bf16[16,16,256]{2,1,0:T(8,128)(2,1)S(1)} async-done(((bf16[16,16,256]{2,1,0:T(8,128)(2,1)}), bf16[16,16,256]{2,1,0:T(8,128)(2,1)S(1)}, u32[]{:S(2)}, u32[]{:S(2)}) %all-to-all-start.4) | async-done | bytes 131104 | tf_op jit(solution)/shard_map/all_to_all | solution.py:429
  103.1 18.7 %all_to_all.38.received = bf16[32,16,256]{2,1,0:T(8,128)(2,1)S(1)} all-to-all(bf16[32,16,256]{2,1,0:T(8,128)(2,1)S(1)} %shard_map.128), channel_id=1, replica_groups=mesh['zh'=4,'core'=2,'zl'=2,'y'=8,'x'=4] {'zh','y'}, dimensions={0} | all-to-all | bytes 524288 | tf_op jit(solution)/shard_map/all_to_all | solution.py:429
  121.8 0.6 shard_map.129
  122.4 11.9 %all_to_all.39.received = bf16[16,16,256]{2,1,0:T(8,128)(2,1)S(1)} all-to-all(bf16[16,16,256]{2,1,0:T(8,128)(2,1)S(1)} %get-tuple-element.67), channel_id=1, replica_groups=mesh['zh'=4,'core'=2,'zl'=2,'y'=8,'x'=4] {'core','zl','x'}, dimensions={0} | all-to-all | bytes 262144 | tf_op jit(solution)/shard_map/all_to_all | solution.py:429
  134.3 0.8 shard_map.130
  (2 shorter events, 0.1 us)
Async XLA Ops:
  2.6 10.6 %collective-permute-start = (bf16[368,256]{1,0:T(8,128)(2,1)}, bf16[368,256]{1,0:T(8,128)(2,1)S(1)}, u32[]{:S(2)}, u32[]{:S(2)}) collective-permute-start(bf16[368,256]{1,0:T(8,128)(2,1)} %get-tuple-element.38), channel_id=1, source_target_pairs={{0,1},{1,2},{2,3},{3,4},{4,5},{5,6},{6,7},{7,8},{8,9},{9,10},{10,1... | collective-permute-start | bytes 565256 | tf_op jit(solution)/shard_map/ppermute | solution.py:453
  6.5 6.6 %collective-permute-start.1 = (bf16[368,256]{1,0:T(8,128)(2,1)}, bf16[368,256]{1,0:T(8,128)(2,1)S(1)}, u32[]{:S(2)}, u32[]{:S(2)}) collective-permute-start(bf16[368,256]{1,0:T(8,128)(2,1)} %get-tuple-element.42), channel_id=1, source_target_pairs={{1,0},{2,1},{3,2},{4,3},{5,4},{6,5},{7,6},{8,7},{9,8},{10,9},{11,1... | collective-permute-start | bytes 565256 | tf_op jit(solution)/shard_map/ppermute | solution.py:454
  7.9 1.0 copy-start
  8.8 0.9 copy-start.1
  9.7 0.8 copy-start.2
  10.5 0.7 copy-start.3
  11.2 0.7 copy-start.4
  12.3 0.8 copy-start.5
  13.8 20.6 %all-to-all-start = ((f32[8,24,128]{2,1,0:T(8,128)}), f32[8,24,128]{2,1,0:T(8,128)S(1)}, u32[]{:S(2)}, u32[]{:S(2)}) async-start(f32[8,24,128]{2,1,0:T(8,128)} %get-tuple-element.43), calls=%async_computation | async-start | bytes 196608 | tf_op jit(solution)/shard_map/all_to_all | solution.py:429
  26.8 1.0 copy-start.6
  58.1 5.7 %collective-permute-start.3 = (f32[8,256]{1,0:T(8,128)S(1)}, f32[8,256]{1,0:T(8,128)S(1)}, u32[]{:S(2)}, u32[]{:S(2)}) collective-permute-start(f32[8,256]{1,0:T(8,128)S(1)} %shard_map.125.own), channel_id=1, source_target_pairs={{1,0},{2,1},{3,2},{4,3},{5,4},{6,5},{7,6},{8,7},{9,8},{10,9},{11,1... | collective-permute-start | bytes 24584 | tf_op jit(solution)/shard_map/ppermute | solution.py:505
  59.4 5.2 %collective-permute-start.2 = (f32[8,256]{1,0:T(8,128)S(1)}, f32[8,256]{1,0:T(8,128)S(1)}, u32[]{:S(2)}, u32[]{:S(2)}) collective-permute-start(f32[8,256]{1,0:T(8,128)S(1)} %shard_map.125.own), channel_id=1, source_target_pairs={{0,1},{1,2},{2,3},{3,4},{4,5},{5,6},{6,7},{7,8},{8,9},{9,10},{10,1... | collective-permute-start | bytes 24584 | tf_op jit(solution)/shard_map/ppermute | solution.py:504
  79.9 23.2 %all-to-all-start.4 = ((bf16[16,16,256]{2,1,0:T(8,128)(2,1)}), bf16[16,16,256]{2,1,0:T(8,128)(2,1)S(1)}, u32[]{:S(2)}, u32[]{:S(2)}) async-start(bf16[16,16,256]{2,1,0:T(8,128)(2,1)} %get-tuple-element.65), calls=%async_computation.4 | async-start | bytes 262144 | tf_op jit(solution)/shard_map/all_to_all | solution.py:429

commit v5 on v4

--- a/solution.py
+++ b/solution.py
@@ -200,7 +200,7 @@
     first_w[...] = jnp.concatenate([forward, jnp.zeros((Q - 9, C), F32)], axis=0).astype(BF)
 
 
-def unpack_kernel(step, low, own_fields, high, part, up, masks, base, fixed, snapshot):
+def unpack_kernel(step, low, own_fields, high, _, part, up, masks, base, fixed, snapshot):
     for k, target in enumerate((up, masks, fixed, snapshot)):
         target[HALO:HALO + R, :] = own_fields[k * R:(k + 1) * R, :]
     for ref, at, first in ((low, 0, R - HALO), (high, HALO + R, 0)):
@@ -293,22 +293,40 @@
                          copies, d2, d1, taps)
     out[...] = result
     total = masked_sum(masks[HALO:HALO + R, :], result)
+    half = jnp.concatenate([total[:R // 2], total[R // 2:]], axis=1)
     for k in range(part.shape[0]):
-        part[k] = total
-
-
-def update_kernel(step, sums, moved, up, masks, out):
-    totals = gathered_sum(sums)
+        part[k, 0:R, :] = result
+        part[k, R:, :] = half
+
+
+def pair_total(received, first):
+    count = received.shape[0] // 2
+    half = received[first, R:, :]
+    for k in range(1, count):
+        half = half + received[first + k, R:, :]
+    return jnp.concatenate([half[:, :W], half[:, W:]], axis=0)
+
+
+def update_kernel(step, place, received, moved, up, masks, out):
+    totals = pair_total(received, place[0])
     out[...] = (up[HALO:HALO + R, :] + moved[...]
                 - step * masks[HALO:HALO + R, :] * twice(totals))
 
 
-def third_kernel(inside, low, own, high, masks, gate2, gate1, third_w, second_w, first_w,
-                 part, moved, copies, d2, d1, taps, whole):
+def third_kernel(step, inside, place, received, own, near, up, masks, gate2, gate1, third_w,
+                 second_w, first_w, part, moved, copies, d2, d1, taps, whole):
     copies[...] = jnp.zeros_like(copies)
-    whole[0:HALO, :] = low[R - HALO:, :]
+    totals = twice(pair_total(received, place[1]))
+    theirs = received[place[2], 0:R, :]
+    after_rows = slice(HALO + R, EXT)
+    low = (up[0:HALO, :] + theirs[R - HALO:]
+           - step * masks[0:HALO, :] * totals[R - HALO:]) * inside[0]
+    high = (up[after_rows, :] + theirs[:HALO]
+            - step * masks[after_rows, :] * totals[:HALO]) * inside[1]
+    odd = place[3] == 1
+    whole[0:HALO, :] = jnp.where(odd, near[R - HALO:, :], low)
     whole[HALO:HALO + R, :] = own[...]
-    whole[HALO + R:, :] = high[:HALO, :]
+    whole[HALO + R:, :] = jnp.where(odd, high, near[:HALO, :])
     field = adjoint_map(0, whole[...], gate2, gate1, third_w[...], second_w[...], first_w[...],
                         copies, d2, d1, taps)
     finish_wide(field, inside[0], inside[1], masks, part, moved)
@@ -466,7 +484,7 @@
     part, up, masks, base = call(
         functools.partial(unpack_kernel, step),
         [((frames, 24, W), F32), ext, ext, ext], [ext, ext],
-        low, own_fields, high)
+        low, own_fields, high, gate2_own)
     sums = exchange(part, TM)
 
     narrow = EXT - 6
@@ -495,18 +513,22 @@
 
     part, moved = call(
         functools.partial(second_kernel, step),
-        [((frames, R, W), F32), ((R, LANES), F32)], slim_scratch,
+        [((2 * frames, R + R // 2, LANES), F32), ((R, LANES), F32)], slim_scratch,
         sums, moved, up, masks, gate2, gate1, *weights)
-    sums = exchange(part, TM)
-
+    groups = [[t * tiles + (k + side) % tiles for side in range(2) for t in range(frames)]
+              for k in range(1, tiles, 2)]
+    received = lax.all_to_all(part, TM + SPACE, 0, 0, axis_index_groups=groups, tiled=True)
+    odd = place % 2
+    mine = frames * (1 - odd)
+    theirs = frames * odd
+    pair_place = jnp.stack([mine, theirs, theirs + lax.axis_index(TM), odd])
     field, = call(functools.partial(update_kernel, step), [((R, LANES), F32)], [],
-                  sums, moved, up, masks)
-    field_low = lax.ppermute(field, SPACE, forward)
-    field_high = lax.ppermute(field, SPACE, backward)
+                  pair_place, received, moved, up, masks, specs=[scalars] + [whole] * 4)
+    near = lax.ppermute(field, SPACE, [(i, i ^ 1) for i in range(tiles)])
     part, moved = call(
-        third_kernel, wide_outs, [copies, d2, d1, taps, ext],
-        inside, field_low, field, field_high, masks, gate2, gate1, *weights,
-        specs=[scalars] + [whole] * 9)
+        functools.partial(third_kernel, step), wide_outs, [copies, d2, d1, taps, ext],
+        inside, pair_place, received, field, near, up, masks, gate2, gate1, *weights,
+        specs=[scalars] * 2 + [whole] * 10)
     sums = exchange(part, TM)
 
     near_sizes = [lax.axis_size(name) for name in NEAR]

time: 136 us -> 138 us (1.015)
  waiting for transfers between devices: 12 us -> 25.1 us
  blocking collectives: 63.2 us -> 55 us
  starting transfers between devices: 40.7 us -> 34.6 us
  local copies, waits for them, and re-layouts: 5.83 us -> 7.43 us
    all_to_all x2, starting transfers between devices: 29.8 us -> 17.5 us  [exchange(): return lax.all_to_all(value, axis, 0, 0, tiled=True)]
    all_to_all x0 -> x1, waiting for transfers between devices: none -> 10.2 us  [per_device(): lax.all_to_all(part, TM + SPACE, 0, 0, axis_index_groups=groups, tiled=True)]
    all_to_all x0 -> x1, starting transfers between devices: none -> 9.72 us  [per_device(): lax.all_to_all(part, TM + SPACE, 0, 0, axis_index_groups=groups, tiled=True)]
    all_to_all x5 -> x4, blocking collectives: 63.2 us -> 55 us  [exchange(): return lax.all_to_all(value, axis, 0, 0, tiled=True)]
    ppermute x2 -> x1, starting transfers between devices: 5.7 us -> 2.05 us  [per_device(): near = lax.ppermute(field, SPACE, [(i, i ^ 1) for i in range(tiles)])]
    ppermute x2 -> x1, waiting for transfers between devices: 0.77 us -> 2.47 us  [per_device(): near = lax.ppermute(field, SPACE, [(i, i ^ 1) for i in range(tiles)])]
    unnamed x14 -> x30, local copies, waits for them, and re-layouts: 5.83 us -> 7.43 us
  transfers between devices with their start and end apart: 6 -> 6, of which waited for: 3 -> 5; matrix products, arithmetic and copies ran while one was open for 0% -> 0% of each run, Pallas kernels for 2% -> 2%
where the time goes in v5:
time: 138 us; the launch traced here: 137 us
  blocking collectives  55 us (40%)
  starting transfers between devices  34.6 us (25%)
  waiting for transfers between devices  25.1 us (18%)
  Pallas kernels  13.7 us (10%)
  local copies, waits for them, and re-layouts  7.43 us (5%)
    all_to_all x4, blocking collectives, exchange(): return lax.all_to_all(value, axis, 0, 0, tiled=True)  55 us
    all_to_all x2, starting transfers between devices, exchange(): return lax.all_to_all(value, axis, 0, 0, tiled=True)  17.5 us
    pallas_call x12, Pallas kernels, call(): pl.pallas_call(kernel, out_shape=[jax.ShapeDtypeStruct(shape, dtype) for...  13.7 us
    all_to_all x2, waiting for transfers between devices, exchange(): return lax.all_to_all(value, axis, 0, 0, tiled=True)  12.3 us
    all_to_all x1, waiting for transfers between devices, per_device(): lax.all_to_all(part, TM + SPACE, 0, 0, axis_index_groups=groups, tiled=True)  10.2 us
    all_to_all x1, starting transfers between devices, per_device(): lax.all_to_all(part, TM + SPACE, 0, 0, axis_index_groups=groups, tiled=True)  9.72 us
    unnamed x30, local copies, waits for them, and re-layouts  7.43 us
    ppermute x1, starting transfers between devices, per_device(): low = lax.ppermute(bottom, SPACE, forward)  3.96 us
  transfers between devices with their start and end apart: 6, of which 5 were waited for; matrix products, arithmetic and copies ran while one was open for 0% of the time, Pallas kernels for 2%

profile of v5, /device:TPU:1, one launch (start us, length us, event | category | flops | bytes accessed | tf_op | source)
XLA Modules:
  0.0 136.7 jit_solution(7780663813399024625)
XLA Ops:
  0.6 1.9 %shard_map.119 = (bf16[512,256]{1,0:T(8,128)(2,1)}, bf16[368,256]{1,0:T(8,128)(2,1)}, bf16[368,256]{1,0:T(8,128)(2,1)}, f32[32,256]{1,0:T(8,128)}) custom-call(f32[2,8,128]{2,1,0:T(8,128)} %upstream.1, f32[2,8,128]{2,1,0:T(8,128)} %equilibrium.1, s32[2,8,128]{2,1,0:T(8,128)} %masks.1, f32[8,128]{1,0:T(8,128)} %measurement.1, bf16[2,64,8,128]{3,2,1,0:T(8,128)(2,1)} %saved.1), custom_call_target="tpu_custom_call" | custom-call | tf_op jit(solution)/shard_map/pallas_call | solution.py:429
  2.6 4.0 %collective-permute-start = (bf16[368,256]{1,0:T(8,128)(2,1)}, bf16[368,256]{1,0:T(8,128)(2,1)S(1)}, u32[]{:S(2)}, u32[]{:S(2)}) collective-permute-start(bf16[368,256]{1,0:T(8,128)(2,1)} %get-tuple-element.38), channel_id=1, source_target_pairs={{0,1},{1,2},{2,3},{3,4},{4,5},{5,6},{6,7},{7,8},{8,9},{9,10},{10,1... | collective-permute-start | bytes 565256 | tf_op jit(solution)/shard_map/ppermute | solution.py:471
  6.5 1.3 collective-permute-start.1
  7.9 0.0 copy-start.4
  7.9 0.9 copy-done.4
  8.8 0.0 copy-start.5
  8.8 0.9 copy-done.5
  9.7 0.0 copy-start.8
  9.7 0.8 copy-done.8
  10.5 0.0 copy-start.13
  10.5 0.7 copy-done.13
  11.2 0.0 copy-start.14
  11.2 0.7 copy-done.14
  11.9 0.5 shard_map.120
  12.3 0.0 copy-start
  12.3 0.7 copy-done
  13.0 0.0 copy-start.11
  13.0 0.0 collective-permute-done.low
  13.0 0.1 collective-permute-done.1.high
  13.1 0.7 shard_map.121
  13.7 0.0 copy-done.11
  13.8 0.0 copy-start.9
  13.8 0.6 copy-done.9
  14.3 13.0 %all-to-all-start = ((f32[8,24,128]{2,1,0:T(8,128)}), f32[8,24,128]{2,1,0:T(8,128)S(1)}, u32[]{:S(2)}, u32[]{:S(2)}) async-start(f32[8,24,128]{2,1,0:T(8,128)} %get-tuple-element.44), calls=%async_computation | async-start | bytes 196608 | tf_op jit(solution)/shard_map/all_to_all | solution.py:447
  27.4 0.1 add_convert_fusion.inside
  27.4 1.6 %shard_map.122 = (f32[1152,256]{1,0:T(8,128)S(1)}, f32[1024,256]{1,0:T(8,128)S(1)}) custom-call(f32[2]{0:T(128)S(1)} %add_convert_fusion.inside, bf16[368,256]{1,0:T(8,128)(2,1)S(1)} %collective-permute-done.low, f32[512,256]{1,0:T(8,128)S(1)} %get-tuple-element.43._.own, bf16[368,256]{1,0:T(8,128)(2,1)S(1)} %collective-permute-done.1.high, ...), custom_call_target="tpu_custom_call" | custom-call | flops 1000000000 | bytes 8000000 | tf_op jit(solution)/shard_map/pallas_call | solution.py:429
  29.1 5.9 %all-to-all-done.sums = f32[8,24,128]{2,1,0:T(8,128)S(1)} async-done(((f32[8,24,128]{2,1,0:T(8,128)}), f32[8,24,128]{2,1,0:T(8,128)S(1)}, u32[]{:S(2)}, u32[]{:S(2)}) %all-to-all-start) | async-done | bytes 98336 | tf_op jit(solution)/shard_map/all_to_all | solution.py:447
  35.0 0.0 copy-start.10
  35.0 0.7 copy-done.10
  35.7 0.0 copy-start.12
  35.7 0.7 copy-done.12
  36.4 1.4 %shard_map.123 = (f32[8,16,128]{2,1,0:T(8,128)S(1)}, f32[14,256]{1,0:T(8,128)S(1)}, f32[1024,256]{1,0:T(8,128)S(1)}, bf16[512,256]{1,0:T(8,128)(2,1)S(1)}, bf16[160,256]{1,0:T(8,128)(2,1)S(1)}) custom-call(f32[2]{0:T(128)S(1)} %add_convert_fusion.inside, f32[8,24,128]{2,1,0:T(8,128)S(1)} %all-to-all-done.sums, f32[20,256]{1,0:T(8,128)S(1)} %get-tuple-element.45.up, ...), custom_call_target="tpu_custom_call" | custom-call | tf_op jit(solution)/shard_map/pallas_call | solution.py:429
  37.8 0.0 copy-start.2
  37.8 0.7 copy-done.2
  38.5 0.0 copy-start.6
  38.5 10.9 %all_to_all.35.sums = f32[8,16,128]{2,1,0:T(8,128)S(1)} all-to-all(f32[8,16,128]{2,1,0:T(8,128)S(1)} %get-tuple-element.53), channel_id=1, replica_groups=mesh['zh'=4,'core'=2,'zl'=2,'y'=8,'x'=4] {'zh','core'}, dimensions={0} | all-to-all | bytes 131072 | tf_op jit(solution)/shard_map/all_to_all | solution.py:447
  49.4 1.8 %shard_map.124 = (f32[16,12,256]{2,1,0:T(8,128)}, f32[8,256]{1,0:T(8,128)S(1)}) custom-call(f32[8,16,128]{2,1,0:T(8,128)S(1)} %all_to_all.35.sums, f32[14,256]{1,0:T(8,128)S(1)} %get-tuple-element.54.moved, f32[20,256]{1,0:T(8,128)S(1)} %get-tuple-element.45.up, f32[20,256]{1,0:T(8,128)S(1)} %get-tuple-element.46.masks, ...), custom_call_target="tpu_custom_call" | custom-call | tf_op jit(solution)/shard_map/pallas_call | solution.py:429
  51.2 0.0 copy-done.6
  51.2 9.7 %all-to-all-start.2 = ((f32[16,12,256]{2,1,0:T(8,128)}), f32[16,12,256]{2,1,0:T(8,128)S(1)}, u32[]{:S(2)}, u32[]{:S(2)}) async-start(f32[16,12,256]{2,1,0:T(8,128)} %get-tuple-element.57), calls=%async_computation.2 | async-start | bytes 524288 | tf_op jit(solution)/shard_map/all_to_all | solution.py:520
  60.9 0.1 pad_add_fusion.place
  61.0 10.2 %all-to-all-done.2.received = f32[16,12,256]{2,1,0:T(8,128)S(1)} async-done(((f32[16,12,256]{2,1,0:T(8,128)}), f32[16,12,256]{2,1,0:T(8,128)S(1)}, u32[]{:S(2)}, u32[]{:S(2)}) %all-to-all-start.2) | async-done | bytes 196640 | tf_op jit(solution)/shard_map/all_to_all | solution.py:520
  71.2 0.6 shard_map.125.own
  71.8 0.0 copy-start.1
  71.8 0.0 copy-start.3
  71.8 0.0 copy-start.7
  71.8 2.1 %collective-permute-start.2 = (f32[8,256]{1,0:T(8,128)S(1)}, f32[8,256]{1,0:T(8,128)S(1)}, u32[]{:S(2)}, u32[]{:S(2)}) collective-permute-start(f32[8,256]{1,0:T(8,128)S(1)} %shard_map.125.own), channel_id=1, source_target_pairs={{0,1},{1,0},{2,3},{3,2},{4,5},{5,4},{6,7},{7,6},{8,9},{9,8},{10,11... | collective-permute-start | bytes 24584 | tf_op jit(solution)/shard_map/ppermute | solution.py:527
  73.9 2.5 %collective-permute-done.2.near = f32[8,256]{1,0:T(8,128)S(1)} collective-permute-done((f32[8,256]{1,0:T(8,128)S(1)}, f32[8,256]{1,0:T(8,128)S(1)}, u32[]{:S(2)}, u32[]{:S(2)}) %collective-permute-start.2) | collective-permute-done | bytes 8224 | tf_op jit(solution)/shard_map/ppermute | solution.py:527
  76.3 1.8 %shard_map.126 = (f32[8,16,128]{2,1,0:T(8,128)S(1)}, f32[14,256]{1,0:T(8,128)S(1)}) custom-call(f32[2]{0:T(128)S(1)} %add_convert_fusion.inside, s32[4]{0:T(128)S(1)} %pad_add_fusion.place, f32[16,12,256]{2,1,0:T(8,128)S(1)} %all-to-all-done.2.received, f32[8,256]{1,0:T(8,128)S(1)} %shard_map.125.own, f32[8,256]{1,0:T(8,128)S(1)} %collective-permute-done.2.near, ...), custom_call_target="tpu_custom_call" | custom-call | tf_op jit(solution)/shard_map/pallas_call | solution.py:429
  78.2 11.4 %all_to_all.36.sums = f32[8,16,128]{2,1,0:T(8,128)S(1)} all-to-all(f32[8,16,128]{2,1,0:T(8,128)S(1)} %get-tuple-element.59), channel_id=1, replica_groups=mesh['zh'=4,'core'=2,'zl'=2,'y'=8,'x'=4] {'zh','core'}, dimensions={0} | all-to-all | bytes 131072 | tf_op jit(solution)/shard_map/all_to_all | solution.py:447
  89.5 0.0 copy-done.1
  89.5 0.0 copy-done.3
  89.5 0.0 copy-done.7
  89.5 2.1 %shard_map.127 = (f32[2,8,128]{2,1,0:T(8,128)}, bf16[16,16,256]{2,1,0:T(8,128)(2,1)}) custom-call(f32[8,16,128]{2,1,0:T(8,128)S(1)} %all_to_all.36.sums, f32[14,256]{1,0:T(8,128)S(1)} %get-tuple-element.60.moved, f32[20,256]{1,0:T(8,128)S(1)} %get-tuple-element.45.up, f32[20,256]{1,0:T(8,128)S(1)} %get-tuple-element.46.masks, ...), custom_call_target="tpu_custom_call" | custom-call | tf_op jit(solution)/shard_map/pallas_call | solution.py:429
  91.6 4.5 %all-to-all-start.4 = ((bf16[16,16,256]{2,1,0:T(8,128)(2,1)}), bf16[16,16,256]{2,1,0:T(8,128)(2,1)S(1)}, u32[]{:S(2)}, u32[]{:S(2)}) async-start(bf16[16,16,256]{2,1,0:T(8,128)(2,1)} %get-tuple-element.65), calls=%async_computation.4 | async-start | bytes 262144 | tf_op jit(solution)/shard_map/all_to_all | solution.py:447
  96.1 6.3 %all-to-all-done.4.received = bf16[16,16,256]{2,1,0:T(8,128)(2,1)S(1)} async-done(((bf16[16,16,256]{2,1,0:T(8,128)(2,1)}), bf16[16,16,256]{2,1,0:T(8,128)(2,1)S(1)}, u32[]{:S(2)}, u32[]{:S(2)}) %all-to-all-start.4) | async-done | bytes 131104 | tf_op jit(solution)/shard_map/all_to_all | solution.py:447
  102.5 20.8 %all_to_all.37.received = bf16[32,16,256]{2,1,0:T(8,128)(2,1)S(1)} all-to-all(bf16[32,16,256]{2,1,0:T(8,128)(2,1)S(1)} %shard_map.128), channel_id=1, replica_groups=mesh['zh'=4,'core'=2,'zl'=2,'y'=8,'x'=4] {'zh','y'}, dimensions={0} | all-to-all | bytes 524288 | tf_op jit(solution)/shard_map/all_to_all | solution.py:447
  123.3 0.6 shard_map.129
  123.9 12.0 %all_to_all.38.received = bf16[16,16,256]{2,1,0:T(8,128)(2,1)S(1)} all-to-all(bf16[16,16,256]{2,1,0:T(8,128)(2,1)S(1)} %get-tuple-element.67), channel_id=1, replica_groups=mesh['zh'=4,'core'=2,'zl'=2,'y'=8,'x'=4] {'core','zl','x'}, dimensions={0} | all-to-all | bytes 262144 | tf_op jit(solution)/shard_map/all_to_all | solution.py:447
  135.9 0.8 shard_map.130
  (1 shorter events, 0.0 us)
Async XLA Ops:
  2.6 10.4 %collective-permute-start = (bf16[368,256]{1,0:T(8,128)(2,1)}, bf16[368,256]{1,0:T(8,128)(2,1)S(1)}, u32[]{:S(2)}, u32[]{:S(2)}) collective-permute-start(bf16[368,256]{1,0:T(8,128)(2,1)} %get-tuple-element.38), channel_id=1, source_target_pairs={{0,1},{1,2},{2,3},{3,4},{4,5},{5,6},{6,7},{7,8},{8,9},{9,10},{10,1... | collective-permute-start | bytes 565256 | tf_op jit(solution)/shard_map/ppermute | solution.py:471
  6.5 6.5 %collective-permute-start.1 = (bf16[368,256]{1,0:T(8,128)(2,1)}, bf16[368,256]{1,0:T(8,128)(2,1)S(1)}, u32[]{:S(2)}, u32[]{:S(2)}) collective-permute-start(bf16[368,256]{1,0:T(8,128)(2,1)} %get-tuple-element.42), channel_id=1, source_target_pairs={{1,0},{2,1},{3,2},{4,3},{5,4},{6,5},{7,6},{8,7},{9,8},{10,9},{11,1... | collective-permute-start | bytes 565256 | tf_op jit(solution)/shard_map/ppermute | solution.py:472
  7.9 1.0 copy-start.4
  8.8 0.9 copy-start.5
  9.7 0.8 copy-start.8
  10.5 0.7 copy-start.13
  11.2 0.7 copy-start.14
  12.3 0.7 copy-start
  13.0 0.7 copy-start.11
  13.8 0.6 copy-start.9
  14.3 20.6 %all-to-all-start = ((f32[8,24,128]{2,1,0:T(8,128)}), f32[8,24,128]{2,1,0:T(8,128)S(1)}, u32[]{:S(2)}, u32[]{:S(2)}) async-start(f32[8,24,128]{2,1,0:T(8,128)} %get-tuple-element.44), calls=%async_computation | async-start | bytes 196608 | tf_op jit(solution)/shard_map/all_to_all | solution.py:447
  35.0 0.7 copy-start.10
  35.7 0.7 copy-start.12
  37.8 0.7 copy-start.2
  38.5 12.7 %copy-start.6 = (bf16[160,256]{1,0:T(8,128)(2,1)}, bf16[160,256]{1,0:T(8,128)(2,1)S(1)}, u32[]{:S(2)}) copy-start(bf16[160,256]{1,0:T(8,128)(2,1)S(1)} %get-tuple-element.63.inputs) | copy-start | bytes 245764
  51.2 20.0 %all-to-all-start.2 = ((f32[16,12,256]{2,1,0:T(8,128)}), f32[16,12,256]{2,1,0:T(8,128)S(1)}, u32[]{:S(2)}, u32[]{:S(2)}) async-start(f32[16,12,256]{2,1,0:T(8,128)} %get-tuple-element.57), calls=%async_computation.2 | async-start | bytes 524288 | tf_op jit(solution)/shard_map/all_to_all | solution.py:520
  71.8 17.7 %copy-start.1 = (bf16[512,256]{1,0:T(8,128)(2,1)S(1)}, bf16[512,256]{1,0:T(8,128)(2,1)}, u32[]{:S(2)}) copy-start(bf16[512,256]{1,0:T(8,128)(2,1)} %copy-done) | copy-start | bytes 786436
  71.8 17.7 %copy-start.3 = (bf16[512,256]{1,0:T(8,128)(2,1)S(1)}, bf16[512,256]{1,0:T(8,128)(2,1)}, u32[]{:S(2)}) copy-start(bf16[512,256]{1,0:T(8,128)(2,1)} %copy-done.2) | copy-start | bytes 786436
  71.8 17.7 %copy-start.7 = (bf16[160,256]{1,0:T(8,128)(2,1)S(1)}, bf16[160,256]{1,0:T(8,128)(2,1)}, u32[]{:S(2)}) copy-start(bf16[160,256]{1,0:T(8,128)(2,1)} %copy-done.6) | copy-start | bytes 245764
  71.8 4.5 %collective-permute-start.2 = (f32[8,256]{1,0:T(8,128)S(1)}, f32[8,256]{1,0:T(8,128)S(1)}, u32[]{:S(2)}, u32[]{:S(2)}) collective-permute-start(f32[8,256]{1,0:T(8,128)S(1)} %shard_map.125.own), channel_id=1, source_target_pairs={{0,1},{1,0},{2,3},{3,2},{4,5},{5,4},{6,7},{7,6},{8,9},{9,8},{10,11... | collective-permute-start | bytes 24584 | tf_op jit(solution)/shard_map/ppermute | solution.py:527
  91.6 10.9 %all-to-all-start.4 = ((bf16[16,16,256]{2,1,0:T(8,128)(2,1)}), bf16[16,16,256]{2,1,0:T(8,128)(2,1)S(1)}, u32[]{:S(2)}, u32[]{:S(2)}) async-start(bf16[16,16,256]{2,1,0:T(8,128)(2,1)} %get-tuple-element.65), calls=%async_computation.4 | async-start | bytes 262144 | tf_op jit(solution)/shard_map/all_to_all | solution.py:447

commit v6 on v5

--- a/solution.py
+++ b/solution.py
@@ -24,6 +24,7 @@
 
 TM = ("zh", "core")
 SPACE = ("zl", "y", "x")
+BEFORE, AFTER, ODD, OWN_HALF, THEIR_ENTRY, THEIR_HALF, NEAR_AT, FAR_AT = range(8)
 NEAR = ("core", "zl", "x")
 FAR = ("zh", "y")
 
@@ -174,7 +175,7 @@
         bottom[:EDGE * C, lanes] = rows[(R - EDGE) * C:]
 
 
-def stage_kernel(first, second, third, saved, own_fields, forward_w, third_w, second_w, first_w,
+def stage_kernel(_, first, second, third, saved, own_fields, forward_w, third_w, second_w, first_w,
                  gate2, hidden2, fields):
     fields[...] = own_fields[...]
     for r in range(R):
@@ -232,7 +233,12 @@
     return value
 
 
-def early_kernel(inside, low, own, high, up, third_w, second_w, gate2, back, copies, d2):
+def ends(places):
+    return places[BEFORE].astype(F32), places[AFTER].astype(F32)
+
+
+def early_kernel(places, low, own, high, up, third_w, second_w, _, gate2, back, copies, d2):
+    before, after = ends(places)
     copies[...] = jnp.zeros_like(copies)
     for k in range(EXT - 2):
         at = k + 1
@@ -241,13 +247,14 @@
         else:
             value = saved_row(low, k) if at < HALO else saved_row(high, at - HALO - R)
             slope = slope_parts(value.astype(F32))[1]
-            gate2[k * C:(k + 1) * C, :] = keep_row(slope, at, inside[0], inside[1])
+            gate2[k * C:(k + 1) * C, :] = keep_row(slope, at, before, after)
     for k, total in back_rows(0, up[...], gate2, third_w[...], second_w[...], copies, d2):
         back[k * C:(k + 1) * C, :] = total
 
 
-def first_kernel(step, inside, sums, up, masks, base, back, first_w, forward_w,
+def first_kernel(step, places, sums, up, masks, base, back, first_w, forward_w,
                  part, moved, gate1, hidden, inputs, copies, d1, taps):
+    before, after = ends(places)
     frame_sum = gathered_sum(sums)[:EXT]
     denoiser_input = base[...] - step * masks[...] * twice(frame_sum)
     copies[...] = jnp.zeros_like(copies)
@@ -257,14 +264,14 @@
         at = k + 2
         value = dot(forward_w[...], take_rows(copies, (at - 1) * Q, (at + 2) * Q).astype(BF))
         logistic, slope = slope_parts(value)
-        slope = keep_row(slope, at, inside[0], inside[1])
+        slope = keep_row(slope, at, before, after)
         gate1[k * C:(k + 1) * C, :] = slope
         if HALO <= at < HALO + R:
             own_at = at - HALO
             hidden[own_at * C:(own_at + 1) * C, :] = (value * logistic).astype(BF)
         d1[k * C:(k + 1) * C, :] = (slope * back[k * C:(k + 1) * C, :]).astype(BF)
     field = map_end(0, up[...], first_w[...], d1, taps)
-    finish_wide(field, inside[0], inside[1], masks, part, moved)
+    finish_wide(field, before, after, masks, part, moved)
 
 
 def finish_wide(field, before, after, masks, part, moved):
@@ -307,29 +314,30 @@
     return jnp.concatenate([half[:, :W], half[:, W:]], axis=0)
 
 
-def update_kernel(step, place, received, moved, up, masks, out):
-    totals = pair_total(received, place[0])
+def update_kernel(step, places, received, moved, up, masks, out):
+    totals = pair_total(received, places[OWN_HALF])
     out[...] = (up[HALO:HALO + R, :] + moved[...]
                 - step * masks[HALO:HALO + R, :] * twice(totals))
 
 
-def third_kernel(step, inside, place, received, own, near, up, masks, gate2, gate1, third_w,
+def third_kernel(step, places, received, own, near, up, masks, gate2, gate1, third_w,
                  second_w, first_w, part, moved, copies, d2, d1, taps, whole):
     copies[...] = jnp.zeros_like(copies)
-    totals = twice(pair_total(received, place[1]))
-    theirs = received[place[2], 0:R, :]
+    before, after = ends(places)
+    totals = twice(pair_total(received, places[THEIR_HALF]))
+    theirs = received[places[THEIR_ENTRY], 0:R, :]
     after_rows = slice(HALO + R, EXT)
     low = (up[0:HALO, :] + theirs[R - HALO:]
-           - step * masks[0:HALO, :] * totals[R - HALO:]) * inside[0]
+           - step * masks[0:HALO, :] * totals[R - HALO:]) * before
     high = (up[after_rows, :] + theirs[:HALO]
-            - step * masks[after_rows, :] * totals[:HALO]) * inside[1]
-    odd = place[3] == 1
+            - step * masks[after_rows, :] * totals[:HALO]) * after
+    odd = places[ODD] == 1
     whole[0:HALO, :] = jnp.where(odd, near[R - HALO:, :], low)
     whole[HALO:HALO + R, :] = own[...]
     whole[HALO + R:, :] = jnp.where(odd, high, near[:HALO, :])
     field = adjoint_map(0, whole[...], gate2, gate1, third_w[...], second_w[...], first_w[...],
                         copies, d2, d1, taps)
-    finish_wide(field, inside[0], inside[1], masks, part, moved)
+    finish_wide(field, before, after, masks, part, moved)
 
 
 def last_kernel(step, sums, moved, up, masks, gate2, gate1, hidden2, hidden, inputs, third_w,
@@ -390,14 +398,14 @@
     return jnp.where(line < rows, total, extra)
 
 
-def near_kernel(rows, stride, place, received, out):
-    total = reduce_pieces(rows, place[0], stride, received).astype(BF)
+def near_kernel(rows, stride, places, received, out):
+    total = reduce_pieces(rows, places[NEAR_AT], stride, received).astype(BF)
     for k in range(out.shape[0]):
         out[k] = total
 
 
-def far_kernel(rows, stride, step, place, received, out, snapshot):
-    total = reduce_pieces(rows, place[0], stride, received)
+def far_kernel(rows, stride, step, places, received, out, snapshot):
+    total = reduce_pieces(rows, places[FAR_AT], stride, received)
     for k in range(R // 2):
         snapshot[2 * k:2 * k + 1, :] = step * total[rows + k:rows + k + 1, :W]
         snapshot[2 * k + 1:2 * k + 2, :] = step * total[rows + k:rows + k + 1, W:]
@@ -457,9 +465,14 @@
     forward = [(i, i + 1) for i in range(tiles - 1)]
     backward = [(i + 1, i) for i in range(tiles - 1)]
     place = lax.axis_index(SPACE)
-    inside = jnp.stack([place > 0, place < tiles - 1]).astype(F32)
+    odd = place % 2
+    places = jnp.stack([place > 0, place < tiles - 1, odd, frames * (1 - odd),
+                        frames * odd + lax.axis_index(TM), frames * odd,
+                        lax.axis_index(NEAR[1:]), lax.axis_index(FAR[1:])]).astype(jnp.int32)
 
     hbm = pl.BlockSpec(memory_space=pltpu.HBM)
+    whole = pl.BlockSpec(memory_space=pltpu.VMEM)
+    scalars = pl.BlockSpec(memory_space=pltpu.SMEM)
     edge = ((EDGE * C + FIELDS * R, LANES), BF)
     fields = ((4 * R, LANES), F32)
     frame = ((2, R, W), F32)
@@ -475,11 +488,10 @@
         stage_kernel,
         [((C, 3 * Q), BF), ((C, 3 * Q), BF), ((3 * C, 3 * C), BF), ((Q, C), BF),
          ((R * C, LANES), F32), ((R * C, LANES), BF), fields], [],
-        conv_first, conv_second, conv_third, own, own_fields,
+        places, conv_first, conv_second, conv_third, own, own_fields,
+        specs=[scalars] + [whole] * 5,
         cost=pl.CostEstimate(flops=2 * 10**6, bytes_accessed=10**6, transcendentals=0))
 
-    whole = pl.BlockSpec(memory_space=pltpu.VMEM)
-    scalars = pl.BlockSpec(memory_space=pltpu.SMEM)
     ext = ((EXT, LANES), F32)
     part, up, masks, base = call(
         functools.partial(unpack_kernel, step),
@@ -499,15 +511,15 @@
     gate2, back = call(
         early_kernel,
         [(((EXT - 2) * C, LANES), F32), (((EXT - 4) * C, LANES), F32)], [copies, d2],
-        inside, low, gate2_own, high, up, third_w, second_w,
-        specs=[scalars] + [whole] * 6,
+        places, low, gate2_own, high, up, third_w, second_w, sums,
+        specs=[scalars] + [whole] * 7,
         cost=pl.CostEstimate(flops=10**9, bytes_accessed=8 * 10**6, transcendentals=3 * 10**5))
     part, moved, gate1, hidden, inputs = call(
         functools.partial(first_kernel, step),
         wide_outs + [(((EXT - 4) * C, LANES), F32), ((R * C, LANES), BF),
                      (((R + 2) * Q, LANES), BF)],
         [copies, d1, taps],
-        inside, sums, up, masks, base, back, first_w, forward_w,
+        places, sums, up, masks, base, back, first_w, forward_w,
         specs=[scalars] + [whole] * 7)
     sums = exchange(part, TM)
 
@@ -518,17 +530,13 @@
     groups = [[t * tiles + (k + side) % tiles for side in range(2) for t in range(frames)]
               for k in range(1, tiles, 2)]
     received = lax.all_to_all(part, TM + SPACE, 0, 0, axis_index_groups=groups, tiled=True)
-    odd = place % 2
-    mine = frames * (1 - odd)
-    theirs = frames * odd
-    pair_place = jnp.stack([mine, theirs, theirs + lax.axis_index(TM), odd])
     field, = call(functools.partial(update_kernel, step), [((R, LANES), F32)], [],
-                  pair_place, received, moved, up, masks, specs=[scalars] + [whole] * 4)
+                  places, received, moved, up, masks, specs=[scalars] + [whole] * 4)
     near = lax.ppermute(field, SPACE, [(i, i ^ 1) for i in range(tiles)])
     part, moved = call(
         functools.partial(third_kernel, step), wide_outs, [copies, d2, d1, taps, ext],
-        inside, pair_place, received, field, near, up, masks, gate2, gate1, *weights,
-        specs=[scalars] * 2 + [whole] * 10)
+        places, received, field, near, up, masks, gate2, gate1, *weights,
+        specs=[scalars] + [whole] * 10)
     sums = exchange(part, TM)
 
     near_sizes = [lax.axis_size(name) for name in NEAR]
@@ -545,16 +553,14 @@
 
     received = exchange(grads, NEAR)
     near_stride = near_count // near_sizes[0]
-    near_place = lax.axis_index(NEAR[1:])[None]
     far_stride = far_count // far_sizes[0]
-    far_place = lax.axis_index(FAR[1:])[None]
     received, = call(
         functools.partial(near_kernel, rows, near_stride),
-        [((far_count, piece, LANES), BF)], [], near_place, received, specs=[scalars, whole])
+        [((far_count, piece, LANES), BF)], [], places, received, specs=[scalars, whole])
     received = exchange(received, FAR)
     received, snapshot = call(
         functools.partial(far_kernel, rows, far_stride, step),
-        [((near_count, piece, LANES), BF), ((R, W), F32)], [], far_place, received,
+        [((near_count, piece, LANES), BF), ((R, W), F32)], [], places, received,
         specs=[scalars, whole])
     received = exchange(received, NEAR)
     grad_first, grad_second, grad_third = call(

time: 138 us -> 134 us (0.971)
  blocking collectives: 55 us -> 105 us
  starting transfers between devices: 34.6 us -> 7.17 us
  waiting for transfers between devices: 25.1 us -> 2.58 us
  local copies, waits for them, and re-layouts: 7.43 us -> 4.08 us
    all_to_all x4 -> x6, blocking collectives: 55 us -> 86.2 us  [exchange(): return lax.all_to_all(value, axis, 0, 0, tiled=True)]
    all_to_all x3 -> x0, starting transfers between devices: 27.3 us -> none  [the longest x2 17.5 us: exchange(): return lax.all_to_all(value, axis, 0, 0, tiled=True)]
    all_to_all x3 -> x0, waiting for transfers between devices: 22.5 us -> none  [the longest x2 12.3 us: exchange(): return lax.all_to_all(value, axis, 0, 0, tiled=True)]
    all_to_all x0 -> x1, blocking collectives: none -> 19.1 us  [per_device(): lax.all_to_all(part, TM + SPACE, 0, 0, axis_index_groups=groups, tiled=True)]
    unnamed x30 -> x10, local copies, waits for them, and re-layouts: 7.43 us -> 3.99 us
  transfers between devices with their start and end apart: 6 -> 3, of which waited for: 5 -> 2; matrix products, arithmetic and copies ran while one was open for 0% -> 0% of each run, Pallas kernels for 2% -> 1%
where the time goes in v6:
time: 134 us
  blocking collectives  105 us (78%)
  Pallas kernels  13.9 us (10%)
  starting transfers between devices  7.17 us (5%)
  local copies, waits for them, and re-layouts  4.08 us (3%)
  waiting for transfers between devices  2.58 us (2%)
    all_to_all x6, blocking collectives, exchange(): return lax.all_to_all(value, axis, 0, 0, tiled=True)  86.2 us
    all_to_all x1, blocking collectives, per_device(): lax.all_to_all(part, TM + SPACE, 0, 0, axis_index_groups=groups, tiled=True)  19.1 us
    pallas_call x12, Pallas kernels, call(): pl.pallas_call(kernel, out_shape=[jax.ShapeDtypeStruct(shape, dtype) for...  13.9 us
    unnamed x10, local copies, waits for them, and re-layouts  3.99 us
    ppermute x1, starting transfers between devices, per_device(): low = lax.ppermute(bottom, SPACE, forward)  3.96 us
  transfers between devices with their start and end apart: 3, of which 2 were waited for; matrix products, arithmetic and copies ran while one was open for 0% of the time, Pallas kernels for 1%

profile of v6, /device:TPU:1, one launch (start us, length us, event | category | flops | bytes accessed | tf_op | source)
XLA Modules:
  0.0 133.8 jit_solution(3650716314872653551)
XLA Ops:
  0.6 1.9 %shard_map.119 = (bf16[512,256]{1,0:T(8,128)(2,1)}, bf16[368,256]{1,0:T(8,128)(2,1)}, bf16[368,256]{1,0:T(8,128)(2,1)}, f32[32,256]{1,0:T(8,128)}) custom-call(f32[2,8,128]{2,1,0:T(8,128)} %upstream.1, f32[2,8,128]{2,1,0:T(8,128)} %equilibrium.1, s32[2,8,128]{2,1,0:T(8,128)} %masks.1, f32[8,128]{1,0:T(8,128)} %measurement.1, bf16[2,64,8,128]{3,2,1,0:T(8,128)(2,1)} %saved.1), custom_call_target="tpu_custom_call" | custom-call | tf_op jit(solution)/shard_map/pallas_call | solution.py:437
  2.6 4.0 %collective-permute-start = (bf16[368,256]{1,0:T(8,128)(2,1)}, bf16[368,256]{1,0:T(8,128)(2,1)S(1)}, u32[]{:S(2)}, u32[]{:S(2)}) collective-permute-start(bf16[368,256]{1,0:T(8,128)(2,1)} %get-tuple-element.38), channel_id=1, source_target_pairs={{0,1},{1,2},{2,3},{3,4},{4,5},{5,6},{6,7},{7,8},{8,9},{9,10},{10,1... | collective-permute-start | bytes 565256 | tf_op jit(solution)/shard_map/ppermute | solution.py:484
  6.6 1.3 collective-permute-start.1
  7.9 0.1 stack.43._.places
  8.0 0.0 copy-start
  8.0 1.0 copy-done
  8.9 0.0 copy-start.1
  8.9 0.9 copy-done.1
  9.8 0.0 copy-start.2
  9.8 0.8 copy-done.2
  10.6 0.0 copy-start.3
  10.6 0.7 copy-done.3
  11.3 0.0 copy-start.4
  11.3 0.7 copy-done.4
  12.0 1.0 shard_map.120
  13.0 0.0 collective-permute-done.low
  13.0 0.1 collective-permute-done.1.high
  13.1 20.4 %all_to_all.35._.sums = f32[8,24,128]{2,1,0:T(8,128)S(1)} all-to-all(f32[8,24,128]{2,1,0:T(8,128)S(1)} %get-tuple-element.44), channel_id=1, replica_groups=mesh['zh'=4,'core'=2,'zl'=2,'y'=8,'x'=4] {'zh','core'}, dimensions={0} | all-to-all | bytes 196608 | tf_op jit(solution)/shard_map/all_to_all | solution.py:455
  33.6 1.6 %shard_map.122 = (f32[1152,256]{1,0:T(8,128)S(1)}, f32[1024,256]{1,0:T(8,128)S(1)}) custom-call(s32[8]{0:T(128)S(1)} %stack.43._.places, bf16[368,256]{1,0:T(8,128)(2,1)S(1)} %collective-permute-done.low, f32[512,256]{1,0:T(8,128)S(1)} %get-tuple-element.43._.own, bf16[368,256]{1,0:T(8,128)(2,1)S(1)} %collective-permute-done.1.high, ...), custom_call_target="tpu_custom_call" | custom-call | flops 1000000000 | bytes 8000000 | tf_op jit(solution)/shard_map/pallas_call | solution.py:437
  35.2 1.4 %shard_map.123 = (f32[8,16,128]{2,1,0:T(8,128)S(1)}, f32[14,256]{1,0:T(8,128)S(1)}, f32[1024,256]{1,0:T(8,128)S(1)}, bf16[512,256]{1,0:T(8,128)(2,1)S(1)}, bf16[160,256]{1,0:T(8,128)(2,1)S(1)}) custom-call(s32[8]{0:T(128)S(1)} %stack.43._.places, f32[8,24,128]{2,1,0:T(8,128)S(1)} %all_to_all.35._.sums, f32[20,256]{1,0:T(8,128)S(1)} %get-tuple-element.45.up, ...), custom_call_target="tpu_custom_call" | custom-call | tf_op jit(solution)/shard_map/pallas_call | solution.py:437
  36.6 10.9 %all_to_all.36.sums = f32[8,16,128]{2,1,0:T(8,128)S(1)} all-to-all(f32[8,16,128]{2,1,0:T(8,128)S(1)} %get-tuple-element.53), channel_id=1, replica_groups=mesh['zh'=4,'core'=2,'zl'=2,'y'=8,'x'=4] {'zh','core'}, dimensions={0} | all-to-all | bytes 131072 | tf_op jit(solution)/shard_map/all_to_all | solution.py:455
  47.5 1.1 shard_map.124
  48.5 19.1 %all_to_all.37.received = f32[16,12,256]{2,1,0:T(8,128)S(1)} all-to-all(f32[16,12,256]{2,1,0:T(8,128)S(1)} %get-tuple-element.57), channel_id=1, replica_groups={{1,65,129,193,257,321,385,449,2,66,130,194,258,322,386,450},{3,67,131,1..., dimensions={0} | all-to-all | bytes 393216 | tf_op jit(solution)/shard_map/all_to_all | solution.py:532
  67.6 0.6 shard_map.125.own
  68.2 1.9 %collective-permute-start.2 = (f32[8,256]{1,0:T(8,128)S(1)}, f32[8,256]{1,0:T(8,128)S(1)}, u32[]{:S(2)}, u32[]{:S(2)}) collective-permute-start(f32[8,256]{1,0:T(8,128)S(1)} %shard_map.125.own), channel_id=1, source_target_pairs={{0,1},{1,0},{2,3},{3,2},{4,5},{5,4},{6,7},{7,6},{8,9},{9,8},{10,11... | collective-permute-start | bytes 24584 | tf_op jit(solution)/shard_map/ppermute | solution.py:535
  70.1 2.5 %collective-permute-done.2.near = f32[8,256]{1,0:T(8,128)S(1)} collective-permute-done((f32[8,256]{1,0:T(8,128)S(1)}, f32[8,256]{1,0:T(8,128)S(1)}, u32[]{:S(2)}, u32[]{:S(2)}) %collective-permute-start.2) | collective-permute-done | bytes 8224 | tf_op jit(solution)/shard_map/ppermute | solution.py:535
  72.6 1.8 %shard_map.126 = (f32[8,16,128]{2,1,0:T(8,128)S(1)}, f32[14,256]{1,0:T(8,128)S(1)}) custom-call(s32[8]{0:T(128)S(1)} %stack.43._.places, f32[16,12,256]{2,1,0:T(8,128)S(1)} %all_to_all.37.received, f32[8,256]{1,0:T(8,128)S(1)} %shard_map.125.own, f32[8,256]{1,0:T(8,128)S(1)} %collective-permute-done.2.near, f32[20,256]{1,0:T(8,128)S(1)} %get-tuple-element.45.up, ...), custom_call_target="tpu_custom_call" | custom-call | tf_op jit(solution)/shard_map/pallas_call | solution.py:437
  74.4 11.4 %all_to_all.38.sums = f32[8,16,128]{2,1,0:T(8,128)S(1)} all-to-all(f32[8,16,128]{2,1,0:T(8,128)S(1)} %get-tuple-element.59), channel_id=1, replica_groups=mesh['zh'=4,'core'=2,'zl'=2,'y'=8,'x'=4] {'zh','core'}, dimensions={0} | all-to-all | bytes 131072 | tf_op jit(solution)/shard_map/all_to_all | solution.py:455
  85.8 1.9 %shard_map.127 = (f32[2,8,128]{2,1,0:T(8,128)}, bf16[16,16,256]{2,1,0:T(8,128)(2,1)S(1)}) custom-call(f32[8,16,128]{2,1,0:T(8,128)S(1)} %all_to_all.38.sums, f32[14,256]{1,0:T(8,128)S(1)} %get-tuple-element.60.moved, f32[20,256]{1,0:T(8,128)S(1)} %get-tuple-element.45.up, f32[20,256]{1,0:T(8,128)S(1)} %get-tuple-element.46.masks, ...), custom_call_target="tpu_custom_call" | custom-call | tf_op jit(solution)/shard_map/pallas_call | solution.py:437
  87.8 10.6 %all_to_all.39.received = bf16[16,16,256]{2,1,0:T(8,128)(2,1)S(1)} all-to-all(bf16[16,16,256]{2,1,0:T(8,128)(2,1)S(1)} %get-tuple-element.65), channel_id=1, replica_groups=mesh['zh'=4,'core'=2,'zl'=2,'y'=8,'x'=4] {'core','zl','x'}, dimensions={0} | all-to-all | bytes 262144 | tf_op jit(solution)/shard_map/all_to_all | solution.py:455
  98.4 0.6 shard_map.128
  99.0 20.8 %all_to_all.40.received = bf16[32,16,256]{2,1,0:T(8,128)(2,1)S(1)} all-to-all(bf16[32,16,256]{2,1,0:T(8,128)(2,1)S(1)} %shard_map.128), channel_id=1, replica_groups=mesh['zh'=4,'core'=2,'zl'=2,'y'=8,'x'=4] {'zh','y'}, dimensions={0} | all-to-all | bytes 524288 | tf_op jit(solution)/shard_map/all_to_all | solution.py:455
  119.8 1.2 shard_map.129
  121.0 12.0 %all_to_all.41.received = bf16[16,16,256]{2,1,0:T(8,128)(2,1)S(1)} all-to-all(bf16[16,16,256]{2,1,0:T(8,128)(2,1)S(1)} %get-tuple-element.67), channel_id=1, replica_groups=mesh['zh'=4,'core'=2,'zl'=2,'y'=8,'x'=4] {'core','zl','x'}, dimensions={0} | all-to-all | bytes 262144 | tf_op jit(solution)/shard_map/all_to_all | solution.py:455
  133.0 0.8 shard_map.130
  (1 shorter events, 0.0 us)
Async XLA Ops:
  2.6 10.4 %collective-permute-start = (bf16[368,256]{1,0:T(8,128)(2,1)}, bf16[368,256]{1,0:T(8,128)(2,1)S(1)}, u32[]{:S(2)}, u32[]{:S(2)}) collective-permute-start(bf16[368,256]{1,0:T(8,128)(2,1)} %get-tuple-element.38), channel_id=1, source_target_pairs={{0,1},{1,2},{2,3},{3,4},{4,5},{5,6},{6,7},{7,8},{8,9},{9,10},{10,1... | collective-permute-start | bytes 565256 | tf_op jit(solution)/shard_map/ppermute | solution.py:484
  6.6 6.5 %collective-permute-start.1 = (bf16[368,256]{1,0:T(8,128)(2,1)}, bf16[368,256]{1,0:T(8,128)(2,1)S(1)}, u32[]{:S(2)}, u32[]{:S(2)}) collective-permute-start(bf16[368,256]{1,0:T(8,128)(2,1)} %get-tuple-element.42), channel_id=1, source_target_pairs={{1,0},{2,1},{3,2},{4,3},{5,4},{6,5},{7,6},{8,7},{9,8},{10,9},{11,1... | collective-permute-start | bytes 565256 | tf_op jit(solution)/shard_map/ppermute | solution.py:485
  8.0 1.0 copy-start
  8.9 0.9 copy-start.1
  9.8 0.8 copy-start.2
  10.6 0.7 copy-start.3
  11.3 0.7 copy-start.4
  68.2 4.4 %collective-permute-start.2 = (f32[8,256]{1,0:T(8,128)S(1)}, f32[8,256]{1,0:T(8,128)S(1)}, u32[]{:S(2)}, u32[]{:S(2)}) collective-permute-start(f32[8,256]{1,0:T(8,128)S(1)} %shard_map.125.own), channel_id=1, source_target_pairs={{0,1},{1,0},{2,3},{3,2},{4,5},{5,4},{6,7},{7,6},{8,9},{9,8},{10,11... | collective-permute-start | bytes 24584 | tf_op jit(solution)/shard_map/ppermute | solution.py:535

commit v7 on v6

--- a/solution.py
+++ b/solution.py
@@ -137,7 +137,7 @@
     return total
 
 
-def pack_kernel(upstream, equilibrium, masks, measurement, saved, out, top, bottom, own_fields,
+def pack_kernel(upstream, equilibrium, masks, measurement, saved, top, bottom, own_fields,
                 up_in, fixed_in, masks_in, snapshot_in, saved_in, sems):
     copies = [
         pltpu.make_async_copy(source, target, sems.at[k])
@@ -170,19 +170,21 @@
     for frame in range(2):
         lanes = slice(frame * W, (frame + 1) * W)
         rows = jnp.swapaxes(saved_in[frame].astype(F32), 0, 1).astype(BF).reshape(R * C, W)
-        out[:, lanes] = rows
         top[:EDGE * C, lanes] = rows[:EDGE * C]
         bottom[:EDGE * C, lanes] = rows[(R - EDGE) * C:]
 
 
-def stage_kernel(_, first, second, third, saved, own_fields, forward_w, third_w, second_w, first_w,
-                 gate2, hidden2, fields):
+def stage_kernel(places, first, second, third, saved, own_fields, forward_w, third_w, second_w,
+                 first_w, gate2, hidden2, fields, table):
     fields[...] = own_fields[...]
-    for r in range(R):
-        value = saved_row(saved, r).astype(F32)
+    for k in range(8):
+        table[k:k + 1, :] = jnp.full((1, W), places[k], jnp.int32)
+    for frame in range(2):
+        lanes = slice(frame * W, (frame + 1) * W)
+        value = jnp.swapaxes(saved[frame].astype(F32), 0, 1).reshape(R * C, W)
         logistic, slope = slope_parts(value)
-        gate2[r * C:(r + 1) * C, :] = slope
-        hidden2[r * C:(r + 1) * C, :] = (value * logistic).astype(BF)
+        gate2[:, lanes] = slope
+        hidden2[:, lanes] = (value * logistic).astype(BF)
     forward = first[...].astype(F32)
     backward = third[...].astype(F32)
     pad = jnp.zeros((Q - 6, C), F32)
@@ -234,12 +236,12 @@
 
 
 def ends(places):
-    return places[BEFORE].astype(F32), places[AFTER].astype(F32)
-
-
-def early_kernel(places, low, own, high, up, third_w, second_w, _, gate2, back, copies, d2):
+    return tuple(twice(places[k:k + 1, :]).astype(F32) for k in (BEFORE, AFTER))
+
+
+def first_kernel(step, places, sums, low, own, high, up, masks, base, third_w, second_w, first_w,
+                 forward_w, part, moved, gate2, gate1, hidden, inputs, copies, d2, d1, taps):
     before, after = ends(places)
-    copies[...] = jnp.zeros_like(copies)
     for k in range(EXT - 2):
         at = k + 1
         if HALO <= at < HALO + R:
@@ -248,13 +250,6 @@
             value = saved_row(low, k) if at < HALO else saved_row(high, at - HALO - R)
             slope = slope_parts(value.astype(F32))[1]
             gate2[k * C:(k + 1) * C, :] = keep_row(slope, at, before, after)
-    for k, total in back_rows(0, up[...], gate2, third_w[...], second_w[...], copies, d2):
-        back[k * C:(k + 1) * C, :] = total
-
-
-def first_kernel(step, places, sums, up, masks, base, back, first_w, forward_w,
-                 part, moved, gate1, hidden, inputs, copies, d1, taps):
-    before, after = ends(places)
     frame_sum = gathered_sum(sums)[:EXT]
     denoiser_input = base[...] - step * masks[...] * twice(frame_sum)
     copies[...] = jnp.zeros_like(copies)
@@ -264,13 +259,12 @@
         at = k + 2
         value = dot(forward_w[...], take_rows(copies, (at - 1) * Q, (at + 2) * Q).astype(BF))
         logistic, slope = slope_parts(value)
-        slope = keep_row(slope, at, before, after)
-        gate1[k * C:(k + 1) * C, :] = slope
+        gate1[k * C:(k + 1) * C, :] = keep_row(slope, at, before, after)
         if HALO <= at < HALO + R:
             own_at = at - HALO
             hidden[own_at * C:(own_at + 1) * C, :] = (value * logistic).astype(BF)
-        d1[k * C:(k + 1) * C, :] = (slope * back[k * C:(k + 1) * C, :]).astype(BF)
-    field = map_end(0, up[...], first_w[...], d1, taps)
+    field = adjoint_map(0, up[...], gate2, gate1, third_w[...], second_w[...], first_w[...],
+                        copies, d2, d1, taps)
     finish_wide(field, before, after, masks, part, moved)
 
 
@@ -315,7 +309,7 @@
 
 
 def update_kernel(step, places, received, moved, up, masks, out):
-    totals = pair_total(received, places[OWN_HALF])
+    totals = pair_total(received, places[OWN_HALF, 0])
     out[...] = (up[HALO:HALO + R, :] + moved[...]
                 - step * masks[HALO:HALO + R, :] * twice(totals))
 
@@ -324,14 +318,14 @@
                  second_w, first_w, part, moved, copies, d2, d1, taps, whole):
     copies[...] = jnp.zeros_like(copies)
     before, after = ends(places)
-    totals = twice(pair_total(received, places[THEIR_HALF]))
-    theirs = received[places[THEIR_ENTRY], 0:R, :]
+    totals = twice(pair_total(received, places[THEIR_HALF, 0]))
+    theirs = received[places[THEIR_ENTRY, 0], 0:R, :]
     after_rows = slice(HALO + R, EXT)
     low = (up[0:HALO, :] + theirs[R - HALO:]
            - step * masks[0:HALO, :] * totals[R - HALO:]) * before
     high = (up[after_rows, :] + theirs[:HALO]
             - step * masks[after_rows, :] * totals[:HALO]) * after
-    odd = places[ODD] == 1
+    odd = twice(places[ODD:ODD + 1, :]) == 1
     whole[0:HALO, :] = jnp.where(odd, near[R - HALO:, :], low)
     whole[HALO:HALO + R, :] = own[...]
     whole[HALO + R:, :] = jnp.where(odd, high, near[:HALO, :])
@@ -399,13 +393,13 @@
 
 
 def near_kernel(rows, stride, places, received, out):
-    total = reduce_pieces(rows, places[NEAR_AT], stride, received).astype(BF)
+    total = reduce_pieces(rows, places[NEAR_AT, 0], stride, received).astype(BF)
     for k in range(out.shape[0]):
         out[k] = total
 
 
 def far_kernel(rows, stride, step, places, received, out, snapshot):
-    total = reduce_pieces(rows, places[FAR_AT], stride, received)
+    total = reduce_pieces(rows, places[FAR_AT, 0], stride, received)
     for k in range(R // 2):
         snapshot[2 * k:2 * k + 1, :] = step * total[rows + k:rows + k + 1, :W]
         snapshot[2 * k + 1:2 * k + 2, :] = step * total[rows + k:rows + k + 1, W:]
@@ -476,19 +470,19 @@
     edge = ((EDGE * C + FIELDS * R, LANES), BF)
     fields = ((4 * R, LANES), F32)
     frame = ((2, R, W), F32)
-    own, top, bottom, own_fields = call(
-        pack_kernel, [((R * C, LANES), BF), edge, edge, fields],
+    top, bottom, own_fields = call(
+        pack_kernel, [edge, edge, fields],
         [frame, frame, ((2, R, W), jnp.int32), ((R, W), F32), ((2, C, R, W), BF)],
         upstream, equilibrium, coding_masks, measurement, saved_second,
         specs=[hbm] * 5, sems=5, limit=60)
     low = lax.ppermute(bottom, SPACE, forward)
     high = lax.ppermute(top, SPACE, backward)
 
-    forward_w, third_w, second_w, first_w, gate2_own, hidden2, own_fields = call(
+    forward_w, third_w, second_w, first_w, gate2_own, hidden2, own_fields, table = call(
         stage_kernel,
         [((C, 3 * Q), BF), ((C, 3 * Q), BF), ((3 * C, 3 * C), BF), ((Q, C), BF),
-         ((R * C, LANES), F32), ((R * C, LANES), BF), fields], [],
-        places, conv_first, conv_second, conv_third, own, own_fields,
+         ((R * C, LANES), F32), ((R * C, LANES), BF), fields, ((8, W), jnp.int32)], [],
+        places, conv_first, conv_second, conv_third, saved_second, own_fields,
         specs=[scalars] + [whole] * 5,
         cost=pl.CostEstimate(flops=2 * 10**6, bytes_accessed=10**6, transcendentals=0))
 
@@ -508,19 +502,12 @@
     slim_scratch = [((2, narrow * Q, W), F32), (((narrow - 2) * C, LANES), BF),
                     (((narrow - 4) * C, LANES), BF), ((2, (narrow - 4) * Q, W), F32)]
     wide_outs = [((frames, 16, W), F32), ((narrow, LANES), F32)]
-    gate2, back = call(
-        early_kernel,
-        [(((EXT - 2) * C, LANES), F32), (((EXT - 4) * C, LANES), F32)], [copies, d2],
-        places, low, gate2_own, high, up, third_w, second_w, sums,
-        specs=[scalars] + [whole] * 7,
-        cost=pl.CostEstimate(flops=10**9, bytes_accessed=8 * 10**6, transcendentals=3 * 10**5))
-    part, moved, gate1, hidden, inputs = call(
+    part, moved, gate2, gate1, hidden, inputs = call(
         functools.partial(first_kernel, step),
-        wide_outs + [(((EXT - 4) * C, LANES), F32), ((R * C, LANES), BF),
-                     (((R + 2) * Q, LANES), BF)],
-        [copies, d1, taps],
-        places, sums, up, masks, base, back, first_w, forward_w,
-        specs=[scalars] + [whole] * 7)
+        wide_outs + [(((EXT - 2) * C, LANES), F32), (((EXT - 4) * C, LANES), F32),
+                     ((R * C, LANES), BF), (((R + 2) * Q, LANES), BF)],
+        [copies, d2, d1, taps],
+        table, sums, low, gate2_own, high, up, masks, base, *weights, forward_w)
     sums = exchange(part, TM)
 
     part, moved = call(
@@ -531,12 +518,11 @@
               for k in range(1, tiles, 2)]
     received = lax.all_to_all(part, TM + SPACE, 0, 0, axis_index_groups=groups, tiled=True)
     field, = call(functools.partial(update_kernel, step), [((R, LANES), F32)], [],
-                  places, received, moved, up, masks, specs=[scalars] + [whole] * 4)
+                  table, received, moved, up, masks)
     near = lax.ppermute(field, SPACE, [(i, i ^ 1) for i in range(tiles)])
     part, moved = call(
         functools.partial(third_kernel, step), wide_outs, [copies, d2, d1, taps, ext],
-        places, received, field, near, up, masks, gate2, gate1, *weights,
-        specs=[scalars] + [whole] * 10)
+        table, received, field, near, up, masks, gate2, gate1, *weights)
     sums = exchange(part, TM)
 
     near_sizes = [lax.axis_size(name) for name in NEAR]
@@ -556,12 +542,11 @@
     far_stride = far_count // far_sizes[0]
     received, = call(
         functools.partial(near_kernel, rows, near_stride),
-        [((far_count, piece, LANES), BF)], [], places, received, specs=[scalars, whole])
+        [((far_count, piece, LANES), BF)], [], table, received)
     received = exchange(received, FAR)
     received, snapshot = call(
         functools.partial(far_kernel, rows, far_stride, step),
-        [((near_count, piece, LANES), BF), ((R, W), F32)], [], places, received,
-        specs=[scalars, whole])
+        [((near_count, piece, LANES), BF), ((R, W), F32)], [], table, received)
     received = exchange(received, NEAR)
     grad_first, grad_second, grad_third = call(
         functools.partial(output_kernel, scale),

time: 134 us -> 131 us (0.978)
  Pallas kernels: 13.9 us -> 10.7 us
    pallas_call x12 -> x11, Pallas kernels: 13.9 us -> 10.7 us  [call(): pl.pallas_call(kernel, out_shape=[jax.ShapeDtypeStruct(shape, dtype) for...]
  transfers between devices with their start and end apart: 3 -> 3, of which waited for: 2 -> 1; matrix products, arithmetic and copies ran while one was open for 0% -> 0% of each run, Pallas kernels for 1% -> 1%
where the time goes in v7:
time: 131 us; the launch traced here: 130 us
  blocking collectives  105 us (80%)
  Pallas kernels  10.7 us (8%)
  starting transfers between devices  7.17 us (5%)
  local copies, waits for them, and re-layouts  4.08 us (3%)
  waiting for transfers between devices  2.47 us (2%)
    all_to_all x6, blocking collectives, exchange(): return lax.all_to_all(value, axis, 0, 0, tiled=True)  86.1 us
    all_to_all x1, blocking collectives, per_device(): lax.all_to_all(part, TM + SPACE, 0, 0, axis_index_groups=groups, tiled=True)  19.1 us
    pallas_call x11, Pallas kernels, call(): pl.pallas_call(kernel, out_shape=[jax.ShapeDtypeStruct(shape, dtype) for...  10.7 us
    unnamed x10, local copies, waits for them, and re-layouts  3.99 us
    ppermute x1, starting transfers between devices, per_device(): low = lax.ppermute(bottom, SPACE, forward)  3.96 us
  transfers between devices with their start and end apart: 3, of which 1 were waited for; matrix products, arithmetic and copies ran while one was open for 0% of the time, Pallas kernels for 1%

profile of v7, /device:TPU:1, one launch (start us, length us, event | category | flops | bytes accessed | tf_op | source)
XLA Modules:
  0.0 130.4 jit_solution(11636818377196989784)
XLA Ops:
  0.6 1.9 %shard_map.119 = (bf16[368,256]{1,0:T(8,128)(2,1)}, bf16[368,256]{1,0:T(8,128)(2,1)}, f32[32,256]{1,0:T(8,128)}) custom-call(f32[2,8,128]{2,1,0:T(8,128)} %upstream.1, f32[2,8,128]{2,1,0:T(8,128)} %equilibrium.1, s32[2,8,128]{2,1,0:T(8,128)} %masks.1, f32[8,128]{1,0:T(8,128)} %measurement.1, bf16[2,64,8,128]{3,2,1,0:T(8,128)(2,1)} %saved.3), custom_call_target="tpu_custom_call" | custom-call | tf_op jit(solution)/shard_map/pallas_call | solution.py:431
  2.5 4.0 %collective-permute-start = (bf16[368,256]{1,0:T(8,128)(2,1)}, bf16[368,256]{1,0:T(8,128)(2,1)S(1)}, u32[]{:S(2)}, u32[]{:S(2)}) collective-permute-start(bf16[368,256]{1,0:T(8,128)(2,1)} %get-tuple-element.39), channel_id=1, source_target_pairs={{0,1},{1,2},{2,3},{3,4},{4,5},{5,6},{6,7},{7,8},{8,9},{9,10},{10,1... | collective-permute-start | bytes 565256 | tf_op jit(solution)/shard_map/ppermute | solution.py:478
  6.5 1.3 collective-permute-start.1
  7.8 0.1 stack.43.places
  7.9 0.0 copy-start
  7.9 1.0 copy-done
  8.8 0.0 copy-start.1
  8.8 0.9 copy-done.1
  9.7 0.0 copy-start.2
  9.7 0.8 copy-done.2
  10.5 0.0 copy-start.3
  10.5 0.7 copy-done.3
  11.2 0.0 copy-start.4
  11.2 0.7 copy-done.4
  11.9 1.1 shard_map.120
  13.0 0.0 collective-permute-done.low
  13.0 0.0 collective-permute-done.1.high
  13.1 20.4 %all_to_all.35.sums = f32[8,24,128]{2,1,0:T(8,128)S(1)} all-to-all(f32[8,24,128]{2,1,0:T(8,128)S(1)} %get-tuple-element.43), channel_id=1, replica_groups=mesh['zh'=4,'core'=2,'zl'=2,'y'=8,'x'=4] {'zh','core'}, dimensions={0} | all-to-all | bytes 196608 | tf_op jit(solution)/shard_map/all_to_all | solution.py:449
  33.5 1.8 %shard_map.122 = (f32[8,16,128]{2,1,0:T(8,128)S(1)}, f32[14,256]{1,0:T(8,128)S(1)}, f32[1152,256]{1,0:T(8,128)S(1)}, f32[1024,256]{1,0:T(8,128)S(1)}, bf16[512,2...) custom-call(s32[8,128]{1,0:T(8,128)S(1)} %get-tuple-element.38.places, f32[8,24,128]{2,1,0:T(8,128)S(1)} %all_to_all.35.sums, ...), custom_call_target="tpu_custom_call" | custom-call | tf_op jit(solution)/shard_map/pallas_call | solution.py:431
  35.3 10.9 %all_to_all.36.sums = f32[8,16,128]{2,1,0:T(8,128)S(1)} all-to-all(f32[8,16,128]{2,1,0:T(8,128)S(1)} %get-tuple-element.51), channel_id=1, replica_groups=mesh['zh'=4,'core'=2,'zl'=2,'y'=8,'x'=4] {'zh','core'}, dimensions={0} | all-to-all | bytes 131072 | tf_op jit(solution)/shard_map/all_to_all | solution.py:449
  46.2 1.1 shard_map.123
  47.2 19.1 %all_to_all.37.received = f32[16,12,256]{2,1,0:T(8,128)S(1)} all-to-all(f32[16,12,256]{2,1,0:T(8,128)S(1)} %get-tuple-element.55), channel_id=1, replica_groups={{1,65,129,193,257,321,385,449,2,66,130,194,258,322,386,450},{3,67,131,1..., dimensions={0} | all-to-all | bytes 393216 | tf_op jit(solution)/shard_map/all_to_all | solution.py:519
  66.4 0.1 shard_map.124.own
  66.4 1.9 %collective-permute-start.2 = (f32[8,256]{1,0:T(8,128)S(1)}, f32[8,256]{1,0:T(8,128)S(1)}, u32[]{:S(2)}, u32[]{:S(2)}) collective-permute-start(f32[8,256]{1,0:T(8,128)S(1)} %shard_map.124.own), channel_id=1, source_target_pairs={{0,1},{1,0},{2,3},{3,2},{4,5},{5,4},{6,7},{7,6},{8,9},{9,8},{10,11... | collective-permute-start | bytes 24584 | tf_op jit(solution)/shard_map/ppermute | solution.py:522
  68.3 2.5 %collective-permute-done.2.near = f32[8,256]{1,0:T(8,128)S(1)} collective-permute-done((f32[8,256]{1,0:T(8,128)S(1)}, f32[8,256]{1,0:T(8,128)S(1)}, u32[]{:S(2)}, u32[]{:S(2)}) %collective-permute-start.2) | collective-permute-done | bytes 8224 | tf_op jit(solution)/shard_map/ppermute | solution.py:522
  70.8 1.3 shard_map.125
  72.1 11.8 %all_to_all.38.sums = f32[8,16,128]{2,1,0:T(8,128)S(1)} all-to-all(f32[8,16,128]{2,1,0:T(8,128)S(1)} %get-tuple-element.57), channel_id=1, replica_groups=mesh['zh'=4,'core'=2,'zl'=2,'y'=8,'x'=4] {'zh','core'}, dimensions={0} | all-to-all | bytes 131072 | tf_op jit(solution)/shard_map/all_to_all | solution.py:449
  83.9 1.9 %shard_map.126 = (f32[2,8,128]{2,1,0:T(8,128)}, bf16[16,16,256]{2,1,0:T(8,128)(2,1)S(1)}) custom-call(f32[8,16,128]{2,1,0:T(8,128)S(1)} %all_to_all.38.sums, f32[14,256]{1,0:T(8,128)S(1)} %get-tuple-element.58.moved, f32[20,256]{1,0:T(8,128)S(1)} %get-tuple-element.44.up, f32[20,256]{1,0:T(8,128)S(1)} %get-tuple-element.45.masks, ...), custom_call_target="tpu_custom_call" | custom-call | tf_op jit(solution)/shard_map/pallas_call | solution.py:431
  85.9 10.3 %all_to_all.39.received = bf16[16,16,256]{2,1,0:T(8,128)(2,1)S(1)} all-to-all(bf16[16,16,256]{2,1,0:T(8,128)(2,1)S(1)} %get-tuple-element.63), channel_id=1, replica_groups=mesh['zh'=4,'core'=2,'zl'=2,'y'=8,'x'=4] {'core','zl','x'}, dimensions={0} | all-to-all | bytes 262144 | tf_op jit(solution)/shard_map/all_to_all | solution.py:449
  96.2 20.8 %all_to_all.40.received = bf16[32,16,256]{2,1,0:T(8,128)(2,1)S(1)} all-to-all(bf16[32,16,256]{2,1,0:T(8,128)(2,1)S(1)} %shard_map.127), channel_id=1, replica_groups=mesh['zh'=4,'core'=2,'zl'=2,'y'=8,'x'=4] {'zh','y'}, dimensions={0} | all-to-all | bytes 524288 | tf_op jit(solution)/shard_map/all_to_all | solution.py:449
  117.0 0.6 shard_map.128
  117.6 12.0 %all_to_all.41.received = bf16[16,16,256]{2,1,0:T(8,128)(2,1)S(1)} all-to-all(bf16[16,16,256]{2,1,0:T(8,128)(2,1)S(1)} %get-tuple-element.65), channel_id=1, replica_groups=mesh['zh'=4,'core'=2,'zl'=2,'y'=8,'x'=4] {'core','zl','x'}, dimensions={0} | all-to-all | bytes 262144 | tf_op jit(solution)/shard_map/all_to_all | solution.py:449
  129.6 0.8 shard_map.129
  (2 shorter events, 0.1 us)
Async XLA Ops:
  2.5 10.5 %collective-permute-start = (bf16[368,256]{1,0:T(8,128)(2,1)}, bf16[368,256]{1,0:T(8,128)(2,1)S(1)}, u32[]{:S(2)}, u32[]{:S(2)}) collective-permute-start(bf16[368,256]{1,0:T(8,128)(2,1)} %get-tuple-element.39), channel_id=1, source_target_pairs={{0,1},{1,2},{2,3},{3,4},{4,5},{5,6},{6,7},{7,8},{8,9},{9,10},{10,1... | collective-permute-start | bytes 565256 | tf_op jit(solution)/shard_map/ppermute | solution.py:478
  6.5 6.6 %collective-permute-start.1 = (bf16[368,256]{1,0:T(8,128)(2,1)}, bf16[368,256]{1,0:T(8,128)(2,1)S(1)}, u32[]{:S(2)}, u32[]{:S(2)}) collective-permute-start(bf16[368,256]{1,0:T(8,128)(2,1)} %get-tuple-element.41), channel_id=1, source_target_pairs={{1,0},{2,1},{3,2},{4,3},{5,4},{6,5},{7,6},{8,7},{9,8},{10,9},{11,1... | collective-permute-start | bytes 565256 | tf_op jit(solution)/shard_map/ppermute | solution.py:479
  7.9 1.0 copy-start
  8.8 0.9 copy-start.1
  9.7 0.8 copy-start.2
  10.5 0.7 copy-start.3
  11.2 0.7 copy-start.4
  66.4 4.4 %collective-permute-start.2 = (f32[8,256]{1,0:T(8,128)S(1)}, f32[8,256]{1,0:T(8,128)S(1)}, u32[]{:S(2)}, u32[]{:S(2)}) collective-permute-start(f32[8,256]{1,0:T(8,128)S(1)} %shard_map.124.own), channel_id=1, source_target_pairs={{0,1},{1,0},{2,3},{3,2},{4,5},{5,4},{6,7},{7,6},{8,9},{9,8},{10,11... | collective-permute-start | bytes 24584 | tf_op jit(solution)/shard_map/ppermute | solution.py:522

commit v8 on v7

--- a/solution.py
+++ b/solution.py
@@ -131,23 +131,30 @@
 
 
 def gathered_sum(ref):
-    total = ref[0]
+    total = ref[0].astype(F32)
     for k in range(1, ref.shape[0]):
-        total = total + ref[k]
+        total = total + ref[k].astype(F32)
     return total
 
 
+def send_all(part, value):
+    fill = jnp.zeros((part.shape[1] - value.shape[0], value.shape[1]), F32)
+    value = jnp.concatenate([value, fill], axis=0).astype(part.dtype)
+    for k in range(part.shape[0]):
+        part[k] = value
+
+
 def pack_kernel(upstream, equilibrium, masks, measurement, saved, top, bottom, own_fields,
-                up_in, fixed_in, masks_in, snapshot_in, saved_in, sems):
-    copies = [
+                up_in, fixed_in, masks_in, snapshot_in, saved_in, top_out, bottom_out, sems):
+    arrivals = [
         pltpu.make_async_copy(source, target, sems.at[k])
         for k, (source, target) in enumerate((
-            (saved, saved_in), (upstream, up_in), (equilibrium, fixed_in), (masks, masks_in),
-            (measurement, snapshot_in)))
+            (saved.at[0], saved_in.at[0]), (saved.at[1], saved_in.at[1]), (upstream, up_in),
+            (equilibrium, fixed_in), (masks, masks_in), (measurement, snapshot_in)))
     ]
-    for copy in copies:
+    for copy in arrivals:
         copy.start()
-    for copy in copies[1:]:
+    for copy in arrivals[2:]:
         copy.wait()
 
     def by_frame(ref):
@@ -164,14 +171,22 @@
     for k in range(0, len(fields), 2):
         pair = jnp.concatenate([field.astype(F32) for field in fields[k:k + 2]], axis=0).astype(BF)
         at = EDGE * C + k * R
-        top[at:at + 2 * R, :] = pair
-        bottom[at:at + 2 * R, :] = pair
-    copies[0].wait()
+        top_out[at:at + 2 * R, :] = pair
+        bottom_out[at:at + 2 * R, :] = pair
+    departures = []
     for frame in range(2):
         lanes = slice(frame * W, (frame + 1) * W)
+        arrivals[frame].wait()
         rows = jnp.swapaxes(saved_in[frame].astype(F32), 0, 1).astype(BF).reshape(R * C, W)
-        top[:EDGE * C, lanes] = rows[:EDGE * C]
-        bottom[:EDGE * C, lanes] = rows[(R - EDGE) * C:]
+        for value, here, there in ((rows[:EDGE * C], top_out, top),
+                                   (rows[(R - EDGE) * C:], bottom_out, bottom)):
+            here[:EDGE * C, lanes] = value
+            copy = pltpu.make_async_copy(here.at[:, lanes], there.at[:, lanes],
+                                         sems.at[len(arrivals) + len(departures)])
+            copy.start()
+            departures.append(copy)
+    for copy in departures:
+        copy.wait()
 
 
 def stage_kernel(places, first, second, third, saved, own_fields, forward_w, third_w, second_w,
@@ -216,10 +231,7 @@
                               (masks, field(4)),
                               (snapshot, twice(field(5)[:, :W] + field(5)[:, W:]))):
             target[at:at + HALO, :] = value[first:first + HALO]
-    total = masked_sum(masks[...], fixed[...])
-    for k in range(part.shape[0]):
-        part[k, 0:EXT, :] = total
-        part[k, EXT:, :] = jnp.zeros((part.shape[1] - EXT, W), F32)
+    send_all(part, masked_sum(masks[...], fixed[...]))
     base[...] = fixed[...] + step * masks[...] * snapshot[...]
 
 
@@ -274,10 +286,7 @@
     keep = jnp.where(row < HALO - 3, before, jnp.where(row >= HALO - 3 + R, after, 1.0))
     field = field * keep
     moved[...] = field
-    total = masked_sum(masks[3:3 + count, :], field)
-    for k in range(part.shape[0]):
-        part[k, 0:count, :] = total
-        part[k, count:, :] = jnp.zeros((part.shape[1] - count, W), F32)
+    send_all(part, masked_sum(masks[3:3 + count, :], field))
 
 
 def narrow_field(step, sums, moved, up, masks):
@@ -295,16 +304,15 @@
     out[...] = result
     total = masked_sum(masks[HALO:HALO + R, :], result)
     half = jnp.concatenate([total[:R // 2], total[R // 2:]], axis=1)
-    for k in range(part.shape[0]):
-        part[k, 0:R, :] = result
-        part[k, R:, :] = half
+    send_all(part, jnp.concatenate([result, half], axis=0))
 
 
 def pair_total(received, first):
     count = received.shape[0] // 2
-    half = received[first, R:, :]
+    half = received[first].astype(F32)
     for k in range(1, count):
-        half = half + received[first + k, R:, :]
+        half = half + received[first + k].astype(F32)
+    half = half[R:R + R // 2]
     return jnp.concatenate([half[:, :W], half[:, W:]], axis=0)
 
 
@@ -319,7 +327,7 @@
     copies[...] = jnp.zeros_like(copies)
     before, after = ends(places)
     totals = twice(pair_total(received, places[THEIR_HALF, 0]))
-    theirs = received[places[THEIR_ENTRY, 0], 0:R, :]
+    theirs = received[places[THEIR_ENTRY, 0]].astype(F32)[:R]
     after_rows = slice(HALO + R, EXT)
     low = (up[0:HALO, :] + theirs[R - HALO:]
            - step * masks[0:HALO, :] * totals[R - HALO:]) * before
@@ -338,8 +346,7 @@
                 second_w, first_w, adjoint, grads, copies, d2, d1, taps, total):
     copies[...] = jnp.zeros_like(copies)
     field = narrow_field(step, sums, moved, up, masks)
-    adjoint[0] = field[3:3 + R, :W]
-    adjoint[1] = field[3:3 + R, W:]
+    adjoint[...] = field[3:3 + R]
     result = adjoint_map(3, field, gate2, gate1, third_w[...], second_w[...], first_w[...],
                          copies, d2, d1, taps)
     snapshot = masked_sum(masks[HALO:HALO + R, :], result)
@@ -408,7 +415,10 @@
         out[k] = total
 
 
-def output_kernel(scale, received, first, second, third, total):
+def output_kernel(scale, received, field, sums, adjoint, snapshot, first, second, third, total):
+    adjoint[0] = field[:, :W]
+    adjoint[1] = field[:, W:]
+    snapshot[...] = sums[...]
     count = received.shape[0]
     rows = 3 * C // count
     for k in range(count):
@@ -425,14 +435,15 @@
             third[tap:tap + 1, :] = total[at:at + 1, 3 * C:] + total[at + 3:at + 4, 3 * C:]
 
 
-def call(kernel, outs, scratch, *operands, specs=None, cost=None, sems=0, limit=40):
+def call(kernel, outs, scratch, *operands, specs=None, cost=None, sems=0, limit=40,
+         out_specs=None):
     if specs is None:
         specs = [pl.BlockSpec(memory_space=pltpu.VMEM)] * len(operands)
     return pl.pallas_call(
         kernel,
         out_shape=[jax.ShapeDtypeStruct(shape, dtype) for shape, dtype in outs],
         in_specs=specs,
-        out_specs=[pl.BlockSpec(memory_space=pltpu.VMEM)] * len(outs),
+        out_specs=out_specs or [pl.BlockSpec(memory_space=pltpu.VMEM)] * len(outs),
         scratch_shapes=[pltpu.VMEM(shape, dtype) for shape, dtype in scratch]
         + [pltpu.SemaphoreType.DMA((sems,))] * (sems > 0),
         compiler_params=pltpu.CompilerParams(vmem_limit_bytes=limit * 2**20),
@@ -472,9 +483,9 @@
     frame = ((2, R, W), F32)
     top, bottom, own_fields = call(
         pack_kernel, [edge, edge, fields],
-        [frame, frame, ((2, R, W), jnp.int32), ((R, W), F32), ((2, C, R, W), BF)],
+        [frame, frame, ((2, R, W), jnp.int32), ((R, W), F32), ((2, C, R, W), BF), edge, edge],
         upstream, equilibrium, coding_masks, measurement, saved_second,
-        specs=[hbm] * 5, sems=5, limit=60)
+        specs=[hbm] * 5, out_specs=[hbm, hbm, whole], sems=10, limit=60)
     low = lax.ppermute(bottom, SPACE, forward)
     high = lax.ppermute(top, SPACE, backward)
 
@@ -489,7 +500,7 @@
     ext = ((EXT, LANES), F32)
     part, up, masks, base = call(
         functools.partial(unpack_kernel, step),
-        [((frames, 24, W), F32), ext, ext, ext], [ext, ext],
+        [((frames, 32, W), BF), ext, ext, ext], [ext, ext],
         low, own_fields, high, gate2_own)
     sums = exchange(part, TM)
 
@@ -501,7 +512,7 @@
     taps = ((2, (EXT - 4) * Q, W), F32)
     slim_scratch = [((2, narrow * Q, W), F32), (((narrow - 2) * C, LANES), BF),
                     (((narrow - 4) * C, LANES), BF), ((2, (narrow - 4) * Q, W), F32)]
-    wide_outs = [((frames, 16, W), F32), ((narrow, LANES), F32)]
+    wide_outs = [((frames, 16, W), BF), ((narrow, LANES), F32)]
     part, moved, gate2, gate1, hidden, inputs = call(
         functools.partial(first_kernel, step),
         wide_outs + [(((EXT - 2) * C, LANES), F32), (((EXT - 4) * C, LANES), F32),
@@ -512,7 +523,7 @@
 
     part, moved = call(
         functools.partial(second_kernel, step),
-        [((2 * frames, R + R // 2, LANES), F32), ((R, LANES), F32)], slim_scratch,
+        [((2 * frames, 2 * R, LANES), BF), ((R, LANES), F32)], slim_scratch,
         sums, moved, up, masks, gate2, gate1, *weights)
     groups = [[t * tiles + (k + side) % tiles for side in range(2) for t in range(frames)]
               for k in range(1, tiles, 2)]
@@ -533,7 +544,7 @@
     piece = -(-(rows + R // 2) // 16) * 16
     adjoint, grads = call(
         functools.partial(last_kernel, step),
-        [((2, R, W), F32), ((near_count, piece, LANES), BF)],
+        [((R, LANES), F32), ((near_count, piece, LANES), BF)],
         slim_scratch + [((3 * C + piece, LANES), F32)],
         sums, moved, up, masks, gate2, gate1, hidden2, hidden, inputs, *weights)
 
@@ -548,11 +559,10 @@
         functools.partial(far_kernel, rows, far_stride, step),
         [((near_count, piece, LANES), BF), ((R, W), F32)], [], table, received)
     received = exchange(received, NEAR)
-    grad_first, grad_second, grad_third = call(
+    return call(
         functools.partial(output_kernel, scale),
-        [((9, C), F32), ((9, C, C), F32), ((9, C), F32)],
-        [((3 * C, LANES), F32)], received)
-    return adjoint, snapshot, grad_first, grad_second, grad_third
+        [((2, R, W), F32), ((R, W), F32), ((9, C), F32), ((9, C, C), F32), ((9, C), F32)],
+        [((3 * C, LANES), F32)], received, adjoint, snapshot)
 
 
 AXES = (("zh", 4), ("core", 2), ("zl", 2), ("y", 8), ("x", 4))

time: 131 us -> 128 us (0.977)
  blocking collectives: 105 us -> 102 us
    all_to_all x1, blocking collectives: 19.1 us -> 15.9 us  [per_device(): lax.all_to_all(part, TM + SPACE, 0, 0, axis_index_groups=groups, tiled=True)]
where the time goes in v8:
time: 128 us; the launch traced here: 127 us
  blocking collectives  102 us (80%)
  Pallas kernels  10.1 us (8%)
  starting transfers between devices  7.17 us (6%)
  local copies, waits for them, and re-layouts  4.08 us (3%)
  waiting for transfers between devices  2.47 us (2%)
    all_to_all x6, blocking collectives, exchange(): return lax.all_to_all(value, axis, 0, 0, tiled=True)  86.5 us
    all_to_all x1, blocking collectives, per_device(): lax.all_to_all(part, TM + SPACE, 0, 0, axis_index_groups=groups, tiled=True)  15.9 us
    pallas_call x11, Pallas kernels, call(): pl.pallas_call(kernel, out_shape=[jax.ShapeDtypeStruct(shape, dtype) for...  10.1 us
    unnamed x10, local copies, waits for them, and re-layouts  3.99 us
    ppermute x1, starting transfers between devices, per_device(): low = lax.ppermute(bottom, SPACE, forward)  3.96 us
  transfers between devices with their start and end apart: 3, of which 1 were waited for; matrix products, arithmetic and copies ran while one was open for 0% of the time, Pallas kernels for 1%

profile of v8, /device:TPU:1, one launch (start us, length us, event | category | flops | bytes accessed | tf_op | source)
XLA Modules:
  0.0 127.0 jit_solution(5923820159554423047)
XLA Ops:
  0.6 2.4 %shard_map.119 = (bf16[368,256]{1,0:T(8,128)(2,1)}, bf16[368,256]{1,0:T(8,128)(2,1)}, f32[32,256]{1,0:T(8,128)}) custom-call(f32[2,8,128]{2,1,0:T(8,128)} %upstream.1, f32[2,8,128]{2,1,0:T(8,128)} %equilibrium.1, s32[2,8,128]{2,1,0:T(8,128)} %masks.1, f32[8,128]{1,0:T(8,128)} %measurement.1, bf16[2,64,8,128]{3,2,1,0:T(8,128)(2,1)} %saved.3), custom_call_target="tpu_custom_call" | custom-call | tf_op jit(solution)/shard_map/pallas_call | solution.py:442
  3.0 4.0 %collective-permute-start = (bf16[368,256]{1,0:T(8,128)(2,1)}, bf16[368,256]{1,0:T(8,128)(2,1)S(1)}, u32[]{:S(2)}, u32[]{:S(2)}) collective-permute-start(bf16[368,256]{1,0:T(8,128)(2,1)} %get-tuple-element.36), channel_id=1, source_target_pairs={{0,1},{1,2},{2,3},{3,4},{4,5},{5,6},{6,7},{7,8},{8,9},{9,10},{10,1... | collective-permute-start | bytes 565256 | tf_op jit(solution)/shard_map/ppermute | solution.py:489
  7.0 1.3 %collective-permute-start.1 = (bf16[368,256]{1,0:T(8,128)(2,1)}, bf16[368,256]{1,0:T(8,128)(2,1)S(1)}, u32[]{:S(2)}, u32[]{:S(2)}) collective-permute-start(bf16[368,256]{1,0:T(8,128)(2,1)} %get-tuple-element.38), channel_id=1, source_target_pairs={{1,0},{2,1},{3,2},{4,3},{5,4},{6,5},{7,6},{8,7},{9,8},{10,9},{11,1... | collective-permute-start | bytes 565256 | tf_op jit(solution)/shard_map/ppermute | solution.py:490
  8.3 0.1 stack.43.places
  8.4 0.0 copy-start
  8.4 1.0 copy-done
  9.4 0.0 copy-start.1
  9.4 0.9 copy-done.1
  10.3 0.0 copy-start.2
  10.3 0.8 copy-done.2
  11.0 0.0 copy-start.3
  11.0 0.7 copy-done.3
  11.7 0.0 copy-start.4
  11.7 0.7 copy-done.4
  12.4 1.1 shard_map.120
  13.5 0.0 collective-permute-done.low
  13.6 0.0 collective-permute-done.1.high
  13.6 20.2 %all_to_all.35.sums = bf16[8,32,128]{2,1,0:T(8,128)(2,1)S(1)} all-to-all(bf16[8,32,128]{2,1,0:T(8,128)(2,1)S(1)} %get-tuple-element.40), channel_id=1, replica_groups=mesh['zh'=4,'core'=2,'zl'=2,'y'=8,'x'=4] {'zh','core'}, dimensions={0} | all-to-all | bytes 131072 | tf_op jit(solution)/shard_map/all_to_all | solution.py:460
  33.8 1.8 %shard_map.122 = (bf16[8,16,128]{2,1,0:T(8,128)(2,1)S(1)}, f32[14,256]{1,0:T(8,128)S(1)}, f32[1152,256]{1,0:T(8,128)S(1)}, f32[1024,256]{1,0:T(8,128)S(1)}, bf16...) custom-call(s32[8,128]{1,0:T(8,128)S(1)} %get-tuple-element.35.places, bf16[8,32,128]{2,1,0:T(8,128)(2,1)S(1)} %all_to_all.35.sums, ...), custom_call_target="tpu_custom_call" | custom-call | tf_op jit(solution)/shard_map/pallas_call | solution.py:442
  35.6 10.3 %all_to_all.36.sums = bf16[8,16,128]{2,1,0:T(8,128)(2,1)S(1)} all-to-all(bf16[8,16,128]{2,1,0:T(8,128)(2,1)S(1)} %get-tuple-element.48), channel_id=1, replica_groups=mesh['zh'=4,'core'=2,'zl'=2,'y'=8,'x'=4] {'zh','core'}, dimensions={0} | all-to-all | bytes 65536 | tf_op jit(solution)/shard_map/all_to_all | solution.py:460
  46.0 1.1 shard_map.123
  47.0 15.9 %all_to_all.37.received = bf16[16,16,256]{2,1,0:T(8,128)(2,1)S(1)} all-to-all(bf16[16,16,256]{2,1,0:T(8,128)(2,1)S(1)} %get-tuple-element.52), channel_id=1, replica_groups={{1,65,129,193,257,321,385,449,2,66,130,194,258,322,386,450},{3,67,131,1..., dimensions={0} | all-to-all | bytes 262144 | tf_op jit(solution)/shard_map/all_to_all | solution.py:530
  62.9 0.1 shard_map.124.own
  63.0 1.9 %collective-permute-start.2 = (f32[8,256]{1,0:T(8,128)S(1)}, f32[8,256]{1,0:T(8,128)S(1)}, u32[]{:S(2)}, u32[]{:S(2)}) collective-permute-start(f32[8,256]{1,0:T(8,128)S(1)} %shard_map.124.own), channel_id=1, source_target_pairs={{0,1},{1,0},{2,3},{3,2},{4,5},{5,4},{6,7},{7,6},{8,9},{9,8},{10,11... | collective-permute-start | bytes 24584 | tf_op jit(solution)/shard_map/ppermute | solution.py:533
  64.9 2.5 %collective-permute-done.2.near = f32[8,256]{1,0:T(8,128)S(1)} collective-permute-done((f32[8,256]{1,0:T(8,128)S(1)}, f32[8,256]{1,0:T(8,128)S(1)}, u32[]{:S(2)}, u32[]{:S(2)}) %collective-permute-start.2) | collective-permute-done | bytes 8224 | tf_op jit(solution)/shard_map/ppermute | solution.py:533
  67.4 1.3 %shard_map.125 = (bf16[8,16,128]{2,1,0:T(8,128)(2,1)S(1)}, f32[14,256]{1,0:T(8,128)S(1)}) custom-call(s32[8,128]{1,0:T(8,128)S(1)} %get-tuple-element.35.places, bf16[16,16,256]{2,1,0:T(8,128)(2,1)S(1)} %all_to_all.37.received, f32[8,256]{1,0:T(8,128)S(1)} %shard_map.124.own, f32[8,256]{1,0:T(8,128)S(1)} %collective-permute-done.2.near, ...), custom_call_target="tpu_custom_call" | custom-call | tf_op jit(solution)/shard_map/pallas_call | solution.py:442
  68.7 11.1 %all_to_all.38.sums = bf16[8,16,128]{2,1,0:T(8,128)(2,1)S(1)} all-to-all(bf16[8,16,128]{2,1,0:T(8,128)(2,1)S(1)} %get-tuple-element.54), channel_id=1, replica_groups=mesh['zh'=4,'core'=2,'zl'=2,'y'=8,'x'=4] {'zh','core'}, dimensions={0} | all-to-all | bytes 65536 | tf_op jit(solution)/shard_map/all_to_all | solution.py:460
  79.8 1.4 %shard_map.126 = (f32[8,256]{1,0:T(8,128)S(1)}, bf16[16,16,256]{2,1,0:T(8,128)(2,1)S(1)}) custom-call(bf16[8,16,128]{2,1,0:T(8,128)(2,1)S(1)} %all_to_all.38.sums, f32[14,256]{1,0:T(8,128)S(1)} %get-tuple-element.55.moved, f32[20,256]{1,0:T(8,128)S(1)} %get-tuple-element.41.up, f32[20,256]{1,0:T(8,128)S(1)} %get-tuple-element.42.masks, ...), custom_call_target="tpu_custom_call" | custom-call | tf_op jit(solution)/shard_map/pallas_call | solution.py:442
  81.2 12.4 %all_to_all.39.received = bf16[16,16,256]{2,1,0:T(8,128)(2,1)S(1)} all-to-all(bf16[16,16,256]{2,1,0:T(8,128)(2,1)S(1)} %get-tuple-element.59), channel_id=1, replica_groups=mesh['zh'=4,'core'=2,'zl'=2,'y'=8,'x'=4] {'core','zl','x'}, dimensions={0} | all-to-all | bytes 262144 | tf_op jit(solution)/shard_map/all_to_all | solution.py:460
  93.7 20.4 %all_to_all.40.received = bf16[32,16,256]{2,1,0:T(8,128)(2,1)S(1)} all-to-all(bf16[32,16,256]{2,1,0:T(8,128)(2,1)S(1)} %shard_map.127), channel_id=1, replica_groups=mesh['zh'=4,'core'=2,'zl'=2,'y'=8,'x'=4] {'zh','y'}, dimensions={0} | all-to-all | bytes 524288 | tf_op jit(solution)/shard_map/all_to_all | solution.py:460
  114.1 0.1 shard_map.128
  114.2 12.0 %all_to_all.41.received = bf16[16,16,256]{2,1,0:T(8,128)(2,1)S(1)} all-to-all(bf16[16,16,256]{2,1,0:T(8,128)(2,1)S(1)} %get-tuple-element.60), channel_id=1, replica_groups=mesh['zh'=4,'core'=2,'zl'=2,'y'=8,'x'=4] {'core','zl','x'}, dimensions={0} | all-to-all | bytes 262144 | tf_op jit(solution)/shard_map/all_to_all | solution.py:460
  126.1 0.8 shard_map.129
  (2 shorter events, 0.1 us)
Async XLA Ops:
  3.0 10.5 %collective-permute-start = (bf16[368,256]{1,0:T(8,128)(2,1)}, bf16[368,256]{1,0:T(8,128)(2,1)S(1)}, u32[]{:S(2)}, u32[]{:S(2)}) collective-permute-start(bf16[368,256]{1,0:T(8,128)(2,1)} %get-tuple-element.36), channel_id=1, source_target_pairs={{0,1},{1,2},{2,3},{3,4},{4,5},{5,6},{6,7},{7,8},{8,9},{9,10},{10,1... | collective-permute-start | bytes 565256 | tf_op jit(solution)/shard_map/ppermute | solution.py:489
  7.0 6.6 %collective-permute-start.1 = (bf16[368,256]{1,0:T(8,128)(2,1)}, bf16[368,256]{1,0:T(8,128)(2,1)S(1)}, u32[]{:S(2)}, u32[]{:S(2)}) collective-permute-start(bf16[368,256]{1,0:T(8,128)(2,1)} %get-tuple-element.38), channel_id=1, source_target_pairs={{1,0},{2,1},{3,2},{4,3},{5,4},{6,5},{7,6},{8,7},{9,8},{10,9},{11,1... | collective-permute-start | bytes 565256 | tf_op jit(solution)/shard_map/ppermute | solution.py:490
  8.4 1.0 copy-start
  9.4 0.9 copy-start.1
  10.3 0.8 copy-start.2
  11.0 0.7 copy-start.3
  11.7 0.7 copy-start.4
  63.0 4.4 %collective-permute-start.2 = (f32[8,256]{1,0:T(8,128)S(1)}, f32[8,256]{1,0:T(8,128)S(1)}, u32[]{:S(2)}, u32[]{:S(2)}) collective-permute-start(f32[8,256]{1,0:T(8,128)S(1)} %shard_map.124.own), channel_id=1, source_target_pairs={{0,1},{1,0},{2,3},{3,2},{4,5},{5,4},{6,7},{7,6},{8,9},{9,8},{10,11... | collective-permute-start | bytes 24584 | tf_op jit(solution)/shard_map/ppermute | solution.py:533

commit v9 on v8

--- a/solution.py
+++ b/solution.py
@@ -23,10 +23,10 @@
 F32 = jnp.float32
 
 TM = ("zh", "core")
-SPACE = ("zl", "y", "x")
+SPACE = ("zl", "yh", "yl", "x")
 BEFORE, AFTER, ODD, OWN_HALF, THEIR_ENTRY, THEIR_HALF, NEAR_AT, FAR_AT = range(8)
-NEAR = ("core", "zl", "x")
-FAR = ("zh", "y")
+NEAR = ("core", "zl", "yl", "x")
+FAR = ("zh", "yh")
 
 
 def roll_cols(value, step):
@@ -145,16 +145,16 @@
 
 
 def pack_kernel(upstream, equilibrium, masks, measurement, saved, top, bottom, own_fields,
-                up_in, fixed_in, masks_in, snapshot_in, saved_in, top_out, bottom_out, sems):
-    arrivals = [
+                up_in, fixed_in, masks_in, snapshot_in, saved_in, sems):
+    copies = [
         pltpu.make_async_copy(source, target, sems.at[k])
         for k, (source, target) in enumerate((
-            (saved.at[0], saved_in.at[0]), (saved.at[1], saved_in.at[1]), (upstream, up_in),
-            (equilibrium, fixed_in), (masks, masks_in), (measurement, snapshot_in)))
+            (saved, saved_in), (upstream, up_in), (equilibrium, fixed_in), (masks, masks_in),
+            (measurement, snapshot_in)))
     ]
-    for copy in arrivals:
+    for copy in copies:
         copy.start()
-    for copy in arrivals[2:]:
+    for copy in copies[1:]:
         copy.wait()
 
     def by_frame(ref):
@@ -171,22 +171,14 @@
     for k in range(0, len(fields), 2):
         pair = jnp.concatenate([field.astype(F32) for field in fields[k:k + 2]], axis=0).astype(BF)
         at = EDGE * C + k * R
-        top_out[at:at + 2 * R, :] = pair
-        bottom_out[at:at + 2 * R, :] = pair
-    departures = []
+        top[at:at + 2 * R, :] = pair
+        bottom[at:at + 2 * R, :] = pair
+    copies[0].wait()
     for frame in range(2):
         lanes = slice(frame * W, (frame + 1) * W)
-        arrivals[frame].wait()
         rows = jnp.swapaxes(saved_in[frame].astype(F32), 0, 1).astype(BF).reshape(R * C, W)
-        for value, here, there in ((rows[:EDGE * C], top_out, top),
-                                   (rows[(R - EDGE) * C:], bottom_out, bottom)):
-            here[:EDGE * C, lanes] = value
-            copy = pltpu.make_async_copy(here.at[:, lanes], there.at[:, lanes],
-                                         sems.at[len(arrivals) + len(departures)])
-            copy.start()
-            departures.append(copy)
-    for copy in departures:
-        copy.wait()
+        top[:EDGE * C, lanes] = rows[:EDGE * C]
+        bottom[:EDGE * C, lanes] = rows[(R - EDGE) * C:]
 
 
 def stage_kernel(places, first, second, third, saved, own_fields, forward_w, third_w, second_w,
@@ -342,7 +334,7 @@
     finish_wide(field, before, after, masks, part, moved)
 
 
-def last_kernel(step, sums, moved, up, masks, gate2, gate1, hidden2, hidden, inputs, third_w,
+def last_kernel(step, cores, sums, moved, up, masks, gate2, gate1, hidden2, hidden, inputs, third_w,
                 second_w, first_w, adjoint, grads, copies, d2, d1, taps, total):
     copies[...] = jnp.zeros_like(copies)
     field = narrow_field(step, sums, moved, up, masks)
@@ -378,13 +370,17 @@
     count = grads.shape[0]
     rows = 3 * C // count
     line = lax.broadcasted_iota(jnp.int32, grads.shape[1:], 0)
-    extra = jnp.zeros(grads.shape[1:], F32)
-    for k in range(R // 2):
-        pair = jnp.concatenate([snapshot[2 * k:2 * k + 1], snapshot[2 * k + 1:2 * k + 2]], axis=1)
-        extra = jnp.where(line == rows + k, pair, extra)
+    extras = []
+    for core in range(cores):
+        extra = jnp.zeros(grads.shape[1:], F32)
+        for k in range(R // 2 // cores):
+            at = 2 * (core * (R // 2 // cores) + k)
+            pair = jnp.concatenate([snapshot[at:at + 1], snapshot[at + 1:at + 2]], axis=1)
+            extra = jnp.where(line == rows + k, pair, extra)
+        extras.append(extra)
     for k in range(count):
         grads[k] = jnp.where(line < rows, total[k * rows:k * rows + grads.shape[1], :],
-                             extra).astype(BF)
+                             extras[k * cores // count]).astype(BF)
 
 
 def reduce_pieces(rows, place, stride, received):
@@ -399,28 +395,24 @@
     return jnp.where(line < rows, total, extra)
 
 
-def near_kernel(rows, stride, places, received, out):
-    total = reduce_pieces(rows, places[NEAR_AT, 0], stride, received).astype(BF)
+def sum_kernel(rows, stride, at, places, received, out):
+    total = reduce_pieces(rows, places[at, 0], stride, received).astype(BF)
     for k in range(out.shape[0]):
         out[k] = total
 
 
-def far_kernel(rows, stride, step, places, received, out, snapshot):
-    total = reduce_pieces(rows, places[FAR_AT, 0], stride, received)
-    for k in range(R // 2):
-        snapshot[2 * k:2 * k + 1, :] = step * total[rows + k:rows + k + 1, :W]
-        snapshot[2 * k + 1:2 * k + 2, :] = step * total[rows + k:rows + k + 1, W:]
-    total = total.astype(BF)
-    for k in range(out.shape[0]):
-        out[k] = total
-
-
-def output_kernel(scale, received, field, sums, adjoint, snapshot, first, second, third, total):
+def output_kernel(step, scale, cores, places, received, field, adjoint, snapshot, first, second,
+                  third, total):
     adjoint[0] = field[:, :W]
     adjoint[1] = field[:, W:]
-    snapshot[...] = sums[...]
     count = received.shape[0]
     rows = 3 * C // count
+    for core in range(cores):
+        piece = received[places[NEAR_AT, 0] + core * (count // cores)].astype(F32) * step
+        for k in range(R // 2 // cores):
+            at = 2 * (core * (R // 2 // cores) + k)
+            snapshot[at:at + 1, :] = piece[rows + k:rows + k + 1, :W]
+            snapshot[at + 1:at + 2, :] = piece[rows + k:rows + k + 1, W:]
     for k in range(count):
         total[k * rows:(k + 1) * rows, :] = received[k].astype(F32)[:rows] * scale
     for i in (-1, 0, 1):
@@ -435,15 +427,14 @@
             third[tap:tap + 1, :] = total[at:at + 1, 3 * C:] + total[at + 3:at + 4, 3 * C:]
 
 
-def call(kernel, outs, scratch, *operands, specs=None, cost=None, sems=0, limit=40,
-         out_specs=None):
+def call(kernel, outs, scratch, *operands, specs=None, cost=None, sems=0, limit=40):
     if specs is None:
         specs = [pl.BlockSpec(memory_space=pltpu.VMEM)] * len(operands)
     return pl.pallas_call(
         kernel,
         out_shape=[jax.ShapeDtypeStruct(shape, dtype) for shape, dtype in outs],
         in_specs=specs,
-        out_specs=out_specs or [pl.BlockSpec(memory_space=pltpu.VMEM)] * len(outs),
+        out_specs=[pl.BlockSpec(memory_space=pltpu.VMEM)] * len(outs),
         scratch_shapes=[pltpu.VMEM(shape, dtype) for shape, dtype in scratch]
         + [pltpu.SemaphoreType.DMA((sems,))] * (sems > 0),
         compiler_params=pltpu.CompilerParams(vmem_limit_bytes=limit * 2**20),
@@ -483,9 +474,9 @@
     frame = ((2, R, W), F32)
     top, bottom, own_fields = call(
         pack_kernel, [edge, edge, fields],
-        [frame, frame, ((2, R, W), jnp.int32), ((R, W), F32), ((2, C, R, W), BF), edge, edge],
+        [frame, frame, ((2, R, W), jnp.int32), ((R, W), F32), ((2, C, R, W), BF)],
         upstream, equilibrium, coding_masks, measurement, saved_second,
-        specs=[hbm] * 5, out_specs=[hbm, hbm, whole], sems=10, limit=60)
+        specs=[hbm] * 5, sems=5, limit=60)
     low = lax.ppermute(bottom, SPACE, forward)
     high = lax.ppermute(top, SPACE, backward)
 
@@ -541,9 +532,9 @@
     near_count = math.prod(near_sizes)
     far_count = math.prod(far_sizes)
     rows = 3 * C // near_count
-    piece = -(-(rows + R // 2) // 16) * 16
+    piece = -(-(rows + R // 2 // near_sizes[0]) // 8) * 8
     adjoint, grads = call(
-        functools.partial(last_kernel, step),
+        functools.partial(last_kernel, step, near_sizes[0]),
         [((R, LANES), F32), ((near_count, piece, LANES), BF)],
         slim_scratch + [((3 * C + piece, LANES), F32)],
         sums, moved, up, masks, gate2, gate1, hidden2, hidden, inputs, *weights)
@@ -552,20 +543,20 @@
     near_stride = near_count // near_sizes[0]
     far_stride = far_count // far_sizes[0]
     received, = call(
-        functools.partial(near_kernel, rows, near_stride),
+        functools.partial(sum_kernel, rows, near_stride, NEAR_AT),
         [((far_count, piece, LANES), BF)], [], table, received)
     received = exchange(received, FAR)
-    received, snapshot = call(
-        functools.partial(far_kernel, rows, far_stride, step),
-        [((near_count, piece, LANES), BF), ((R, W), F32)], [], table, received)
+    received, = call(
+        functools.partial(sum_kernel, rows, far_stride, FAR_AT),
+        [((near_count, piece, LANES), BF)], [], table, received)
     received = exchange(received, NEAR)
     return call(
-        functools.partial(output_kernel, scale),
+        functools.partial(output_kernel, step, scale, near_sizes[0]),
         [((2, R, W), F32), ((R, W), F32), ((9, C), F32), ((9, C, C), F32), ((9, C), F32)],
-        [((3 * C, LANES), F32)], received, adjoint, snapshot)
-
-
-AXES = (("zh", 4), ("core", 2), ("zl", 2), ("y", 8), ("x", 4))
+        [((3 * C, LANES), F32)], table, received, adjoint)
+
+
+AXES = (("zh", 4), ("core", 2), ("zl", 2), ("yh", 4), ("yl", 2), ("x", 4))
 
 
 def solution(mesh, axes=AXES):

time: 128 us -> 126 us (0.984)
  no operation moved by 1% of the time
where the time goes in v9:
time: 126 us; the launch traced here: 125 us
  blocking collectives  101 us (80%)
  Pallas kernels  9.6 us (8%)
  starting transfers between devices  7.17 us (6%)
  local copies, waits for them, and re-layouts  4.08 us (3%)
  waiting for transfers between devices  2.47 us (2%)
    all_to_all x6, blocking collectives, exchange(): return lax.all_to_all(value, axis, 0, 0, tiled=True)  85.4 us
    all_to_all x1, blocking collectives, per_device(): lax.all_to_all(part, TM + SPACE, 0, 0, axis_index_groups=groups, tiled=True)  15.9 us
    pallas_call x11, Pallas kernels, call(): pl.pallas_call(kernel, out_shape=[jax.ShapeDtypeStruct(shape, dtype) for...  9.6 us
    unnamed x10, local copies, waits for them, and re-layouts  3.99 us
    ppermute x1, starting transfers between devices, per_device(): low = lax.ppermute(bottom, SPACE, forward)  3.96 us
  transfers between devices with their start and end apart: 3, of which 1 were waited for; matrix products, arithmetic and copies ran while one was open for 0% of the time, Pallas kernels for 1%

profile of v9, /device:TPU:1, one launch (start us, length us, event | category | flops | bytes accessed | tf_op | source)
XLA Modules:
  0.0 125.4 jit_solution(115253414493774885)
XLA Ops:
  0.6 1.9 %shard_map.119 = (bf16[368,256]{1,0:T(8,128)(2,1)}, bf16[368,256]{1,0:T(8,128)(2,1)}, f32[32,256]{1,0:T(8,128)}) custom-call(f32[2,8,128]{2,1,0:T(8,128)} %upstream.1, f32[2,8,128]{2,1,0:T(8,128)} %equilibrium.1, s32[2,8,128]{2,1,0:T(8,128)} %masks.1, f32[8,128]{1,0:T(8,128)} %measurement.1, bf16[2,64,8,128]{3,2,1,0:T(8,128)(2,1)} %saved.3), custom_call_target="tpu_custom_call" | custom-call | tf_op jit(solution)/shard_map/pallas_call | solution.py:433
  2.5 4.0 %collective-permute-start = (bf16[368,256]{1,0:T(8,128)(2,1)}, bf16[368,256]{1,0:T(8,128)(2,1)S(1)}, u32[]{:S(2)}, u32[]{:S(2)}) collective-permute-start(bf16[368,256]{1,0:T(8,128)(2,1)} %get-tuple-element.34), channel_id=1, source_target_pairs={{0,1},{1,2},{2,3},{3,4},{4,5},{5,6},{6,7},{7,8},{8,9},{9,10},{10,1... | collective-permute-start | bytes 565256 | tf_op jit(solution)/shard_map/ppermute | solution.py:480
  6.5 1.3 %collective-permute-start.1 = (bf16[368,256]{1,0:T(8,128)(2,1)}, bf16[368,256]{1,0:T(8,128)(2,1)S(1)}, u32[]{:S(2)}, u32[]{:S(2)}) collective-permute-start(bf16[368,256]{1,0:T(8,128)(2,1)} %get-tuple-element.36), channel_id=1, source_target_pairs={{1,0},{2,1},{3,2},{4,3},{5,4},{6,5},{7,6},{8,7},{9,8},{10,9},{11,1... | collective-permute-start | bytes 565256 | tf_op jit(solution)/shard_map/ppermute | solution.py:481
  7.8 0.1 stack.43.places
  7.9 0.0 copy-start
  7.9 1.0 copy-done
  8.8 0.0 copy-start.1
  8.8 0.9 copy-done.1
  9.7 0.0 copy-start.2
  9.7 0.8 copy-done.2
  10.5 0.0 copy-start.3
  10.5 0.7 copy-done.3
  11.2 0.0 copy-start.4
  11.2 0.7 copy-done.4
  11.9 1.1 shard_map.120
  13.0 0.0 collective-permute-done.low
  13.0 0.0 collective-permute-done.1.high
  13.1 20.2 %all_to_all.35.sums = bf16[8,32,128]{2,1,0:T(8,128)(2,1)S(1)} all-to-all(bf16[8,32,128]{2,1,0:T(8,128)(2,1)S(1)} %get-tuple-element.38), channel_id=1, replica_groups=mesh['zh'=4,'core'=2,'zl'=2,'yh'=4,'yl'=2,'x'=4] {'zh','core'}, dimensions={0} | all-to-all | bytes 131072 | tf_op jit(solution)/shard_map/all_to_all | solution.py:451
  33.3 1.8 %shard_map.122 = (bf16[8,16,128]{2,1,0:T(8,128)(2,1)S(1)}, f32[14,256]{1,0:T(8,128)S(1)}, f32[1152,256]{1,0:T(8,128)S(1)}, f32[1024,256]{1,0:T(8,128)S(1)}, bf16...) custom-call(s32[8,128]{1,0:T(8,128)S(1)} %get-tuple-element.33.places, bf16[8,32,128]{2,1,0:T(8,128)(2,1)S(1)} %all_to_all.35.sums, ...), custom_call_target="tpu_custom_call" | custom-call | tf_op jit(solution)/shard_map/pallas_call | solution.py:433
  35.1 10.3 %all_to_all.36.sums = bf16[8,16,128]{2,1,0:T(8,128)(2,1)S(1)} all-to-all(bf16[8,16,128]{2,1,0:T(8,128)(2,1)S(1)} %get-tuple-element.46), channel_id=1, replica_groups=mesh['zh'=4,'core'=2,'zl'=2,'yh'=4,'yl'=2,'x'=4] {'zh','core'}, dimensions={0} | all-to-all | bytes 65536 | tf_op jit(solution)/shard_map/all_to_all | solution.py:451
  45.4 1.1 shard_map.123
  46.5 15.9 %all_to_all.37.received = bf16[16,16,256]{2,1,0:T(8,128)(2,1)S(1)} all-to-all(bf16[16,16,256]{2,1,0:T(8,128)(2,1)S(1)} %get-tuple-element.50), channel_id=1, replica_groups={{1,65,129,193,257,321,385,449,2,66,130,194,258,322,386,450},{3,67,131,1..., dimensions={0} | all-to-all | bytes 262144 | tf_op jit(solution)/shard_map/all_to_all | solution.py:521
  62.4 0.1 shard_map.124.own
  62.5 1.9 %collective-permute-start.2 = (f32[8,256]{1,0:T(8,128)S(1)}, f32[8,256]{1,0:T(8,128)S(1)}, u32[]{:S(2)}, u32[]{:S(2)}) collective-permute-start(f32[8,256]{1,0:T(8,128)S(1)} %shard_map.124.own), channel_id=1, source_target_pairs={{0,1},{1,0},{2,3},{3,2},{4,5},{5,4},{6,7},{7,6},{8,9},{9,8},{10,11... | collective-permute-start | bytes 24584 | tf_op jit(solution)/shard_map/ppermute | solution.py:524
  64.4 2.5 %collective-permute-done.2.near = f32[8,256]{1,0:T(8,128)S(1)} collective-permute-done((f32[8,256]{1,0:T(8,128)S(1)}, f32[8,256]{1,0:T(8,128)S(1)}, u32[]{:S(2)}, u32[]{:S(2)}) %collective-permute-start.2) | collective-permute-done | bytes 8224 | tf_op jit(solution)/shard_map/ppermute | solution.py:524
  66.9 1.3 %shard_map.125 = (bf16[8,16,128]{2,1,0:T(8,128)(2,1)S(1)}, f32[14,256]{1,0:T(8,128)S(1)}) custom-call(s32[8,128]{1,0:T(8,128)S(1)} %get-tuple-element.33.places, bf16[16,16,256]{2,1,0:T(8,128)(2,1)S(1)} %all_to_all.37.received, f32[8,256]{1,0:T(8,128)S(1)} %shard_map.124.own, f32[8,256]{1,0:T(8,128)S(1)} %collective-permute-done.2.near, ...), custom_call_target="tpu_custom_call" | custom-call | tf_op jit(solution)/shard_map/pallas_call | solution.py:433
  68.2 11.1 %all_to_all.38.sums = bf16[8,16,128]{2,1,0:T(8,128)(2,1)S(1)} all-to-all(bf16[8,16,128]{2,1,0:T(8,128)(2,1)S(1)} %get-tuple-element.52), channel_id=1, replica_groups=mesh['zh'=4,'core'=2,'zl'=2,'yh'=4,'yl'=2,'x'=4] {'zh','core'}, dimensions={0} | all-to-all | bytes 65536 | tf_op jit(solution)/shard_map/all_to_all | solution.py:451
  79.3 1.4 %shard_map.126 = (f32[8,256]{1,0:T(8,128)S(1)}, bf16[32,8,256]{2,1,0:T(8,128)(2,1)S(1)}) custom-call(bf16[8,16,128]{2,1,0:T(8,128)(2,1)S(1)} %all_to_all.38.sums, f32[14,256]{1,0:T(8,128)S(1)} %get-tuple-element.53.moved, f32[20,256]{1,0:T(8,128)S(1)} %get-tuple-element.39.up, f32[20,256]{1,0:T(8,128)S(1)} %get-tuple-element.40.masks, ...), custom_call_target="tpu_custom_call" | custom-call | tf_op jit(solution)/shard_map/pallas_call | solution.py:433
  80.7 13.5 %all_to_all.39.received = bf16[32,8,256]{2,1,0:T(8,128)(2,1)S(1)} all-to-all(bf16[32,8,256]{2,1,0:T(8,128)(2,1)S(1)} %get-tuple-element.57), channel_id=1, replica_groups=mesh['zh'=4,'core'=2,'zl'=2,'yh'=4,'yl'=2,'x'=4] {'core','zl','yl','x'}, dimensions={0} | all-to-all | bytes 262144 | tf_op jit(solution)/shard_map/all_to_all | solution.py:451
  94.3 18.5 %all_to_all.40.received = bf16[16,8,256]{2,1,0:T(8,128)(2,1)S(1)} all-to-all(bf16[16,8,256]{2,1,0:T(8,128)(2,1)S(1)} %shard_map.127), channel_id=1, replica_groups=mesh['zh'=4,'core'=2,'zl'=2,'yh'=4,'yl'=2,'x'=4] {'zh','yh'}, dimensions={0} | all-to-all | bytes 131072 | tf_op jit(solution)/shard_map/all_to_all | solution.py:451
  112.7 0.1 shard_map.128
  112.8 11.8 %all_to_all.41.received = bf16[32,8,256]{2,1,0:T(8,128)(2,1)S(1)} all-to-all(bf16[32,8,256]{2,1,0:T(8,128)(2,1)S(1)} %shard_map.128), channel_id=1, replica_groups=mesh['zh'=4,'core'=2,'zl'=2,'yh'=4,'yl'=2,'x'=4] {'core','zl','yl','x'}, dimensions={0} | all-to-all | bytes 262144 | tf_op jit(solution)/shard_map/all_to_all | solution.py:451
  124.6 0.8 shard_map.129
  (2 shorter events, 0.1 us)
Async XLA Ops:
  2.5 10.5 %collective-permute-start = (bf16[368,256]{1,0:T(8,128)(2,1)}, bf16[368,256]{1,0:T(8,128)(2,1)S(1)}, u32[]{:S(2)}, u32[]{:S(2)}) collective-permute-start(bf16[368,256]{1,0:T(8,128)(2,1)} %get-tuple-element.34), channel_id=1, source_target_pairs={{0,1},{1,2},{2,3},{3,4},{4,5},{5,6},{6,7},{7,8},{8,9},{9,10},{10,1... | collective-permute-start | bytes 565256 | tf_op jit(solution)/shard_map/ppermute | solution.py:480
  6.5 6.6 %collective-permute-start.1 = (bf16[368,256]{1,0:T(8,128)(2,1)}, bf16[368,256]{1,0:T(8,128)(2,1)S(1)}, u32[]{:S(2)}, u32[]{:S(2)}) collective-permute-start(bf16[368,256]{1,0:T(8,128)(2,1)} %get-tuple-element.36), channel_id=1, source_target_pairs={{1,0},{2,1},{3,2},{4,3},{5,4},{6,5},{7,6},{8,7},{9,8},{10,9},{11,1... | collective-permute-start | bytes 565256 | tf_op jit(solution)/shard_map/ppermute | solution.py:481
  7.9 1.0 copy-start
  8.8 0.9 copy-start.1
  9.7 0.8 copy-start.2
  10.5 0.7 copy-start.3
  11.2 0.7 copy-start.4
  62.5 4.4 %collective-permute-start.2 = (f32[8,256]{1,0:T(8,128)S(1)}, f32[8,256]{1,0:T(8,128)S(1)}, u32[]{:S(2)}, u32[]{:S(2)}) collective-permute-start(f32[8,256]{1,0:T(8,128)S(1)} %shard_map.124.own), channel_id=1, source_target_pairs={{0,1},{1,0},{2,3},{3,2},{4,5},{5,4},{6,7},{7,6},{8,9},{9,8},{10,11... | collective-permute-start | bytes 24584 | tf_op jit(solution)/shard_map/ppermute | solution.py:524

commit v10 on v9

--- a/solution.py
+++ b/solution.py
@@ -23,9 +23,9 @@
 F32 = jnp.float32
 
 TM = ("zh", "core")
-SPACE = ("zl", "yh", "yl", "x")
+SPACE = ("zl", "yh", "yl", "xh", "xl")
 BEFORE, AFTER, ODD, OWN_HALF, THEIR_ENTRY, THEIR_HALF, NEAR_AT, FAR_AT = range(8)
-NEAR = ("core", "zl", "yl", "x")
+NEAR = ("core", "zl", "yl", "xh", "xl")
 FAR = ("zh", "yh")
 
 
@@ -326,9 +326,9 @@
     high = (up[after_rows, :] + theirs[:HALO]
             - step * masks[after_rows, :] * totals[:HALO]) * after
     odd = twice(places[ODD:ODD + 1, :]) == 1
-    whole[0:HALO, :] = jnp.where(odd, near[R - HALO:, :], low)
+    whole[0:HALO, :] = jnp.where(odd, near[0, R - HALO:, :], low)
     whole[HALO:HALO + R, :] = own[...]
-    whole[HALO + R:, :] = jnp.where(odd, high, near[:HALO, :])
+    whole[HALO + R:, :] = jnp.where(odd, high, near[1, :HALO, :])
     field = adjoint_map(0, whole[...], gate2, gate1, third_w[...], second_w[...], first_w[...],
                         copies, d2, d1, taps)
     finish_wide(field, before, after, masks, part, moved)
@@ -521,7 +521,7 @@
     received = lax.all_to_all(part, TM + SPACE, 0, 0, axis_index_groups=groups, tiled=True)
     field, = call(functools.partial(update_kernel, step), [((R, LANES), F32)], [],
                   table, received, moved, up, masks)
-    near = lax.ppermute(field, SPACE, [(i, i ^ 1) for i in range(tiles)])
+    near = lax.all_gather(field, SPACE[-1])
     part, moved = call(
         functools.partial(third_kernel, step), wide_outs, [copies, d2, d1, taps, ext],
         table, received, field, near, up, masks, gate2, gate1, *weights)
@@ -556,7 +556,7 @@
         [((3 * C, LANES), F32)], table, received, adjoint)
 
 
-AXES = (("zh", 4), ("core", 2), ("zl", 2), ("yh", 4), ("yl", 2), ("x", 4))
+AXES = (("zh", 4), ("core", 2), ("zl", 2), ("yh", 4), ("yl", 2), ("xh", 2), ("xl", 2))
 
 
 def solution(mesh, axes=AXES):

time: 126 us -> 125 us (level)
  blocking collectives: 101 us -> 105 us
  waiting for transfers between devices: 2.47 us -> 0.01 us
  starting transfers between devices: 7.17 us -> 5.25 us
    all_gather x0 -> x1, blocking collectives: none -> 3.22 us  [per_device(): near = lax.all_gather(field, SPACE[-1])]
    ppermute x1 -> x0, waiting for transfers between devices: 2.47 us -> none  [per_device(): near = lax.ppermute(field, SPACE, [(i, i ^ 1) for i in range(tiles)])]
    ppermute x1 -> x0, starting transfers between devices: 1.92 us -> none  [per_device(): near = lax.ppermute(field, SPACE, [(i, i ^ 1) for i in range(tiles)])]
  transfers between devices with their start and end apart: 3 -> 2, of which waited for: 1 -> 0; matrix products, arithmetic and copies ran while one was open for 0% -> 0% of each run, Pallas kernels for 1% -> 1%
where the time goes in v10:
time: 125 us; the launch traced here: 124 us
  blocking collectives  105 us (84%)
  Pallas kernels  9.6 us (8%)
  starting transfers between devices  5.25 us (4%)
  local copies, waits for them, and re-layouts  4.08 us (3%)
    all_to_all x6, blocking collectives, exchange(): return lax.all_to_all(value, axis, 0, 0, tiled=True)  85.3 us
    all_to_all x1, blocking collectives, per_device(): lax.all_to_all(part, TM + SPACE, 0, 0, axis_index_groups=groups, tiled=True)  16 us
    pallas_call x11, Pallas kernels, call(): pl.pallas_call(kernel, out_shape=[jax.ShapeDtypeStruct(shape, dtype) for...  9.6 us
    unnamed x10, local copies, waits for them, and re-layouts  3.99 us
    ppermute x1, starting transfers between devices, per_device(): low = lax.ppermute(bottom, SPACE, forward)  3.96 us
    all_gather x1, blocking collectives, per_device(): near = lax.all_gather(field, SPACE[-1])  3.22 us
  transfers between devices with their start and end apart: 2, of which 0 were waited for; matrix products, arithmetic and copies ran while one was open for 0% of the time, Pallas kernels for 1%

profile of v10, /device:TPU:1, one launch (start us, length us, event | category | flops | bytes accessed | tf_op | source)
XLA Modules:
  0.0 124.2 jit_solution(11599296121078185237)
XLA Ops:
  0.6 1.9 %shard_map.119 = (bf16[368,256]{1,0:T(8,128)(2,1)}, bf16[368,256]{1,0:T(8,128)(2,1)}, f32[32,256]{1,0:T(8,128)}) custom-call(f32[2,8,128]{2,1,0:T(8,128)} %upstream.1, f32[2,8,128]{2,1,0:T(8,128)} %equilibrium.1, s32[2,8,128]{2,1,0:T(8,128)} %masks.1, f32[8,128]{1,0:T(8,128)} %measurement.1, bf16[2,64,8,128]{3,2,1,0:T(8,128)(2,1)} %saved.3), custom_call_target="tpu_custom_call" | custom-call | tf_op jit(solution)/shard_map/pallas_call | solution.py:433
  2.5 4.0 %collective-permute-start = (bf16[368,256]{1,0:T(8,128)(2,1)}, bf16[368,256]{1,0:T(8,128)(2,1)S(1)}, u32[]{:S(2)}, u32[]{:S(2)}) collective-permute-start(bf16[368,256]{1,0:T(8,128)(2,1)} %get-tuple-element.34), channel_id=1, source_target_pairs={{0,1},{1,2},{2,3},{3,4},{4,5},{5,6},{6,7},{7,8},{8,9},{9,10},{10,1... | collective-permute-start | bytes 565256 | tf_op jit(solution)/shard_map/ppermute | solution.py:480
  6.5 1.3 %collective-permute-start.1 = (bf16[368,256]{1,0:T(8,128)(2,1)}, bf16[368,256]{1,0:T(8,128)(2,1)S(1)}, u32[]{:S(2)}, u32[]{:S(2)}) collective-permute-start(bf16[368,256]{1,0:T(8,128)(2,1)} %get-tuple-element.36), channel_id=1, source_target_pairs={{1,0},{2,1},{3,2},{4,3},{5,4},{6,5},{7,6},{8,7},{9,8},{10,9},{11,1... | collective-permute-start | bytes 565256 | tf_op jit(solution)/shard_map/ppermute | solution.py:481
  7.8 0.1 stack.43.places
  7.9 0.0 copy-start
  7.9 1.0 copy-done
  8.8 0.0 copy-start.1
  8.8 0.9 copy-done.1
  9.7 0.0 copy-start.2
  9.7 0.8 copy-done.2
  10.5 0.0 copy-start.3
  10.5 0.7 copy-done.3
  11.2 0.0 copy-start.4
  11.2 0.7 copy-done.4
  11.9 1.1 shard_map.120
  13.0 0.0 collective-permute-done.low
  13.0 0.0 collective-permute-done.1.high
  13.1 20.2 %all_to_all.35.sums = bf16[8,32,128]{2,1,0:T(8,128)(2,1)S(1)} all-to-all(bf16[8,32,128]{2,1,0:T(8,128)(2,1)S(1)} %get-tuple-element.38), channel_id=1, replica_groups=mesh['zh'=4,'core'=2,'zl'=2,'yh'=4,'yl'=2,'xh'=2,'xl'=2] {'zh','core'}, dimensions={0} | all-to-all | bytes 131072 | tf_op jit(solution)/shard_map/all_to_all | solution.py:451
  33.3 1.8 %shard_map.122 = (bf16[8,16,128]{2,1,0:T(8,128)(2,1)S(1)}, f32[14,256]{1,0:T(8,128)S(1)}, f32[1152,256]{1,0:T(8,128)S(1)}, f32[1024,256]{1,0:T(8,128)S(1)}, bf16...) custom-call(s32[8,128]{1,0:T(8,128)S(1)} %get-tuple-element.33.places, bf16[8,32,128]{2,1,0:T(8,128)(2,1)S(1)} %all_to_all.35.sums, ...), custom_call_target="tpu_custom_call" | custom-call | tf_op jit(solution)/shard_map/pallas_call | solution.py:433
  35.1 10.3 %all_to_all.36.sums = bf16[8,16,128]{2,1,0:T(8,128)(2,1)S(1)} all-to-all(bf16[8,16,128]{2,1,0:T(8,128)(2,1)S(1)} %get-tuple-element.46), channel_id=1, replica_groups=mesh['zh'=4,'core'=2,'zl'=2,'yh'=4,'yl'=2,'xh'=2,'xl'=2] {'zh','core'}, dimensions={0} | all-to-all | bytes 65536 | tf_op jit(solution)/shard_map/all_to_all | solution.py:451
  45.4 1.1 shard_map.123
  46.5 16.0 %all_to_all.37.received = bf16[16,16,256]{2,1,0:T(8,128)(2,1)S(1)} all-to-all(bf16[16,16,256]{2,1,0:T(8,128)(2,1)S(1)} %get-tuple-element.50), channel_id=1, replica_groups={{1,65,129,193,257,321,385,449,2,66,130,194,258,322,386,450},{3,67,131,1..., dimensions={0} | all-to-all | bytes 262144 | tf_op jit(solution)/shard_map/all_to_all | solution.py:521
  62.4 0.1 shard_map.124.own
  62.5 3.2 %all-gather = f32[16,256]{1,0:T(8,128)S(1)} all-gather(f32[8,256]{1,0:T(8,128)S(1)} %shard_map.124.own), channel_id=2, replica_groups=mesh['zh'=4,'core'=2,'zl'=2,'yh'=4,'yl'=2,'xh'=2,'xl'=2] {'xl'}, dimensions={0}, use_global_device_ids=true | all-gather | bytes 24576 | tf_op jit(solution)/shard_map/all_gather | solution.py:524
  65.7 1.3 %shard_map.125 = (bf16[8,16,128]{2,1,0:T(8,128)(2,1)S(1)}, f32[14,256]{1,0:T(8,128)S(1)}) custom-call(s32[8,128]{1,0:T(8,128)S(1)} %get-tuple-element.33.places, bf16[16,16,256]{2,1,0:T(8,128)(2,1)S(1)} %all_to_all.37.received, f32[8,256]{1,0:T(8,128)S(1)} %shard_map.124.own, f32[2,8,256]{2,1,0:T(8,128)S(1)} %bitcast.9, f32[20,256]{1,0:T(8,128)S(1)} %get-tuple-element.39.up, ...), custom_call_target="tpu_custom_call" | custom-call | tf_op jit(solution)/shard_map/pallas_call | solution.py:433
  67.0 11.1 %all_to_all.38.sums = bf16[8,16,128]{2,1,0:T(8,128)(2,1)S(1)} all-to-all(bf16[8,16,128]{2,1,0:T(8,128)(2,1)S(1)} %get-tuple-element.52), channel_id=1, replica_groups=mesh['zh'=4,'core'=2,'zl'=2,'yh'=4,'yl'=2,'xh'=2,'xl'=2] {'zh','core'}, dimensions={0} | all-to-all | bytes 65536 | tf_op jit(solution)/shard_map/all_to_all | solution.py:451
  78.1 1.4 %shard_map.126 = (f32[8,256]{1,0:T(8,128)S(1)}, bf16[32,8,256]{2,1,0:T(8,128)(2,1)S(1)}) custom-call(bf16[8,16,128]{2,1,0:T(8,128)(2,1)S(1)} %all_to_all.38.sums, f32[14,256]{1,0:T(8,128)S(1)} %get-tuple-element.53.moved, f32[20,256]{1,0:T(8,128)S(1)} %get-tuple-element.39.up, f32[20,256]{1,0:T(8,128)S(1)} %get-tuple-element.40.masks, ...), custom_call_target="tpu_custom_call" | custom-call | tf_op jit(solution)/shard_map/pallas_call | solution.py:433
  79.5 13.5 %all_to_all.39.received = bf16[32,8,256]{2,1,0:T(8,128)(2,1)S(1)} all-to-all(bf16[32,8,256]{2,1,0:T(8,128)(2,1)S(1)} %get-tuple-element.57), channel_id=1, replica_groups=mesh['zh'=4,'core'=2,'zl'=2,'yh'=4,'yl'=2,'xh'=2,'xl'=2] {'core','zl','y..., dimensions={0} | all-to-all | bytes 262144 | tf_op jit(solution)/shard_map/all_to_all | solution.py:451
  93.1 18.5 %all_to_all.40.received = bf16[16,8,256]{2,1,0:T(8,128)(2,1)S(1)} all-to-all(bf16[16,8,256]{2,1,0:T(8,128)(2,1)S(1)} %shard_map.127), channel_id=1, replica_groups=mesh['zh'=4,'core'=2,'zl'=2,'yh'=4,'yl'=2,'xh'=2,'xl'=2] {'zh','yh'}, dimensions={0} | all-to-all | bytes 131072 | tf_op jit(solution)/shard_map/all_to_all | solution.py:451
  111.5 0.1 shard_map.128
  111.6 11.8 %all_to_all.41.received = bf16[32,8,256]{2,1,0:T(8,128)(2,1)S(1)} all-to-all(bf16[32,8,256]{2,1,0:T(8,128)(2,1)S(1)} %shard_map.128), channel_id=1, replica_groups=mesh['zh'=4,'core'=2,'zl'=2,'yh'=4,'yl'=2,'xh'=2,'xl'=2] {'core','zl','y..., dimensions={0} | all-to-all | bytes 262144 | tf_op jit(solution)/shard_map/all_to_all | solution.py:451
  123.4 0.8 shard_map.129
  (2 shorter events, 0.1 us)
Async XLA Ops:
  2.5 10.5 %collective-permute-start = (bf16[368,256]{1,0:T(8,128)(2,1)}, bf16[368,256]{1,0:T(8,128)(2,1)S(1)}, u32[]{:S(2)}, u32[]{:S(2)}) collective-permute-start(bf16[368,256]{1,0:T(8,128)(2,1)} %get-tuple-element.34), channel_id=1, source_target_pairs={{0,1},{1,2},{2,3},{3,4},{4,5},{5,6},{6,7},{7,8},{8,9},{9,10},{10,1... | collective-permute-start | bytes 565256 | tf_op jit(solution)/shard_map/ppermute | solution.py:480
  6.5 6.6 %collective-permute-start.1 = (bf16[368,256]{1,0:T(8,128)(2,1)}, bf16[368,256]{1,0:T(8,128)(2,1)S(1)}, u32[]{:S(2)}, u32[]{:S(2)}) collective-permute-start(bf16[368,256]{1,0:T(8,128)(2,1)} %get-tuple-element.36), channel_id=1, source_target_pairs={{1,0},{2,1},{3,2},{4,3},{5,4},{6,5},{7,6},{8,7},{9,8},{10,9},{11,1... | collective-permute-start | bytes 565256 | tf_op jit(solution)/shard_map/ppermute | solution.py:481
  7.9 1.0 copy-start
  8.8 0.9 copy-start.1
  9.7 0.8 copy-start.2
  10.5 0.7 copy-start.3
  11.2 0.7 copy-start.4

commit v11 on v10

--- a/solution.py
+++ b/solution.py
@@ -144,13 +144,16 @@
         part[k] = value
 
 
-def pack_kernel(upstream, equilibrium, masks, measurement, saved, top, bottom, own_fields,
-                up_in, fixed_in, masks_in, snapshot_in, saved_in, sems):
+def pack_kernel(upstream, equilibrium, masks, measurement, saved, conv_first, conv_second,
+                conv_third, to_near, to_far, bundle, narrow, up_in, fixed_in, masks_in,
+                snapshot_in, saved_in, first_in, second_in, third_in, sems):
+    odd = lax.broadcast_in_dim(lax.axis_index(SPACE[-1]), (1, W), ()) == 1
     copies = [
         pltpu.make_async_copy(source, target, sems.at[k])
         for k, (source, target) in enumerate((
             (saved, saved_in), (upstream, up_in), (equilibrium, fixed_in), (masks, masks_in),
-            (measurement, snapshot_in)))
+            (measurement, snapshot_in), (conv_first, first_in), (conv_second, second_in),
+            (conv_third, third_in)))
     ]
     for copy in copies:
         copy.start()
@@ -165,35 +168,44 @@
     mask = by_frame(masks_in).astype(F32)
     snapshot = snapshot_in[...]
     for k, field in enumerate((up, mask, fixed, twice(snapshot))):
-        own_fields[k * R:(k + 1) * R, :] = field
+        narrow[k * R:(k + 1) * R, :] = field
+    narrow[4 * R:, :] = jnp.zeros((4 * R, LANES), F32)
+    narrow[4 * R:4 * R + 9, :C] = first_in[...].astype(F32)
+    narrow[6 * R:6 * R + 9, :C] = third_in[...].astype(F32)
+    for k in range(9):
+        at = R * C + (k // 4) * C
+        bundle[at:at + C, (k % 4) * C:(k % 4 + 1) * C] = second_in[k]
+    bundle[(R + 2) * C:, C:] = jnp.zeros((C, 3 * C), BF)
     fields = (*split_parts(up), *split_parts(fixed), mask.astype(BF),
               jnp.concatenate(split_parts(snapshot), axis=1))
     for k in range(0, len(fields), 2):
         pair = jnp.concatenate([field.astype(F32) for field in fields[k:k + 2]], axis=0).astype(BF)
         at = EDGE * C + k * R
-        top[at:at + 2 * R, :] = pair
-        bottom[at:at + 2 * R, :] = pair
+        to_near[at:at + 2 * R, :] = pair
+        to_far[at:at + 2 * R, :] = pair
     copies[0].wait()
     for frame in range(2):
         lanes = slice(frame * W, (frame + 1) * W)
-        rows = jnp.swapaxes(saved_in[frame].astype(F32), 0, 1).astype(BF).reshape(R * C, W)
-        top[:EDGE * C, lanes] = rows[:EDGE * C]
-        bottom[:EDGE * C, lanes] = rows[(R - EDGE) * C:]
-
-
-def stage_kernel(places, first, second, third, saved, own_fields, forward_w, third_w, second_w,
-                 first_w, gate2, hidden2, fields, table):
-    fields[...] = own_fields[...]
+        rows = jnp.swapaxes(saved_in[frame].astype(F32), 0, 1).reshape(R * C, W)
+        bundle[:R * C, lanes] = rows.astype(BF)
+        top = rows[:EDGE * C]
+        bottom = rows[(R - EDGE) * C:]
+        to_near[:EDGE * C, lanes] = jnp.where(odd, top, bottom).astype(BF)
+        to_far[:EDGE * C, lanes] = jnp.where(odd, bottom, top).astype(BF)
+
+
+def stage_kernel(places, bundle, narrow, forward_w, third_w, second_w, first_w, gate2, hidden2,
+                 fields, table):
+    fields[...] = narrow[:4 * R, :]
     for k in range(8):
         table[k:k + 1, :] = jnp.full((1, W), places[k], jnp.int32)
-    for frame in range(2):
-        lanes = slice(frame * W, (frame + 1) * W)
-        value = jnp.swapaxes(saved[frame].astype(F32), 0, 1).reshape(R * C, W)
+    for r in range(R):
+        value = saved_row(bundle, r).astype(F32)
         logistic, slope = slope_parts(value)
-        gate2[:, lanes] = slope
-        hidden2[:, lanes] = (value * logistic).astype(BF)
-    forward = first[...].astype(F32)
-    backward = third[...].astype(F32)
+        gate2[r * C:(r + 1) * C, :] = slope
+        hidden2[r * C:(r + 1) * C, :] = (value * logistic).astype(BF)
+    forward = narrow[4 * R:4 * R + 9, :C]
+    backward = narrow[6 * R:6 * R + 9, :C]
     pad = jnp.zeros((Q - 6, C), F32)
     ahead = []
     back = []
@@ -203,18 +215,20 @@
         row = backward[6 - 3 * i:9 - 3 * i]
         back += [row, row, pad]
         for j in range(3):
-            tile = second[3 * (2 - i) + j].astype(F32)
+            tap = 3 * (2 - i) + j
+            at = R * C + (tap // 4) * C
+            tile = bundle[at:at + C, (tap % 4) * C:(tap % 4 + 1) * C].astype(F32)
             second_w[j * C:(j + 1) * C, i * C:(i + 1) * C] = jnp.transpose(tile).astype(BF)
     forward_w[...] = jnp.transpose(jnp.concatenate(ahead, axis=0)).astype(BF)
     third_w[...] = jnp.transpose(jnp.concatenate(back, axis=0)).astype(BF)
     first_w[...] = jnp.concatenate([forward, jnp.zeros((Q - 9, C), F32)], axis=0).astype(BF)
 
 
-def unpack_kernel(step, low, own_fields, high, _, part, up, masks, base, fixed, snapshot):
+def unpack_kernel(step, places, near, far, own_fields, _, part, up, masks, base, fixed, snapshot):
     for k, target in enumerate((up, masks, fixed, snapshot)):
         target[HALO:HALO + R, :] = own_fields[k * R:(k + 1) * R, :]
-    for ref, at, first in ((low, 0, R - HALO), (high, HALO + R, 0)):
-        fields = ref[EDGE * C:EDGE * C + FIELDS * R, :].astype(F32)
+    for side, at, first in ((0, 0, R - HALO), (1, HALO + R, 0)):
+        fields = edge_rows(places, near, far, side, EDGE * C, FIELDS * R)
 
         def field(k):
             return fields[k * R:(k + 1) * R]
@@ -227,6 +241,12 @@
     base[...] = fixed[...] + step * masks[...] * snapshot[...]
 
 
+def edge_rows(places, near, far, side, at, count):
+    from_pair = twice(places[ODD:ODD + 1, :]) == 1 - side
+    return jnp.where(from_pair, near[side, at:at + count, :].astype(F32),
+                     far[at:at + count, :].astype(F32))
+
+
 def saved_row(ref, at):
     return ref[at * C:(at + 1) * C, :]
 
@@ -243,7 +263,7 @@
     return tuple(twice(places[k:k + 1, :]).astype(F32) for k in (BEFORE, AFTER))
 
 
-def first_kernel(step, places, sums, low, own, high, up, masks, base, third_w, second_w, first_w,
+def first_kernel(step, places, sums, near, far, own, up, masks, base, third_w, second_w, first_w,
                  forward_w, part, moved, gate2, gate1, hidden, inputs, copies, d2, d1, taps):
     before, after = ends(places)
     for k in range(EXT - 2):
@@ -251,8 +271,8 @@
         if HALO <= at < HALO + R:
             gate2[k * C:(k + 1) * C, :] = saved_row(own, at - HALO)
         else:
-            value = saved_row(low, k) if at < HALO else saved_row(high, at - HALO - R)
-            slope = slope_parts(value.astype(F32))[1]
+            side, row = (0, k) if at < HALO else (1, at - HALO - R)
+            slope = slope_parts(edge_rows(places, near, far, side, row * C, C))[1]
             gate2[k * C:(k + 1) * C, :] = keep_row(slope, at, before, after)
     frame_sum = gathered_sum(sums)[:EXT]
     denoiser_input = base[...] - step * masks[...] * twice(frame_sum)
@@ -458,8 +478,6 @@
     total_frames = 2 * frames
     step = 1.0 / total_frames
     scale = 1.0 / math.sqrt(total_frames * R * tiles * W)
-    forward = [(i, i + 1) for i in range(tiles - 1)]
-    backward = [(i + 1, i) for i in range(tiles - 1)]
     place = lax.axis_index(SPACE)
     odd = place % 2
     places = jnp.stack([place > 0, place < tiles - 1, odd, frames * (1 - odd),
@@ -472,27 +490,28 @@
     edge = ((EDGE * C + FIELDS * R, LANES), BF)
     fields = ((4 * R, LANES), F32)
     frame = ((2, R, W), F32)
-    top, bottom, own_fields = call(
-        pack_kernel, [edge, edge, fields],
-        [frame, frame, ((2, R, W), jnp.int32), ((R, W), F32), ((2, C, R, W), BF)],
-        upstream, equilibrium, coding_masks, measurement, saved_second,
-        specs=[hbm] * 5, sems=5, limit=60)
-    low = lax.ppermute(bottom, SPACE, forward)
-    high = lax.ppermute(top, SPACE, backward)
+    to_near, to_far, bundle, narrow_bundle = call(
+        pack_kernel, [edge, edge, (((R + 3) * C, LANES), BF), ((8 * R, LANES), F32)],
+        [frame, frame, ((2, R, W), jnp.int32), ((R, W), F32), ((2, C, R, W), BF), ((9, C), BF),
+         ((9, C, C), BF), ((9, C), BF)],
+        upstream, equilibrium, coding_masks, measurement, saved_second, conv_first, conv_second,
+        conv_third, specs=[hbm] * 8, sems=8, limit=60)
+    far = lax.ppermute(to_far, SPACE, [(k + side, k + 1 - side) for k in range(1, tiles - 1, 2)
+                                       for side in range(2)])
+    near = lax.all_gather(to_near, SPACE[-1])
 
     forward_w, third_w, second_w, first_w, gate2_own, hidden2, own_fields, table = call(
         stage_kernel,
         [((C, 3 * Q), BF), ((C, 3 * Q), BF), ((3 * C, 3 * C), BF), ((Q, C), BF),
          ((R * C, LANES), F32), ((R * C, LANES), BF), fields, ((8, W), jnp.int32)], [],
-        places, conv_first, conv_second, conv_third, saved_second, own_fields,
-        specs=[scalars] + [whole] * 5,
+        places, bundle, narrow_bundle, specs=[scalars] + [whole] * 2,
         cost=pl.CostEstimate(flops=2 * 10**6, bytes_accessed=10**6, transcendentals=0))
 
     ext = ((EXT, LANES), F32)
     part, up, masks, base = call(
         functools.partial(unpack_kernel, step),
         [((frames, 32, W), BF), ext, ext, ext], [ext, ext],
-        low, own_fields, high, gate2_own)
+        table, near, far, own_fields, gate2_own)
     sums = exchange(part, TM)
 
     narrow = EXT - 6
@@ -509,7 +528,7 @@
         wide_outs + [(((EXT - 2) * C, LANES), F32), (((EXT - 4) * C, LANES), F32),
                      ((R * C, LANES), BF), (((R + 2) * Q, LANES), BF)],
         [copies, d2, d1, taps],
-        table, sums, low, gate2_own, high, up, masks, base, *weights, forward_w)
+        table, sums, near, far, gate2_own, up, masks, base, *weights, forward_w)
     sums = exchange(part, TM)
 
     part, moved = call(

time: 125 us -> 125 us (level)
  blocking collectives: 105 us -> 112 us
  starting transfers between devices: 5.25 us -> 0.67 us
  local copies, waits for them, and re-layouts: 4.08 us -> 1.91 us
    all_gather x0 -> x1, blocking collectives: none -> 8.39 us  [per_device(): near = lax.all_gather(to_near, SPACE[-1])]
    ppermute x2 -> x1, starting transfers between devices: 5.25 us -> 0.67 us  [per_device(): lax.ppermute(to_far, SPACE, [(k + side, k + 1 - side) for k in range(1, t...]
    unnamed x10 -> x4, local copies, waits for them, and re-layouts: 3.99 us -> 1.83 us
  transfers between devices with their start and end apart: 2 -> 1, of which waited for: 0 -> 0; matrix products, arithmetic and copies ran while one was open for 0% -> 0% of each run, Pallas kernels for 1% -> 1%
where the time goes in v11:
time: 125 us
  blocking collectives  112 us (90%)
  Pallas kernels  10.1 us (8%)
  local copies, waits for them, and re-layouts  1.91 us (2%)
    all_to_all x6, blocking collectives, exchange(): return lax.all_to_all(value, axis, 0, 0, tiled=True)  84.7 us
    all_to_all x1, blocking collectives, per_device(): lax.all_to_all(part, TM + SPACE, 0, 0, axis_index_groups=groups, tiled=True)  15.3 us
    pallas_call x11, Pallas kernels, call(): pl.pallas_call(kernel, out_shape=[jax.ShapeDtypeStruct(shape, dtype) for...  10.1 us
    all_gather x1, blocking collectives, per_device(): near = lax.all_gather(to_near, SPACE[-1])  8.39 us
    all_gather x1, blocking collectives, per_device(): near = lax.all_gather(field, SPACE[-1])  3.22 us
  transfers between devices with their start and end apart: 1, of which 0 were waited for; matrix products, arithmetic and copies ran while one was open for 0% of the time, Pallas kernels for 1%

profile of v11, /device:TPU:1, one launch (start us, length us, event | category | flops | bytes accessed | tf_op | source)
XLA Modules:
  0.0 125.0 jit_solution(7656669443382146463)
XLA Ops:
  0.6 2.2 %shard_map.119 = (bf16[368,256]{1,0:T(8,128)(2,1)}, bf16[368,256]{1,0:T(8,128)(2,1)}, bf16[704,256]{1,0:T(8,128)(2,1)}, f32[64,256]{1,0:T(8,128)}) custom-call(f32[2,8,128]{2,1,0:T(8,128)} %upstream.1, f32[2,8,128]{2,1,0:T(8,128)} %equilibrium.1, s32[2,8,128]{2,1,0:T(8,128)} %masks.1, f32[8,128]{1,0:T(8,128)} %measurement.1, bf16[2,64,8,128]{3,2,1,0:T(8,128)(2,1)} %saved.1, ...), custom_call_target="tpu_custom_call" | custom-call | tf_op jit(solution)/shard_map/pallas_call | solution.py:453
  2.9 0.7 collective-permute-start
  3.6 0.1 stack.43.places
  3.7 0.0 copy-start
  3.7 1.0 copy-done
  4.7 0.0 copy-start.1
  4.7 0.8 copy-done.1
  5.5 1.1 shard_map.120
  6.6 8.4 %all-gather = bf16[736,256]{1,0:T(8,128)(2,1)S(1)} all-gather(bf16[368,256]{1,0:T(8,128)(2,1)} %get-tuple-element.36), channel_id=2, replica_groups=mesh['zh'=4,'core'=2,'zl'=2,'yh'=4,'yl'=2,'xh'=2,'xl'=2] {'xl'}, dimensions={0}, use_global_device_ids=true | all-gather | bytes 565248 | tf_op jit(solution)/shard_map/all_gather | solution.py:501
  15.0 0.0 collective-permute-done.far
  15.0 20.2 %all_to_all.35.sums = bf16[8,32,128]{2,1,0:T(8,128)(2,1)S(1)} all-to-all(bf16[8,32,128]{2,1,0:T(8,128)(2,1)S(1)} %get-tuple-element.40), channel_id=1, replica_groups=mesh['zh'=4,'core'=2,'zl'=2,'yh'=4,'yl'=2,'xh'=2,'xl'=2] {'zh','core'}, dimensions={0} | all-to-all | bytes 131072 | tf_op jit(solution)/shard_map/all_to_all | solution.py:471
  35.3 1.9 %shard_map.122 = (bf16[8,16,128]{2,1,0:T(8,128)(2,1)S(1)}, f32[14,256]{1,0:T(8,128)S(1)}, f32[1152,256]{1,0:T(8,128)S(1)}, f32[1024,256]{1,0:T(8,128)S(1)}, bf16...) custom-call(s32[8,128]{1,0:T(8,128)S(1)} %get-tuple-element.35.places, bf16[8,32,128]{2,1,0:T(8,128)(2,1)S(1)} %all_to_all.35.sums, ...), custom_call_target="tpu_custom_call" | custom-call | tf_op jit(solution)/shard_map/pallas_call | solution.py:453
  37.2 10.3 %all_to_all.36.sums = bf16[8,16,128]{2,1,0:T(8,128)(2,1)S(1)} all-to-all(bf16[8,16,128]{2,1,0:T(8,128)(2,1)S(1)} %get-tuple-element.48), channel_id=1, replica_groups=mesh['zh'=4,'core'=2,'zl'=2,'yh'=4,'yl'=2,'xh'=2,'xl'=2] {'zh','core'}, dimensions={0} | all-to-all | bytes 65536 | tf_op jit(solution)/shard_map/all_to_all | solution.py:471
  47.6 1.0 shard_map.123
  48.6 15.3 %all_to_all.37.received = bf16[16,16,256]{2,1,0:T(8,128)(2,1)S(1)} all-to-all(bf16[16,16,256]{2,1,0:T(8,128)(2,1)S(1)} %get-tuple-element.52), channel_id=1, replica_groups={{1,65,129,193,257,321,385,449,2,66,130,194,258,322,386,450},{3,67,131,1..., dimensions={0} | all-to-all | bytes 262144 | tf_op jit(solution)/shard_map/all_to_all | solution.py:540
  63.9 0.1 shard_map.124.own
  64.0 3.2 %all-gather.1 = f32[16,256]{1,0:T(8,128)S(1)} all-gather(f32[8,256]{1,0:T(8,128)S(1)} %shard_map.124.own), channel_id=3, replica_groups=mesh['zh'=4,'core'=2,'zl'=2,'yh'=4,'yl'=2,'xh'=2,'xl'=2] {'xl'}, dimensions={0}, use_global_device_ids=true | all-gather | bytes 24576 | tf_op jit(solution)/shard_map/all_gather | solution.py:543
  67.2 1.3 %shard_map.125 = (bf16[8,16,128]{2,1,0:T(8,128)(2,1)S(1)}, f32[14,256]{1,0:T(8,128)S(1)}) custom-call(s32[8,128]{1,0:T(8,128)S(1)} %get-tuple-element.35.places, bf16[16,16,256]{2,1,0:T(8,128)(2,1)S(1)} %all_to_all.37.received, f32[8,256]{1,0:T(8,128)S(1)} %shard_map.124.own, f32[2,8,256]{2,1,0:T(8,128)S(1)} %bitcast.12, ...), custom_call_target="tpu_custom_call" | custom-call | tf_op jit(solution)/shard_map/pallas_call | solution.py:453
  68.5 11.0 %all_to_all.38.sums = bf16[8,16,128]{2,1,0:T(8,128)(2,1)S(1)} all-to-all(bf16[8,16,128]{2,1,0:T(8,128)(2,1)S(1)} %get-tuple-element.54), channel_id=1, replica_groups=mesh['zh'=4,'core'=2,'zl'=2,'yh'=4,'yl'=2,'xh'=2,'xl'=2] {'zh','core'}, dimensions={0} | all-to-all | bytes 65536 | tf_op jit(solution)/shard_map/all_to_all | solution.py:471
  79.6 1.4 %shard_map.126 = (f32[8,256]{1,0:T(8,128)S(1)}, bf16[32,8,256]{2,1,0:T(8,128)(2,1)S(1)}) custom-call(bf16[8,16,128]{2,1,0:T(8,128)(2,1)S(1)} %all_to_all.38.sums, f32[14,256]{1,0:T(8,128)S(1)} %get-tuple-element.55.moved, f32[20,256]{1,0:T(8,128)S(1)} %get-tuple-element.41.up, f32[20,256]{1,0:T(8,128)S(1)} %get-tuple-element.42.masks, ...), custom_call_target="tpu_custom_call" | custom-call | tf_op jit(solution)/shard_map/pallas_call | solution.py:453
  81.0 14.1 %all_to_all.39.received = bf16[32,8,256]{2,1,0:T(8,128)(2,1)S(1)} all-to-all(bf16[32,8,256]{2,1,0:T(8,128)(2,1)S(1)} %get-tuple-element.59), channel_id=1, replica_groups=mesh['zh'=4,'core'=2,'zl'=2,'yh'=4,'yl'=2,'xh'=2,'xl'=2] {'core','zl','y..., dimensions={0} | all-to-all | bytes 262144 | tf_op jit(solution)/shard_map/all_to_all | solution.py:471
  95.1 17.2 %all_to_all.40.received = bf16[16,8,256]{2,1,0:T(8,128)(2,1)S(1)} all-to-all(bf16[16,8,256]{2,1,0:T(8,128)(2,1)S(1)} %shard_map.127), channel_id=1, replica_groups=mesh['zh'=4,'core'=2,'zl'=2,'yh'=4,'yl'=2,'xh'=2,'xl'=2] {'zh','yh'}, dimensions={0} | all-to-all | bytes 131072 | tf_op jit(solution)/shard_map/all_to_all | solution.py:471
  112.3 0.1 shard_map.128
  112.4 11.8 %all_to_all.41.received = bf16[32,8,256]{2,1,0:T(8,128)(2,1)S(1)} all-to-all(bf16[32,8,256]{2,1,0:T(8,128)(2,1)S(1)} %shard_map.128), channel_id=1, replica_groups=mesh['zh'=4,'core'=2,'zl'=2,'yh'=4,'yl'=2,'xh'=2,'xl'=2] {'core','zl','y..., dimensions={0} | all-to-all | bytes 262144 | tf_op jit(solution)/shard_map/all_to_all | solution.py:471
  124.1 0.8 shard_map.129
  (2 shorter events, 0.1 us)
Async XLA Ops:
  2.9 12.1 %collective-permute-start = (bf16[368,256]{1,0:T(8,128)(2,1)}, bf16[368,256]{1,0:T(8,128)(2,1)S(1)}, u32[]{:S(2)}, u32[]{:S(2)}) collective-permute-start(bf16[368,256]{1,0:T(8,128)(2,1)} %get-tuple-element.37), channel_id=1, source_target_pairs={{1,2},{2,1},{3,4},{4,3},{5,6},{6,5},{7,8},{8,7},{9,10},{10,9},{11,... | collective-permute-start | bytes 565256 | tf_op jit(solution)/shard_map/ppermute | solution.py:499
  3.7 1.0 copy-start
  4.7 0.8 copy-start.1

commit v12 on v11

--- a/solution.py
+++ b/solution.py
@@ -16,6 +16,9 @@
 HALO = 6
 EXT = R + 2 * HALO
 EDGE = HALO - 1
+FIELDS_AT = (R + 3) * C
+FIRST_AT = FIELDS_AT + 6 * R
+THIRD_AT = FIRST_AT + 16
 FIELDS = 6
 Q = 16
 PIECE = 32
@@ -145,7 +148,7 @@
 
 
 def pack_kernel(upstream, equilibrium, masks, measurement, saved, conv_first, conv_second,
-                conv_third, to_near, to_far, bundle, narrow, up_in, fixed_in, masks_in,
+                conv_third, to_near, to_far, bundle, up_in, fixed_in, masks_in,
                 snapshot_in, saved_in, first_in, second_in, third_in, sems):
     odd = lax.broadcast_in_dim(lax.axis_index(SPACE[-1]), (1, W), ()) == 1
     copies = [
@@ -167,15 +170,14 @@
     fixed = by_frame(fixed_in)
     mask = by_frame(masks_in).astype(F32)
     snapshot = snapshot_in[...]
-    for k, field in enumerate((up, mask, fixed, twice(snapshot))):
-        narrow[k * R:(k + 1) * R, :] = field
-    narrow[4 * R:, :] = jnp.zeros((4 * R, LANES), F32)
-    narrow[4 * R:4 * R + 9, :C] = first_in[...].astype(F32)
-    narrow[6 * R:6 * R + 9, :C] = third_in[...].astype(F32)
+    for at, ref in ((FIRST_AT, first_in), (THIRD_AT, third_in)):
+        taps = jnp.concatenate([ref[...].astype(F32), jnp.zeros((Q - 9, C), F32)], axis=0)
+        taps = jnp.concatenate([taps, jnp.zeros((Q, 3 * C), F32)], axis=1)
+        bundle[at:at + Q, :] = taps.astype(BF)
     for k in range(9):
         at = R * C + (k // 4) * C
         bundle[at:at + C, (k % 4) * C:(k % 4 + 1) * C] = second_in[k]
-    bundle[(R + 2) * C:, C:] = jnp.zeros((C, 3 * C), BF)
+    bundle[(R + 2) * C:FIELDS_AT, C:] = jnp.zeros((C, 3 * C), BF)
     fields = (*split_parts(up), *split_parts(fixed), mask.astype(BF),
               jnp.concatenate(split_parts(snapshot), axis=1))
     for k in range(0, len(fields), 2):
@@ -183,6 +185,7 @@
         at = EDGE * C + k * R
         to_near[at:at + 2 * R, :] = pair
         to_far[at:at + 2 * R, :] = pair
+        bundle[FIELDS_AT + k * R:FIELDS_AT + (k + 2) * R, :] = pair
     copies[0].wait()
     for frame in range(2):
         lanes = slice(frame * W, (frame + 1) * W)
@@ -194,18 +197,29 @@
         to_far[:EDGE * C, lanes] = jnp.where(odd, bottom, top).astype(BF)
 
 
-def stage_kernel(places, bundle, narrow, forward_w, third_w, second_w, first_w, gate2, hidden2,
+def stage_kernel(frames, tiles, bundle, forward_w, third_w, second_w, first_w, gate2, hidden2,
                  fields, table):
-    fields[...] = narrow[:4 * R, :]
-    for k in range(8):
-        table[k:k + 1, :] = jnp.full((1, W), places[k], jnp.int32)
+    place = lax.axis_index(SPACE)
+    odd = lax.axis_index(SPACE[-1])
+    entries = {BEFORE: jnp.minimum(place, 1), AFTER: jnp.minimum(tiles - 1 - place, 1), ODD: odd,
+               OWN_HALF: frames * (1 - odd), THEIR_ENTRY: frames * odd + lax.axis_index(TM),
+               THEIR_HALF: frames * odd, NEAR_AT: lax.axis_index(NEAR[1:]),
+               FAR_AT: lax.axis_index(FAR[1:])}
+    for k, entry in entries.items():
+        table[k:k + 1, :] = lax.broadcast_in_dim(entry.astype(jnp.int32), (1, W), ())
+    rows = bundle[FIELDS_AT:FIRST_AT, :].astype(F32)
+    pair = rows[5 * R:]
+    for k, field in enumerate((rows[:R] + rows[R:2 * R], rows[4 * R:5 * R],
+                               rows[2 * R:3 * R] + rows[3 * R:4 * R],
+                               twice(pair[:, :W] + pair[:, W:]))):
+        fields[k * R:(k + 1) * R, :] = field
     for r in range(R):
         value = saved_row(bundle, r).astype(F32)
         logistic, slope = slope_parts(value)
         gate2[r * C:(r + 1) * C, :] = slope
         hidden2[r * C:(r + 1) * C, :] = (value * logistic).astype(BF)
-    forward = narrow[4 * R:4 * R + 9, :C]
-    backward = narrow[6 * R:6 * R + 9, :C]
+    forward = bundle[FIRST_AT:FIRST_AT + Q, :].astype(F32)[:9, :C]
+    backward = bundle[THIRD_AT:THIRD_AT + Q, :].astype(F32)[:9, :C]
     pad = jnp.zeros((Q - 6, C), F32)
     ahead = []
     back = []
@@ -478,20 +492,13 @@
     total_frames = 2 * frames
     step = 1.0 / total_frames
     scale = 1.0 / math.sqrt(total_frames * R * tiles * W)
-    place = lax.axis_index(SPACE)
-    odd = place % 2
-    places = jnp.stack([place > 0, place < tiles - 1, odd, frames * (1 - odd),
-                        frames * odd + lax.axis_index(TM), frames * odd,
-                        lax.axis_index(NEAR[1:]), lax.axis_index(FAR[1:])]).astype(jnp.int32)
-
     hbm = pl.BlockSpec(memory_space=pltpu.HBM)
     whole = pl.BlockSpec(memory_space=pltpu.VMEM)
-    scalars = pl.BlockSpec(memory_space=pltpu.SMEM)
     edge = ((EDGE * C + FIELDS * R, LANES), BF)
     fields = ((4 * R, LANES), F32)
     frame = ((2, R, W), F32)
-    to_near, to_far, bundle, narrow_bundle = call(
-        pack_kernel, [edge, edge, (((R + 3) * C, LANES), BF), ((8 * R, LANES), F32)],
+    to_near, to_far, bundle = call(
+        pack_kernel, [edge, edge, ((THIRD_AT + Q, LANES), BF)],
         [frame, frame, ((2, R, W), jnp.int32), ((R, W), F32), ((2, C, R, W), BF), ((9, C), BF),
          ((9, C, C), BF), ((9, C), BF)],
         upstream, equilibrium, coding_masks, measurement, saved_second, conv_first, conv_second,
@@ -501,10 +508,10 @@
     near = lax.all_gather(to_near, SPACE[-1])
 
     forward_w, third_w, second_w, first_w, gate2_own, hidden2, own_fields, table = call(
-        stage_kernel,
+        functools.partial(stage_kernel, frames, tiles),
         [((C, 3 * Q), BF), ((C, 3 * Q), BF), ((3 * C, 3 * C), BF), ((Q, C), BF),
          ((R * C, LANES), F32), ((R * C, LANES), BF), fields, ((8, W), jnp.int32)], [],
-        places, bundle, narrow_bundle, specs=[scalars] + [whole] * 2,
+        bundle,
         cost=pl.CostEstimate(flops=2 * 10**6, bytes_accessed=10**6, transcendentals=0))
 
     ext = ((EXT, LANES), F32)

time: 125 us -> 124 us (level)
  transfers between devices with their start and end apart: 1 -> 1, of which waited for: 0 -> 0; matrix products, arithmetic and copies ran while one was open for 0% -> 0% of each run, Pallas kernels for 1% -> 0%
where the time goes in v12:
time: 124 us; the launch traced here: 123 us
  blocking collectives  112 us (90%)
  Pallas kernels  9.52 us (8%)
    all_to_all x6, blocking collectives, exchange(): return lax.all_to_all(value, axis, 0, 0, tiled=True)  85.3 us
    all_to_all x1, blocking collectives, per_device(): lax.all_to_all(part, TM + SPACE, 0, 0, axis_index_groups=groups, tiled=True)  14.7 us
    pallas_call x11, Pallas kernels, call(): pl.pallas_call(kernel, out_shape=[jax.ShapeDtypeStruct(shape, dtype) for...  9.52 us
    all_gather x1, blocking collectives, per_device(): near = lax.all_gather(to_near, SPACE[-1])  8.39 us
    all_gather x1, blocking collectives, per_device(): near = lax.all_gather(field, SPACE[-1])  3.22 us
  transfers between devices with their start and end apart: 1, of which 0 were waited for; matrix products, arithmetic and copies ran while one was open for 0% of the time, Pallas kernels for 0%

profile of v12, /device:TPU:1, one launch (start us, length us, event | category | flops | bytes accessed | tf_op | source)
XLA Modules:
  0.0 123.5 jit_solution(16161735431111596898)
XLA Ops:
  0.6 2.3 %shard_map.119 = (bf16[368,256]{1,0:T(8,128)(2,1)}, bf16[368,256]{1,0:T(8,128)(2,1)}, bf16[784,256]{1,0:T(8,128)(2,1)}) custom-call(f32[2,8,128]{2,1,0:T(8,128)} %upstream.1, f32[2,8,128]{2,1,0:T(8,128)} %equilibrium.1, s32[2,8,128]{2,1,0:T(8,128)} %masks.1, f32[8,128]{1,0:T(8,128)} %measurement.1, bf16[2,64,8,128]{3,2,1,0:T(8,128)(2,1)} %saved.1, ...), custom_call_target="tpu_custom_call" | custom-call | tf_op jit(solution)/shard_map/pallas_call | solution.py:467
  2.9 0.7 collective-permute-start
  3.6 0.0 copy-start
  3.6 1.0 copy-done
  4.6 0.6 shard_map.120
  5.1 8.4 %all-gather = bf16[736,256]{1,0:T(8,128)(2,1)S(1)} all-gather(bf16[368,256]{1,0:T(8,128)(2,1)} %get-tuple-element.34), channel_id=2, replica_groups=mesh['zh'=4,'core'=2,'zl'=2,'yh'=4,'yl'=2,'xh'=2,'xl'=2] {'xl'}, dimensions={0}, use_global_device_ids=true | all-gather | bytes 565248 | tf_op jit(solution)/shard_map/all_gather | solution.py:508
  13.5 0.0 collective-permute-done.far
  13.6 20.2 %all_to_all.35.sums = bf16[8,32,128]{2,1,0:T(8,128)(2,1)S(1)} all-to-all(bf16[8,32,128]{2,1,0:T(8,128)(2,1)S(1)} %get-tuple-element.38), channel_id=1, replica_groups=mesh['zh'=4,'core'=2,'zl'=2,'yh'=4,'yl'=2,'xh'=2,'xl'=2] {'zh','core'}, dimensions={0} | all-to-all | bytes 131072 | tf_op jit(solution)/shard_map/all_to_all | solution.py:485
  33.8 1.9 %shard_map.122 = (bf16[8,16,128]{2,1,0:T(8,128)(2,1)S(1)}, f32[14,256]{1,0:T(8,128)S(1)}, f32[1152,256]{1,0:T(8,128)S(1)}, f32[1024,256]{1,0:T(8,128)S(1)}, bf16...) custom-call(s32[8,128]{1,0:T(8,128)S(1)} %get-tuple-element.33.places, bf16[8,32,128]{2,1,0:T(8,128)(2,1)S(1)} %all_to_all.35.sums, ...), custom_call_target="tpu_custom_call" | custom-call | tf_op jit(solution)/shard_map/pallas_call | solution.py:467
  35.8 10.3 %all_to_all.36.sums = bf16[8,16,128]{2,1,0:T(8,128)(2,1)S(1)} all-to-all(bf16[8,16,128]{2,1,0:T(8,128)(2,1)S(1)} %get-tuple-element.46), channel_id=1, replica_groups=mesh['zh'=4,'core'=2,'zl'=2,'yh'=4,'yl'=2,'xh'=2,'xl'=2] {'zh','core'}, dimensions={0} | all-to-all | bytes 65536 | tf_op jit(solution)/shard_map/all_to_all | solution.py:485
  46.1 1.0 shard_map.123
  47.1 14.7 %all_to_all.37.received = bf16[16,16,256]{2,1,0:T(8,128)(2,1)S(1)} all-to-all(bf16[16,16,256]{2,1,0:T(8,128)(2,1)S(1)} %get-tuple-element.50), channel_id=1, replica_groups={{1,65,129,193,257,321,385,449,2,66,130,194,258,322,386,450},{3,67,131,1..., dimensions={0} | all-to-all | bytes 262144 | tf_op jit(solution)/shard_map/all_to_all | solution.py:547
  61.8 0.1 shard_map.124.own
  61.9 3.2 %all-gather.1 = f32[16,256]{1,0:T(8,128)S(1)} all-gather(f32[8,256]{1,0:T(8,128)S(1)} %shard_map.124.own), channel_id=3, replica_groups=mesh['zh'=4,'core'=2,'zl'=2,'yh'=4,'yl'=2,'xh'=2,'xl'=2] {'xl'}, dimensions={0}, use_global_device_ids=true | all-gather | bytes 24576 | tf_op jit(solution)/shard_map/all_gather | solution.py:550
  65.1 1.3 %shard_map.125 = (bf16[8,16,128]{2,1,0:T(8,128)(2,1)S(1)}, f32[14,256]{1,0:T(8,128)S(1)}) custom-call(s32[8,128]{1,0:T(8,128)S(1)} %get-tuple-element.33.places, bf16[16,16,256]{2,1,0:T(8,128)(2,1)S(1)} %all_to_all.37.received, f32[8,256]{1,0:T(8,128)S(1)} %shard_map.124.own, f32[2,8,256]{2,1,0:T(8,128)S(1)} %bitcast.4, f32[20,256]{1,0:T(8,128)S(1)} %get-tuple-element.39.up, ...), custom_call_target="tpu_custom_call" | custom-call | tf_op jit(solution)/shard_map/pallas_call | solution.py:467
  66.4 11.3 %all_to_all.38.sums = bf16[8,16,128]{2,1,0:T(8,128)(2,1)S(1)} all-to-all(bf16[8,16,128]{2,1,0:T(8,128)(2,1)S(1)} %get-tuple-element.52), channel_id=1, replica_groups=mesh['zh'=4,'core'=2,'zl'=2,'yh'=4,'yl'=2,'xh'=2,'xl'=2] {'zh','core'}, dimensions={0} | all-to-all | bytes 65536 | tf_op jit(solution)/shard_map/all_to_all | solution.py:485
  77.7 1.4 %shard_map.126 = (f32[8,256]{1,0:T(8,128)S(1)}, bf16[32,8,256]{2,1,0:T(8,128)(2,1)S(1)}) custom-call(bf16[8,16,128]{2,1,0:T(8,128)(2,1)S(1)} %all_to_all.38.sums, f32[14,256]{1,0:T(8,128)S(1)} %get-tuple-element.53.moved, f32[20,256]{1,0:T(8,128)S(1)} %get-tuple-element.39.up, f32[20,256]{1,0:T(8,128)S(1)} %get-tuple-element.40.masks, ...), custom_call_target="tpu_custom_call" | custom-call | tf_op jit(solution)/shard_map/pallas_call | solution.py:467
  79.1 14.5 %all_to_all.39.received = bf16[32,8,256]{2,1,0:T(8,128)(2,1)S(1)} all-to-all(bf16[32,8,256]{2,1,0:T(8,128)(2,1)S(1)} %get-tuple-element.57), channel_id=1, replica_groups=mesh['zh'=4,'core'=2,'zl'=2,'yh'=4,'yl'=2,'xh'=2,'xl'=2] {'core','zl','y..., dimensions={0} | all-to-all | bytes 262144 | tf_op jit(solution)/shard_map/all_to_all | solution.py:485
  93.6 17.2 %all_to_all.40.received = bf16[16,8,256]{2,1,0:T(8,128)(2,1)S(1)} all-to-all(bf16[16,8,256]{2,1,0:T(8,128)(2,1)S(1)} %shard_map.127), channel_id=1, replica_groups=mesh['zh'=4,'core'=2,'zl'=2,'yh'=4,'yl'=2,'xh'=2,'xl'=2] {'zh','yh'}, dimensions={0} | all-to-all | bytes 131072 | tf_op jit(solution)/shard_map/all_to_all | solution.py:485
  110.8 0.1 shard_map.128
  110.9 11.8 %all_to_all.41.received = bf16[32,8,256]{2,1,0:T(8,128)(2,1)S(1)} all-to-all(bf16[32,8,256]{2,1,0:T(8,128)(2,1)S(1)} %shard_map.128), channel_id=1, replica_groups=mesh['zh'=4,'core'=2,'zl'=2,'yh'=4,'yl'=2,'xh'=2,'xl'=2] {'core','zl','y..., dimensions={0} | all-to-all | bytes 262144 | tf_op jit(solution)/shard_map/all_to_all | solution.py:485
  122.6 0.8 shard_map.129
  (2 shorter events, 0.1 us)
Async XLA Ops:
  2.9 10.6 %collective-permute-start = (bf16[368,256]{1,0:T(8,128)(2,1)}, bf16[368,256]{1,0:T(8,128)(2,1)S(1)}, u32[]{:S(2)}, u32[]{:S(2)}) collective-permute-start(bf16[368,256]{1,0:T(8,128)(2,1)} %get-tuple-element.35), channel_id=1, source_target_pairs={{1,2},{2,1},{3,4},{4,3},{5,6},{6,5},{7,8},{8,7},{9,10},{10,9},{11,... | collective-permute-start | bytes 565256 | tf_op jit(solution)/shard_map/ppermute | solution.py:506
  3.6 1.0 copy-start

commit v13 on v12

--- a/solution.py
+++ b/solution.py
@@ -342,10 +342,11 @@
     return jnp.concatenate([half[:, :W], half[:, W:]], axis=0)
 
 
-def update_kernel(step, places, received, moved, up, masks, out):
+def update_kernel(step, places, received, moved, up, masks, out, sent):
     totals = pair_total(received, places[OWN_HALF, 0])
     out[...] = (up[HALO:HALO + R, :] + moved[...]
                 - step * masks[HALO:HALO + R, :] * twice(totals))
+    sent[...] = out[...].astype(BF)
 
 
 def third_kernel(step, places, received, own, near, up, masks, gate2, gate1, third_w,
@@ -360,9 +361,9 @@
     high = (up[after_rows, :] + theirs[:HALO]
             - step * masks[after_rows, :] * totals[:HALO]) * after
     odd = twice(places[ODD:ODD + 1, :]) == 1
-    whole[0:HALO, :] = jnp.where(odd, near[0, R - HALO:, :], low)
+    whole[0:HALO, :] = jnp.where(odd, near[0].astype(F32)[R - HALO:], low)
     whole[HALO:HALO + R, :] = own[...]
-    whole[HALO + R:, :] = jnp.where(odd, high, near[1, :HALO, :])
+    whole[HALO + R:, :] = jnp.where(odd, high, near[1].astype(F32)[:HALO])
     field = adjoint_map(0, whole[...], gate2, gate1, third_w[...], second_w[...], first_w[...],
                         copies, d2, d1, taps)
     finish_wide(field, before, after, masks, part, moved)
@@ -517,7 +518,7 @@
     ext = ((EXT, LANES), F32)
     part, up, masks, base = call(
         functools.partial(unpack_kernel, step),
-        [((frames, 32, W), BF), ext, ext, ext], [ext, ext],
+        [((frames, 24, W), BF), ext, ext, ext], [ext, ext],
         table, near, far, own_fields, gate2_own)
     sums = exchange(part, TM)
 
@@ -545,9 +546,10 @@
     groups = [[t * tiles + (k + side) % tiles for side in range(2) for t in range(frames)]
               for k in range(1, tiles, 2)]
     received = lax.all_to_all(part, TM + SPACE, 0, 0, axis_index_groups=groups, tiled=True)
-    field, = call(functools.partial(update_kernel, step), [((R, LANES), F32)], [],
+    field, sent = call(functools.partial(update_kernel, step),
+                       [((R, LANES), F32), ((R, LANES), BF)], [],
                   table, received, moved, up, masks)
-    near = lax.all_gather(field, SPACE[-1])
+    near = lax.all_gather(sent, SPACE[-1])
     part, moved = call(
         functools.partial(third_kernel, step), wide_outs, [copies, d2, d1, taps, ext],
         table, received, field, near, up, masks, gate2, gate1, *weights)

time: 124 us -> 124 us (level)
  no operation moved by 1% of the time
where the time goes in v13:
time: 124 us; the launch traced here: 123 us
  blocking collectives  111 us (90%)
  Pallas kernels  9.54 us (8%)
    all_to_all x6, blocking collectives, exchange(): return lax.all_to_all(value, axis, 0, 0, tiled=True)  85 us
    all_to_all x1, blocking collectives, per_device(): lax.all_to_all(part, TM + SPACE, 0, 0, axis_index_groups=groups, tiled=True)  14.8 us
    pallas_call x11, Pallas kernels, call(): pl.pallas_call(kernel, out_shape=[jax.ShapeDtypeStruct(shape, dtype) for...  9.54 us
    all_gather x1, blocking collectives, per_device(): near = lax.all_gather(to_near, SPACE[-1])  8.39 us
    all_gather x1, blocking collectives, per_device(): near = lax.all_gather(sent, SPACE[-1])  3.19 us
  transfers between devices with their start and end apart: 1, of which 0 were waited for; matrix products, arithmetic and copies ran while one was open for 0% of the time, Pallas kernels for 0%

profile of v13, /device:TPU:1, one launch (start us, length us, event | category | flops | bytes accessed | tf_op | source)
XLA Modules:
  0.0 123.3 jit_solution(14459707007789433757)
XLA Ops:
  0.6 2.3 %shard_map.119 = (bf16[368,256]{1,0:T(8,128)(2,1)}, bf16[368,256]{1,0:T(8,128)(2,1)}, bf16[784,256]{1,0:T(8,128)(2,1)}) custom-call(f32[2,8,128]{2,1,0:T(8,128)} %upstream.1, f32[2,8,128]{2,1,0:T(8,128)} %equilibrium.1, s32[2,8,128]{2,1,0:T(8,128)} %masks.1, f32[8,128]{1,0:T(8,128)} %measurement.1, bf16[2,64,8,128]{3,2,1,0:T(8,128)(2,1)} %saved.1, ...), custom_call_target="tpu_custom_call" | custom-call | tf_op jit(solution)/shard_map/pallas_call | solution.py:468
  2.9 0.7 collective-permute-start
  3.6 0.0 copy-start
  3.6 1.0 copy-done
  4.6 0.6 shard_map.120
  5.1 8.4 %all-gather = bf16[736,256]{1,0:T(8,128)(2,1)S(1)} all-gather(bf16[368,256]{1,0:T(8,128)(2,1)} %get-tuple-element.36), channel_id=2, replica_groups=mesh['zh'=4,'core'=2,'zl'=2,'yh'=4,'yl'=2,'xh'=2,'xl'=2] {'xl'}, dimensions={0}, use_global_device_ids=true | all-gather | bytes 565248 | tf_op jit(solution)/shard_map/all_gather | solution.py:509
  13.5 0.0 collective-permute-done.far
  13.6 20.1 %all_to_all.35.sums = bf16[8,24,128]{2,1,0:T(8,128)(2,1)S(1)} all-to-all(bf16[8,24,128]{2,1,0:T(8,128)(2,1)S(1)} %get-tuple-element.40), channel_id=1, replica_groups=mesh['zh'=4,'core'=2,'zl'=2,'yh'=4,'yl'=2,'xh'=2,'xl'=2] {'zh','core'}, dimensions={0} | all-to-all | bytes 98304 | tf_op jit(solution)/shard_map/all_to_all | solution.py:486
  33.7 1.9 %shard_map.122 = (bf16[8,16,128]{2,1,0:T(8,128)(2,1)S(1)}, f32[14,256]{1,0:T(8,128)S(1)}, f32[1152,256]{1,0:T(8,128)S(1)}, f32[1024,256]{1,0:T(8,128)S(1)}, bf16...) custom-call(s32[8,128]{1,0:T(8,128)S(1)} %get-tuple-element.35.places, bf16[8,24,128]{2,1,0:T(8,128)(2,1)S(1)} %all_to_all.35.sums, ...), custom_call_target="tpu_custom_call" | custom-call | tf_op jit(solution)/shard_map/pallas_call | solution.py:468
  35.6 10.3 %all_to_all.36.sums = bf16[8,16,128]{2,1,0:T(8,128)(2,1)S(1)} all-to-all(bf16[8,16,128]{2,1,0:T(8,128)(2,1)S(1)} %get-tuple-element.48), channel_id=1, replica_groups=mesh['zh'=4,'core'=2,'zl'=2,'yh'=4,'yl'=2,'xh'=2,'xl'=2] {'zh','core'}, dimensions={0} | all-to-all | bytes 65536 | tf_op jit(solution)/shard_map/all_to_all | solution.py:486
  46.0 1.0 shard_map.123
  47.0 14.8 %all_to_all.37.received = bf16[16,16,256]{2,1,0:T(8,128)(2,1)S(1)} all-to-all(bf16[16,16,256]{2,1,0:T(8,128)(2,1)S(1)} %get-tuple-element.52), channel_id=1, replica_groups={{1,65,129,193,257,321,385,449,2,66,130,194,258,322,386,450},{3,67,131,1..., dimensions={0} | all-to-all | bytes 262144 | tf_op jit(solution)/shard_map/all_to_all | solution.py:548
  61.8 0.1 shard_map.124
  61.9 3.2 %all-gather.1 = bf16[16,256]{1,0:T(8,128)(2,1)S(1)} all-gather(bf16[8,256]{1,0:T(8,128)(2,1)S(1)} %get-tuple-element.55), channel_id=3, replica_groups=mesh['zh'=4,'core'=2,'zl'=2,'yh'=4,'yl'=2,'xh'=2,'xl'=2] {'xl'}, dimensions={0}, use_global_device_ids=true | all-gather | bytes 12288 | tf_op jit(solution)/shard_map/all_gather | solution.py:552
  65.0 1.3 %shard_map.125 = (bf16[8,16,128]{2,1,0:T(8,128)(2,1)S(1)}, f32[14,256]{1,0:T(8,128)S(1)}) custom-call(s32[8,128]{1,0:T(8,128)S(1)} %get-tuple-element.35.places, bf16[16,16,256]{2,1,0:T(8,128)(2,1)S(1)} %all_to_all.37.received, f32[8,256]{1,0:T(8,128)S(1)} %get-tuple-element.54.own, bf16[2,8,256]{2,1,0:T(8,128)(2,1)S(1)} %bitcast.4, ...), custom_call_target="tpu_custom_call" | custom-call | tf_op jit(solution)/shard_map/pallas_call | solution.py:468
  66.4 11.2 %all_to_all.38.sums = bf16[8,16,128]{2,1,0:T(8,128)(2,1)S(1)} all-to-all(bf16[8,16,128]{2,1,0:T(8,128)(2,1)S(1)} %get-tuple-element.56), channel_id=1, replica_groups=mesh['zh'=4,'core'=2,'zl'=2,'yh'=4,'yl'=2,'xh'=2,'xl'=2] {'zh','core'}, dimensions={0} | all-to-all | bytes 65536 | tf_op jit(solution)/shard_map/all_to_all | solution.py:486
  77.6 1.4 %shard_map.126 = (f32[8,256]{1,0:T(8,128)S(1)}, bf16[32,8,256]{2,1,0:T(8,128)(2,1)S(1)}) custom-call(bf16[8,16,128]{2,1,0:T(8,128)(2,1)S(1)} %all_to_all.38.sums, f32[14,256]{1,0:T(8,128)S(1)} %get-tuple-element.57.moved, f32[20,256]{1,0:T(8,128)S(1)} %get-tuple-element.41.up, f32[20,256]{1,0:T(8,128)S(1)} %get-tuple-element.42.masks, ...), custom_call_target="tpu_custom_call" | custom-call | tf_op jit(solution)/shard_map/pallas_call | solution.py:468
  79.0 14.4 %all_to_all.39.received = bf16[32,8,256]{2,1,0:T(8,128)(2,1)S(1)} all-to-all(bf16[32,8,256]{2,1,0:T(8,128)(2,1)S(1)} %get-tuple-element.61), channel_id=1, replica_groups=mesh['zh'=4,'core'=2,'zl'=2,'yh'=4,'yl'=2,'xh'=2,'xl'=2] {'core','zl','y..., dimensions={0} | all-to-all | bytes 262144 | tf_op jit(solution)/shard_map/all_to_all | solution.py:486
  93.5 17.2 %all_to_all.40.received = bf16[16,8,256]{2,1,0:T(8,128)(2,1)S(1)} all-to-all(bf16[16,8,256]{2,1,0:T(8,128)(2,1)S(1)} %shard_map.127), channel_id=1, replica_groups=mesh['zh'=4,'core'=2,'zl'=2,'yh'=4,'yl'=2,'xh'=2,'xl'=2] {'zh','yh'}, dimensions={0} | all-to-all | bytes 131072 | tf_op jit(solution)/shard_map/all_to_all | solution.py:486
  110.6 0.1 shard_map.128
  110.7 11.8 %all_to_all.41.received = bf16[32,8,256]{2,1,0:T(8,128)(2,1)S(1)} all-to-all(bf16[32,8,256]{2,1,0:T(8,128)(2,1)S(1)} %shard_map.128), channel_id=1, replica_groups=mesh['zh'=4,'core'=2,'zl'=2,'yh'=4,'yl'=2,'xh'=2,'xl'=2] {'core','zl','y..., dimensions={0} | all-to-all | bytes 262144 | tf_op jit(solution)/shard_map/all_to_all | solution.py:486
  122.5 0.8 shard_map.129
  (2 shorter events, 0.1 us)
Async XLA Ops:
  2.9 10.6 %collective-permute-start = (bf16[368,256]{1,0:T(8,128)(2,1)}, bf16[368,256]{1,0:T(8,128)(2,1)S(1)}, u32[]{:S(2)}, u32[]{:S(2)}) collective-permute-start(bf16[368,256]{1,0:T(8,128)(2,1)} %get-tuple-element.37), channel_id=1, source_target_pairs={{1,2},{2,1},{3,4},{4,3},{5,6},{6,5},{7,8},{8,7},{9,10},{10,9},{11,... | collective-permute-start | bytes 565256 | tf_op jit(solution)/shard_map/ppermute | solution.py:507
  3.6 1.0 copy-start
